TPU v7x, 128 devices: a whole 4x4x4 slice. The times are simulated.
128 devices in a mesh: fsdp: 32 (over y, z_lo, x), tp: 4 (over z_hi, core).
Axes of the slice: x: 4, y: 4, z: 4 (z_hi: 2, z_lo: 2; z = z_hi * 2 + z_lo), core: 2. Of those that a mesh axis runs over, the one named last changes fastest.
Arguments:
- ref_rows: bfloat16 [1024, 4096], P(('fsdp', 'tp')), may hold values from -6 to 6
- ref_gain: float32 [4096], replicated, may hold values from 0.5 to 1.5
- trainee_rows: bfloat16 [1024, 8192], P('fsdp', 'tp'), may hold values from -6 to 6
- trainee_gain: float32 [8192], replicated, may hold values from 0.5 to 1.5
- ref_head: bfloat16 [4096, 65536], P(None, ('fsdp', 'tp'))
- trainee_head: bfloat16 [8192, 65536], P(None, ('fsdp', 'tp'))
- targets: int32 [1024], replicated, may hold values from 0 to 65535
- selected: int32 [1024], replicated, may hold values 0 or 1
Outputs:
- excess: float32 [1024], P(('fsdp', 'tp'))
- head_grad: bfloat16 [8192, 65536], P(None, ('fsdp', 'tp'))
All inputs are finite; a program needn't handle non-finite values.
Results may differ from a plain program's by a relative error of at most 0.0051.
Values may be sent and summed in bfloat16 or wider, within the bound.
No kernel may reach another device: no remote copies, remote signals or barrier semaphores. Data moves between devices by JAX's collectives and lax.ppermute only.
A program may use at most 128 MiB of HBM per device.

v0:
```python
import jax
import jax.numpy as jnp
from jax import lax
from jax.sharding import PartitionSpec as P

EPSILON = 1e-05


def normalize(values, gain):
    widened = values.astype(jnp.float32)
    factor = lax.rsqrt(jnp.mean(widened * widened, axis=1, keepdims=True) + EPSILON)
    return (widened * factor * gain).astype(jnp.bfloat16)


def head_stats(normed, head, wanted, first_column):
    logits = jnp.dot(normed, head, preferred_element_type=jnp.float32)
    column = first_column + jnp.arange(head.shape[1], dtype=jnp.int32)
    highest = jnp.max(logits, axis=1)
    summed = jnp.sum(jnp.exp(logits - highest[:, None]), axis=1)
    target_hit = jnp.sum(jnp.where(wanted[:, None] == column[None, :], logits, 0.0), axis=1)
    return (logits, highest, summed, target_hit)


def shards(
    ref_rows, ref_gain, trainee_rows, trainee_gain, ref_head, trainee_head, targets, selected
):
    devices_all = lax.axis_size(("fsdp", "tp"))
    shard_index = lax.axis_index(("fsdp", "tp"))
    vocab_local = trainee_head.shape[1]
    first_column = shard_index * vocab_local
    ref_normed = normalize(ref_rows, ref_gain)
    logits, highest, summed, target_hit = head_stats(
        lax.all_gather(ref_normed, ("fsdp", "tp"), axis=0, tiled=True),
        ref_head,
        targets,
        first_column,
    )
    ref_parts = jnp.stack([highest, summed, target_hit])
    widened_rows = lax.all_gather(trainee_rows, "tp", axis=1, tiled=True)
    own_normed = lax.all_gather(normalize(widened_rows, trainee_gain), "fsdp", axis=0, tiled=True)
    own_logits, own_high, own_sum, own_hit = head_stats(
        own_normed, trainee_head, targets, first_column
    )
    ref_peak, own_peak = lax.pmax((ref_parts[0], own_high), ("fsdp", "tp"))
    ref_sum, ref_hit, own_sum, own_hit = lax.psum(
        (
            ref_parts[1] * jnp.exp(ref_parts[0] - ref_peak),
            ref_parts[2],
            own_sum * jnp.exp(own_high - own_peak),
            own_hit,
        ),
        ("fsdp", "tp"),
    )
    own_high = own_peak
    ref_lse = ref_peak + jnp.log(ref_sum)
    own_lse = own_high + jnp.log(own_sum)
    excess = own_lse - own_hit - (ref_lse - ref_hit)
    weight = selected.astype(jnp.float32)
    column = first_column + jnp.arange(vocab_local, dtype=jnp.int32)
    onehot = (targets[:, None] == column[None, :]).astype(jnp.float32)
    scaled = (weight[:, None] * (jnp.exp(own_logits - own_lse[:, None]) - onehot)).astype(
        jnp.bfloat16
    )
    head_grad = lax.dot_general(
        own_normed, scaled, (((0,), (0,)), ((), ())), preferred_element_type=jnp.float32
    ).astype(jnp.bfloat16)
    per_device = targets.shape[0] // devices_all
    own_excess = lax.dynamic_slice_in_dim(excess, shard_index * per_device, per_device)
    return (own_excess, head_grad)


def solution(mesh):
    in_specs = (
        P(("fsdp", "tp"), None),
        P(),
        P("fsdp", "tp"),
        P(),
        P(None, ("fsdp", "tp")),
        P(None, ("fsdp", "tp")),
        P(),
        P(),
    )
    out_specs = (P(("fsdp", "tp")), P(None, ("fsdp", "tp")))
    return jax.shard_map(shards, mesh=mesh, in_specs=in_specs, out_specs=out_specs, check_vma=False)
```

profile of v0, /device:TPU:1, one launch (start us, length us, event | category | flops | bytes accessed | tf_op | source)
XLA Modules:
  0.0 582.8 jit_solution(10104219051896448847)
XLA Ops:
  7.2 0.0 copy-start.1
  7.2 0.0 all-gather.5.cloned.1.call-start
  7.2 1.0 fusion.13
  8.2 1.6 fusion.15
  9.8 0.0 all-gather.5.cloned.1.call-update
  9.8 0.0 all-gather.3.cloned.1.call-start
  9.8 11.1 %all_gather.9 = bf16[32,8192]{1,0:T(8,128)(2,1)S(1)} all-gather(bf16[32,2048]{1,0:T(8,128)(2,1)} %param.10), channel_id=1, replica_groups=mesh['fsdp'=32,'tp'=4] {'tp'}, dimensions={1}, use_global_device_ids=true | all-gather | bytes 655360 | tf_op jit(solution)/shard_map/all_gather | solution.py:39
  21.0 0.2 fusion.5
  21.2 1.8 fusion.7
  23.0 0.0 all-gather.3.cloned.1.call-update
  23.0 0.0 copy-done.1
  23.1 193.3 %all-gather.5.cloned.1.call-done = bf16[1024,4096]{1,0:T(8,128)(2,1)} async-done(((bf16[8,4096]{1,0:T(8,128)(2,1)}), bf16[1024,4096]{1,0:T(8,128)(2,1)}) %all-gather.5.cloned.1.call-update) | async-done | bytes 8388624 | tf_op jit(solution)/shard_map/all_gather | solution.py:33
  216.4 10.4 %fusion.16 = (f32[1024]{0:T(1024)S(1)}, f32[1024,512]{0,1:T(8,128)}) fusion(bf16[1024,4096]{1,0:T(8,128)(2,1)} %all-gather.5.cloned.1.call-done, bf16[4096,512]{1,0:T(8,128)(2,1)} %param.12), kind=kOutput, calls=%fused_computation.32 | convolution fusion | flops 4295490560 | bytes 14684160 | tf_op jit(solution)/shard_map/dot_general | solution.py:16
  226.8 0.0 copy-start
  226.8 177.5 %all-gather.3.cloned.1.call-done = bf16[1024,8192]{1,0:T(8,128)(2,1)} async-done(((bf16[32,8192]{1,0:T(8,128)(2,1)}), bf16[1024,8192]{1,0:T(8,128)(2,1)}) %all-gather.3.cloned.1.call-update) | async-done | bytes 16777232 | tf_op jit(solution)/shard_map/all_gather | solution.py:40
  404.3 17.3 %fusion.17 = (f32[1024]{0:T(1024)S(1)}, f32[1024,512]{0,1:T(8,128)S(1)}) fusion(bf16[1024,8192]{1,0:T(8,128)(2,1)} %all-gather.3.cloned.1.call-done, bf16[8192,512]{1,0:T(8,128)(2,1)} %param.13), kind=kOutput, calls=%fused_computation.33 | convolution fusion | flops 8590457856 | bytes 27267072 | tf_op jit(solution)/shard_map/dot_general | solution.py:16
  421.7 68.4 %all-reduce.1 = (f32[1024]{0:T(1024)S(1)}, f32[1024]{0:T(1024)S(1)}) all-reduce(f32[1024]{0:T(1024)S(1)} %get-tuple-element.16, f32[1024]{0:T(1024)S(1)} %get-tuple-element.18), channel_id=1, replica_groups=mesh['fsdp'=32,'tp'=4] {'fsdp','tp'}, use_global_device_ids=true, to_apply=%region_9.10 | all-reduce | flops 2048 | bytes 16384 | tf_op jit(solution)/shard_map/pmax | solution.py:44
  490.0 0.0 copy-done
  490.0 2.6 exponential_reduce_fusion
  492.7 64.7 %all-reduce = (f32[1024]{0:T(1024)S(1)}, f32[1024]{0:T(1024)S(1)}, f32[1024]{0:T(1024)S(1)}, f32[1024]{0:T(1024)S(1)}) all-reduce(f32[1024]{0:T(1024)S(1)} %get-tuple-element.5, f32[1024]{0:T(1024)S(1)} %get-tuple-element.20, f32[1024]{0:T(1024)S(1)} %get-tuple-element.21, ...), channel_id=1, replica_groups=mesh['fsdp'=32,'tp'=4] {'fsdp','tp'}, use_global_device_ids=true, to_apply=%region_13.14 | all-reduce | flops 4096 | bytes 32768 | tf_op jit(solution)/shard_map/psum | solution.py:45
  557.4 0.6 dynamic_slice.3
  558.0 17.9 %convolution_convert_fusion = bf16[8192,512]{1,0:T(8,128)(2,1)} fusion(bf16[1024,8192]{1,0:T(8,128)(2,1)} %all-gather.3.cloned.1.call-done, f32[1024,512]{0,1:T(8,128)S(1)} %get-tuple-element.19, f32[1024]{0:T(1024)S(1)} %get-tuple-element.15, f32[1024]{0:T(1024)S(1)} %convert_element_type.28, s32[1024]{0:T(1024)S(1)} %copy-done, s32[512]{0:T(512)S(1)} %iota_add_fusion), kind=kOutput, calls=%fused_computation | convolution fusion | flops 8597274624 | bytes 27277312 | tf_op jit(solution)/shard_map/dot_general | solution.py:64
  (6 shorter events, 0.0 us)
Async XLA Ops:
  7.2 15.9 %copy-start.1 = (s32[1024]{0:T(1024)S(1)}, s32[1024]{0:T(1024)}, u32[]{:S(2)}) copy-start(s32[1024]{0:T(1024)} %param.15) | copy-start | bytes 12292
  7.2 209.2 %all-gather.5.cloned.1.call-start = ((), (), s32[]{:S(2)}) async-start(), calls=%async_computation.1 | async-start | bytes 8454144 | tf_op jit(solution)/shard_map/all_gather | solution.py:33
  9.8 394.5 %all-gather.3.cloned.1.call-start = ((), (), s32[]{:S(2)}) async-start(), calls=%async_computation | async-start | bytes 17301504 | tf_op jit(solution)/shard_map/all_gather | solution.py:40
  226.8 263.2 %copy-start = (s32[1024]{0:T(1024)S(1)}, s32[1024]{0:T(1024)}, u32[]{:S(2)}) copy-start(s32[1024]{0:T(1024)} %param.14) | copy-start | bytes 12292
Sparse Core Ops, SparseCore 0:
  10.3 206.0 all-gather.4
  218.1 186.2 all-gather.2
where the time goes:
time: 583 us
  waiting for transfers between devices  371 us (64%)
  blocking collectives  144 us (25%)
  matrix products  45.7 us (8%)
  between operations  14.1 us (2%)
  other arithmetic  7.24 us (1%)
    all_gather x1, waiting for transfers between devices, shards(): lax.all_gather(ref_normed, ('fsdp', 'tp'), axis=0, tiled=True)  193 us
    all_gather x1, waiting for transfers between devices, shards(): lax.all_gather(normalize(widened_rows, trainee_gain), 'fsdp', axis=0, til...  177 us
    pmax x1, blocking collectives, shards(): ref_peak, own_peak = lax.pmax((ref_parts[0], own_high), ('fsdp', 'tp'))  68.4 us
    psum x1, blocking collectives, shards(): lax.psum((ref_parts[1] * jnp.exp(ref_parts[0] - ref_peak), ref_parts[2],...  64.7 us
    dot_general x2, matrix products, head_stats(): logits = jnp.dot(normed, head, preferred_element_type=jnp.float32)  27.8 us
    dot_general x1, matrix products, shards(): lax.dot_general(own_normed, scaled, (((0,), (0,)), ((), ())), preferred_e...  17.9 us
  transfers between devices with their start and end apart: 2, of which 2 were waited for; matrix products, arithmetic and copies ran while one was open for 2% of the time, Pallas kernels for 0%

commit v1 on v0

v1 whole, which is shorter than its diff:
```python
import functools

import jax
import jax.numpy as jnp
from jax import lax
from jax.experimental import pallas as pl
from jax.experimental.pallas import tpu as pltpu
from jax.sharding import PartitionSpec as P

EPSILON = 1e-05
ALL = ("fsdp", "tp")
ORDERS = ("yzx", "zxy", "xyz")
WIDE = 4096
TOKENS = 1024
MIB = 1 << 20
BLOCK = 1024
DEEP = 512


def flat(x, y, z, core):
    return (((y % 4) * 2 + (z % 4) % 2) * 4 + (x % 4)) * 4 + ((z % 4) // 2) * 2 + core


def place(index):
    x = (index // 4) % 4
    y = index // 32
    z = ((index // 2) % 2) * 2 + (index // 16) % 2
    return x, y, z, index % 2


def shifted(axis, steps):
    pairs = []
    for index in range(128):
        x, y, z, core = place(index)
        at = {"x": x, "y": y, "z": z}
        at[axis] += steps[core]
        pairs.append((index, flat(at["x"], at["y"], at["z"], core)))
    return pairs


def send(values, axis, steps):
    return lax.ppermute(values, ALL, shifted(axis, steps))


def exchange(values, bits):
    return lax.ppermute(values, ALL, [(index, index ^ bits) for index in range(128)])


def normalize(values, gain):
    widened = values.astype(jnp.float32)
    factor = lax.rsqrt(jnp.mean(widened * widened, axis=1, keepdims=True) + EPSILON)
    return (widened * factor * gain).astype(jnp.bfloat16)


def gather(parts):
    level = parts
    for stage in (0, 1):
        grown = []
        for rows, order in zip(level, ORDERS):
            axis = order[stage]
            near = [send(rows, axis, steps) for steps in ((1, -1), (-1, 1), (2, 2))]
            grown.append(jnp.concatenate([rows, *near], axis=0))
        level = grown
    slots = []
    firsts = [send(rows, order[2], (1, -1)) for rows, order in zip(level, ORDERS)]
    seconds = [send(rows, order[2], (-1, 1)) for rows, order in zip(level, ORDERS)]
    thirds = [send(rows, order[2], (1, -1)) for rows, order in zip(firsts, ORDERS)]
    for mine in zip(level, firsts, seconds, thirds):
        slots.append([*mine, *(exchange(piece, 1) for piece in mine)])
    return slots


def row_table(me):
    here = place(me)
    t = jnp.arange(3 * 8 * 16, dtype=jnp.int32)
    part, slot, group = t // 128, (t // 16) % 8, t % 16
    core = jnp.where(slot >= 4, 1 - here[3], here[3])

    def offset(j):
        return jnp.where(j == 0, 0, jnp.where(j == 3, 2, (2 * j - 3) * (1 - 2 * core)))

    along = (offset(group % 4), offset(group // 4), offset(slot % 4))
    at = []
    for axis, start in zip("xyz", here):
        step = jnp.zeros_like(t)
        for number, order in enumerate(ORDERS):
            step = jnp.where(part == number, along[order.index(axis)], step)
        at.append(start + step + 4)
    return 8 * flat(*at, core)


def copy_in(pieces, head, at, xbuf, hbuf, sems):
    copies = []
    for number, piece in enumerate(pieces):
        copies.append(
            pltpu.make_async_copy(
                piece, xbuf.at[at, pl.ds(128 * number, 128), :], sems.at[at, number]
            )
        )
    copies.append(pltpu.make_async_copy(head, hbuf.at[at], sems.at[at, len(pieces)]))
    for copy in copies:
        copy.start()
    return copies


def add_logits(at, slots, table, xbuf, hbuf, tmp, total):
    rows = 128 * len(slots)
    tmp[pl.ds(0, rows), :] = jnp.zeros((rows, 512), jnp.float32)

    def deep(step, carry):
        cut = pl.ds(pl.multiple_of(step * DEEP, DEEP), DEEP)
        tmp[pl.ds(0, rows), :] += jnp.dot(
            xbuf[at, pl.ds(0, rows), cut], hbuf[at, cut, :], preferred_element_type=jnp.float32
        )
        return carry

    lax.fori_loop(0, WIDE // DEEP, deep, 0)
    for number, slot in enumerate(slots):

        def place_rows(group, carry):
            first = pl.multiple_of(table[(at * 8 + slot) * 16 + group], 8)
            source = pl.multiple_of(128 * number + 8 * group, 8)
            total[min(at, 2) // 2, pl.ds(first, 8), :] += tmp[pl.ds(source, 8), :]
            return carry

        lax.fori_loop(0, 16, place_rows, 0, unroll=4)


EARLY = (0, 4, 1, 5, 2, 6)
LATE = (3, 7)


def early_kernel(table, *refs):
    pieces, (own_head, ref_head, total, xbuf, hbuf, tmp, sems) = refs[:18], refs[18:]
    heads = (own_head.at[pl.ds(0, WIDE), :], own_head.at[pl.ds(WIDE, WIDE), :], ref_head)
    waits = [copy_in(pieces[6 * k : 6 * k + 6], heads[k], k, xbuf, hbuf, sems) for k in range(3)]
    total[...] = jnp.zeros_like(total)
    for k in range(3):
        for copy in waits[k]:
            copy.wait()
        add_logits(k, EARLY, table, xbuf, hbuf, tmp, total)


def late_kernel(table, *refs):
    pieces = refs[:6]
    own_head, ref_head, before, info, total, stats, xbuf, hbuf, tmp, sems = refs[6:]
    heads = (own_head.at[pl.ds(0, WIDE), :], own_head.at[pl.ds(WIDE, WIDE), :], ref_head)
    copy = pltpu.make_async_copy(before, total, sems.at[3, 0])
    copy.start()
    waits = [copy_in(pieces[2 * k : 2 * k + 2], heads[k], k, xbuf, hbuf, sems) for k in range(3)]
    copy.wait()
    for k in range(3):
        for copy in waits[k]:
            copy.wait()
        add_logits(k, LATE, table, xbuf, hbuf, tmp, total)

    def chunk(step, carry):
        rows = pl.ds(pl.multiple_of(step * 128, 128), 128)
        wanted = jnp.transpose(info[:, rows])[:, 0:1]
        column = lax.broadcasted_iota(jnp.int32, (128, 512), 1).astype(jnp.float32)
        found = []
        for which in (0, 1):
            logits = total[which, rows, :]
            peak = jnp.max(logits, axis=1, keepdims=True)
            summed = jnp.sum(jnp.exp(logits - peak), axis=1, keepdims=True)
            hit = jnp.sum(jnp.where(column == wanted, logits, 0.0), axis=1, keepdims=True)
            found.append((peak + jnp.log(summed), hit))
        lane = lax.broadcasted_iota(jnp.int32, (128, 128), 1)
        block = jnp.where(
            lane == 0,
            found[0][0],
            jnp.where(lane == 1, found[1][0], jnp.where(lane == 2, found[0][1] - found[1][1], 0.0)),
        )
        stats[:, rows] = jnp.transpose(block)[0:8, :]
        return carry

    lax.fori_loop(0, TOKENS // 128, chunk, 0)


def grad_kernel(table, *refs):
    pieces, (logits, joined, info, out, plain, ordered, scaled) = refs[:16], refs[16:]
    step = pl.program_id(0)
    half = WIDE // BLOCK

    @pl.when(step == 0)
    def _():
        def chunk(number, carry):
            rows = pl.ds(pl.multiple_of(number * 128, 128), 128)
            told = jnp.transpose(info[:, rows])
            lse = jnp.transpose(joined[:, rows])[:, 0:1]
            column = lax.broadcasted_iota(jnp.int32, (128, 512), 1).astype(jnp.float32)
            hit = (column == told[:, 0:1]).astype(jnp.float32)
            plain[rows, :] = told[:, 1:2] * (jnp.exp(logits[0, rows, :] - lse) - hit)
            return carry

        lax.fori_loop(0, TOKENS // 128, chunk, 0)
        for part in (0, 1):

            def place_rows(group, carry):
                first = pl.multiple_of(table[part * 128 + group], 8)
                ordered[pl.ds(pl.multiple_of(8 * group, 8), 8), :] = plain[pl.ds(first, 8), :]
                return carry

            lax.fori_loop(0, 128, place_rows, 0, unroll=8)
            scaled[part] = ordered[...].astype(jnp.bfloat16)

    for part in (0, 1):

        @pl.when(step // half == part)
        def _():
            rows = jnp.concatenate([piece[...] for piece in pieces[8 * part : 8 * part + 8]], axis=0)
            out[...] = lax.dot_general(
                rows, scaled[part], (((0,), (0,)), ((), ())), preferred_element_type=jnp.float32
            ).astype(jnp.bfloat16)


ANY = pl.BlockSpec(memory_space=pl.ANY)
INSIDE = pl.BlockSpec(memory_space=pltpu.VMEM)
TABLE = pl.BlockSpec(memory_space=pltpu.SMEM)


def logits_call(kernel, slots, table, pieces, heads, extra, out_shape, extra_specs):
    rows = 128 * len(slots)
    outs = jax.tree.map(lambda _: INSIDE, out_shape)
    return pl.pallas_call(
        kernel,
        out_shape=out_shape,
        in_specs=[TABLE] + [ANY] * (len(pieces) + 2) + extra_specs,
        out_specs=outs,
        scratch_shapes=[
            pltpu.VMEM((3, rows, WIDE), jnp.bfloat16),
            pltpu.VMEM((3, WIDE, 512), jnp.bfloat16),
            pltpu.VMEM((rows, 512), jnp.float32),
            pltpu.SemaphoreType.DMA((4, len(slots) + 1)),
        ],
        compiler_params=pltpu.CompilerParams(vmem_limit_bytes=48 * MIB),
        cost_estimate=pl.CostEstimate(
            flops=2 * 3 * rows * WIDE * 512,
            bytes_accessed=3 * (rows * WIDE * 2 + WIDE * 1024) + 4 * MIB,
            transcendentals=0,
        ),
    )(table, *pieces, *heads, *extra)


def grad_call(table, pieces, logits, joined, info):
    half = WIDE // BLOCK
    first = pl.BlockSpec((128, BLOCK), lambda b: (0, jnp.minimum(b, half - 1)))
    second = pl.BlockSpec((128, BLOCK), lambda b: (0, jnp.maximum(b - half, 0)))
    return pl.pallas_call(
        grad_kernel,
        grid=(2 * half,),
        out_shape=jax.ShapeDtypeStruct((2 * WIDE, 512), jnp.bfloat16),
        in_specs=[TABLE]
        + [first] * 8
        + [second] * 8
        + [pl.BlockSpec((1, TOKENS, 512), lambda b: (0, 0, 0))]
        + [pl.BlockSpec((8, TOKENS), lambda b: (0, 0))] * 2,
        out_specs=pl.BlockSpec((BLOCK, 512), lambda b: (b, 0)),
        scratch_shapes=[
            pltpu.VMEM((TOKENS, 512), jnp.float32),
            pltpu.VMEM((TOKENS, 512), jnp.float32),
            pltpu.VMEM((2, TOKENS, 512), jnp.bfloat16),
        ],
        compiler_params=pltpu.CompilerParams(vmem_limit_bytes=48 * MIB),
        cost_estimate=pl.CostEstimate(
            flops=2 * TOKENS * 2 * WIDE * 512, bytes_accessed=26 * MIB, transcendentals=0
        ),
    )(table, *pieces, logits, joined, info)


def join(terms):
    peak = functools.reduce(jnp.maximum, terms)
    logs = peak + jnp.log(sum(jnp.exp(term - peak) for term in terms))
    row = lax.broadcasted_iota(jnp.int32, peak.shape, 0)
    return jnp.where(row < 2, logs, sum(terms))


def everywhere(values):
    values = join([values, exchange(values, 1)])
    for axis in "xyz":
        values = join([values] + [send(values, axis, (s, s)) for s in (1, -1, 2)])
    return values


def own_rows(block, member):
    arrived = []
    for bits in range(4):
        there = member ^ bits
        cut = lax.dynamic_slice_in_dim(block, 8 * there, 8)
        arrived.append(exchange(cut, bits) if bits else cut)
    quarters = []
    for quarter in range(4):
        found = arrived[0]
        for bits in (1, 2, 3):
            found = jnp.where((member ^ bits) == quarter, arrived[bits], found)
        quarters.append(found)
    return jnp.concatenate(quarters, axis=1)


def shards(
    ref_rows, ref_gain, trainee_rows, trainee_gain, ref_head, trainee_head, targets, selected
):
    me = lax.axis_index(ALL)
    own = normalize(own_rows(trainee_rows, lax.axis_index("tp")), trainee_gain)
    ref = normalize(ref_rows, ref_gain)
    slots = gather([own[:, :WIDE], own[:, WIDE:], ref])

    table = row_table(me)
    wanted = (targets - me * trainee_head.shape[1]).astype(jnp.float32)
    row = lax.broadcasted_iota(jnp.int32, (8, TOKENS), 0)
    info = jnp.where(
        row == 0, wanted[None], jnp.where(row == 1, selected.astype(jnp.float32)[None], 0.0)
    )

    totals = jax.ShapeDtypeStruct((2, TOKENS, 512), jnp.float32)
    heads = (trainee_head, ref_head)
    early = [part[slot] for part in slots for slot in EARLY]
    late = [part[slot] for part in slots for slot in LATE]
    before = logits_call(early_kernel, EARLY, table, early, heads, (), totals, [])
    logits, stats = logits_call(
        late_kernel,
        LATE,
        table,
        late,
        heads,
        (before, info),
        (totals, jax.ShapeDtypeStruct((8, TOKENS), jnp.float32)),
        [ANY, INSIDE],
    )
    joined = everywhere(stats)
    excess = joined[0] - joined[1] - joined[2]
    head_grad = grad_call(table, [*slots[0], *slots[1]], logits, joined, info)
    return lax.dynamic_slice_in_dim(excess, me * 8, 8), head_grad


def solution(mesh):
    in_specs = (P(ALL, None), P(), P("fsdp", "tp"), P(), P(None, ALL), P(None, ALL), P(), P())
    out_specs = (P(ALL), P(None, ALL))
    return jax.shard_map(shards, mesh=mesh, in_specs=in_specs, out_specs=out_specs, check_vma=False)
```

time: 583 us -> 221 us (0.38)
  waiting for transfers between devices: 371 us -> 53.8 us
  blocking collectives: 144 us -> 0 us
  starting transfers between devices: 0.08 us -> 89.9 us
  Pallas kernels: 0 us -> 58.5 us
  matrix products: 45.7 us -> 0 us
  between operations: 14.1 us -> 1.36 us
  local copies, waits for them, and re-layouts: 0.6 us -> 8.98 us
    all_gather x2 -> x0, waiting for transfers between devices: 371 us -> none  [the longest x1 193 us: shards(): lax.all_gather(ref_normed, ('fsdp', 'tp'), axis=0, tiled=True)]
    ppermute x0 -> x52, starting transfers between devices: none -> 89.9 us  [the longest x36 47.7 us: send(): return lax.ppermute(values, ALL, shifted(axis, steps))]
    pmax x1 -> x0, blocking collectives: 68.4 us -> none  [shards(): ref_peak, own_peak = lax.pmax((ref_parts[0], own_high), ('fsdp', 'tp'))]
    psum x1 -> x0, blocking collectives: 64.7 us -> none  [shards(): lax.psum((ref_parts[1] * jnp.exp(ref_parts[0] - ref_peak), ref_parts[2],...]
    pallas_call x0 -> x3, Pallas kernels: none -> 58.5 us  [the longest x2 39.3 us: logits_call(): pl.pallas_call(kernel, out_shape=out_shape, in_specs=[TABLE] + [ANY] * (l...]
    ppermute x0 -> x52, waiting for transfers between devices: none -> 53.8 us  [the longest x36 51.1 us: send(): return lax.ppermute(values, ALL, shifted(axis, steps))]
    dot_general x3 -> x0, matrix products: 45.7 us -> none  [the longest x2 27.8 us: head_stats(): logits = jnp.dot(normed, head, preferred_element_type=jnp.float32)]
    all_gather x1 -> x0, blocking collectives: 11.1 us -> none  [shards(): widened_rows = lax.all_gather(trainee_rows, 'tp', axis=1, tiled=True)]
  transfers between devices with their start and end apart: 2 -> 52, of which waited for: 2 -> 19; matrix products, arithmetic and copies ran while one was open for 2% -> 2% of each run, Pallas kernels for 0% -> 10%
where the time goes in v1:
time: 221 us; the launch traced here: 217 us
  starting transfers between devices  89.9 us (41%)
  Pallas kernels  58.5 us (26%)
  waiting for transfers between devices  53.8 us (24%)
  local copies, waits for them, and re-layouts  8.98 us (4%)
  other arithmetic  4.87 us (2%)
    ppermute x36, waiting for transfers between devices, send(): return lax.ppermute(values, ALL, shifted(axis, steps))  51.1 us
    ppermute x36, starting transfers between devices, send(): return lax.ppermute(values, ALL, shifted(axis, steps))  47.7 us
    ppermute x16, starting transfers between devices, exchange(): lax.ppermute(values, ALL, [(index, index ^ bits) for index in range(128)])  42.2 us
    pallas_call x2, Pallas kernels, logits_call(): pl.pallas_call(kernel, out_shape=out_shape, in_specs=[TABLE] + [ANY] * (l...  39.3 us
    pallas_call x1, Pallas kernels, grad_call(): pl.pallas_call(grad_kernel, grid=(2 * half,), out_shape=jax.ShapeDtypeStr...  19.2 us
    unnamed x57, local copies, waits for them, and re-layouts  8.09 us
  transfers between devices with their start and end apart: 52, of which 19 were waited for; matrix products, arithmetic and copies ran while one was open for 2% of the time, Pallas kernels for 10%

profile of v1, /device:TPU:1, one launch (start us, length us, event | category | flops | bytes accessed | tf_op | source)
XLA Modules:
  0.0 217.4 jit_solution(16327552768402112440)
XLA Ops:
  0.7 0.8 constant_dynamic-slice_fusion.3
  1.5 1.5 collective-permute-start.2
  2.9 3.7 %collective-permute-start.1 = (bf16[8,2048]{1,0:T(8,128)(2,1)S(1)}, bf16[8,2048]{1,0:T(8,128)(2,1)S(1)}, u32[]{:S(2)}, u32[]{:S(2)}) collective-permute-start(bf16[8,2048]{1,0:T(8,128)(2,1)S(1)} %get-tuple-element.17), channel_id=1, source_target_pairs={{0,2},{1,3},{2,0},{3,1},{4,6},{5,7},{6,4},{7,5},{8,10},{9,11},{10,... | collective-permute-start | bytes 98312 | tf_op jit(solution)/shard_map/ppermute | solution.py:46
  6.7 1.0 fusion.3
  7.7 0.9 constant_dynamic-update-slice_fusion.20
  8.6 2.8 %collective-permute-start.23 = (bf16[8,4096]{1,0:T(8,128)(2,1)S(1)}, bf16[8,4096]{1,0:T(8,128)(2,1)S(1)}, u32[]{:S(2)}, u32[]{:S(2)}) collective-permute-start(bf16[8,4096]{1,0:T(8,128)(2,1)S(1)} %get-tuple-element.7), channel_id=1, source_target_pairs={{0,8},{1,9},{2,10},{3,11},{4,12},{5,13},{6,14},{7,15},{8,0},{9,1},... | collective-permute-start | bytes 196616 | tf_op jit(solution)/shard_map/ppermute | solution.py:42
  11.8 2.4 %collective-permute-start.21 = (bf16[8,4096]{1,0:T(8,128)(2,1)S(1)}, bf16[8,4096]{1,0:T(8,128)(2,1)S(1)}, u32[]{:S(2)}, u32[]{:S(2)}) collective-permute-start(bf16[8,4096]{1,0:T(8,128)(2,1)S(1)} %get-tuple-element.7), channel_id=1, source_target_pairs={{0,4},{1,13},{2,6},{3,15},{4,8},{5,1},{6,10},{7,3},{8,12},{9,5},{1... | collective-permute-start | bytes 196616 | tf_op jit(solution)/shard_map/ppermute | solution.py:42
  14.2 0.8 select_select_fusion.4
  15.2 0.9 fusion.2
  16.1 3.2 %collective-permute-start.14 = (bf16[8,4096]{1,0:T(8,128)(2,1)S(1)}, bf16[8,4096]{1,0:T(8,128)(2,1)S(1)}, u32[]{:S(2)}, u32[]{:S(2)}) collective-permute-start(bf16[8,4096]{1,0:T(8,128)(2,1)S(1)} %get-tuple-element.12), channel_id=1, source_target_pairs={{0,2},{1,3},{2,0},{3,1},{4,6},{5,7},{6,4},{7,5},{8,10},{9,11},{10,... | collective-permute-start | bytes 196616 | tf_op jit(solution)/shard_map/ppermute | solution.py:42
  19.3 0.7 collective-permute-start.13
  20.0 2.9 %collective-permute-start.5 = (bf16[8,4096]{1,0:T(8,128)(2,1)S(1)}, bf16[8,4096]{1,0:T(8,128)(2,1)S(1)}, u32[]{:S(2)}, u32[]{:S(2)}) collective-permute-start(bf16[8,4096]{1,0:T(8,128)(2,1)S(1)} %get-tuple-element.15), channel_id=1, source_target_pairs={{0,64},{1,65},{2,66},{3,67},{4,68},{5,69},{6,70},{7,71},{8,72},{9,... | collective-permute-start | bytes 196616 | tf_op jit(solution)/shard_map/ppermute | solution.py:42
  23.5 2.3 %collective-permute-start.3 = (bf16[8,4096]{1,0:T(8,128)(2,1)S(1)}, bf16[8,4096]{1,0:T(8,128)(2,1)S(1)}, u32[]{:S(2)}, u32[]{:S(2)}) collective-permute-start(bf16[8,4096]{1,0:T(8,128)(2,1)S(1)} %get-tuple-element.15), channel_id=1, source_target_pairs={{0,32},{1,97},{2,34},{3,99},{4,36},{5,101},{6,38},{7,103},{8,40},{... | collective-permute-start | bytes 196616 | tf_op jit(solution)/shard_map/ppermute | solution.py:42
  25.8 2.0 collective-permute-start.12
  27.9 2.3 %collective-permute-start.26 = (bf16[32,4096]{1,0:T(8,128)(2,1)S(1)}, bf16[32,4096]{1,0:T(8,128)(2,1)S(1)}, u32[]{:S(2)}, u32[]{:S(2)}) collective-permute-start(bf16[32,4096]{1,0:T(8,128)(2,1)S(1)} %pad_maximum_fusion.2), channel_id=1, source_target_pairs={{0,64},{1,65},{2,66},{3,67},{4,68},{5,69},{6,70},{7,71},{8,72},{9,... | collective-permute-start | bytes 786440 | tf_op jit(solution)/shard_map/ppermute | solution.py:42
  30.6 2.3 %collective-permute-start.24 = (bf16[32,4096]{1,0:T(8,128)(2,1)S(1)}, bf16[32,4096]{1,0:T(8,128)(2,1)S(1)}, u32[]{:S(2)}, u32[]{:S(2)}) collective-permute-start(bf16[32,4096]{1,0:T(8,128)(2,1)S(1)} %pad_maximum_fusion.2), channel_id=1, source_target_pairs={{0,32},{1,97},{2,34},{3,99},{4,36},{5,101},{6,38},{7,103},{8,40},{... | collective-permute-start | bytes 786440 | tf_op jit(solution)/shard_map/ppermute | solution.py:42
  33.1 2.0 collective-permute-start.7
  35.2 7.0 %collective-permute-done.24 = bf16[32,4096]{1,0:T(8,128)(2,1)S(1)} collective-permute-done((bf16[32,4096]{1,0:T(8,128)(2,1)S(1)}, bf16[32,4096]{1,0:T(8,128)(2,1)S(1)}, u32[]{:S(2)}, u32[]{:S(2)}) %collective-permute-start.24) | collective-permute-done | bytes 262176 | tf_op jit(solution)/shard_map/ppermute | solution.py:42
  42.2 1.0 collective-permute-done.25
  43.4 4.0 %collective-permute-done.6 = bf16[32,4096]{1,0:T(8,128)(2,1)S(1)} collective-permute-done((bf16[32,4096]{1,0:T(8,128)(2,1)S(1)}, bf16[32,4096]{1,0:T(8,128)(2,1)S(1)}, u32[]{:S(2)}, u32[]{:S(2)}) %collective-permute-start.6) | collective-permute-done | bytes 262176 | tf_op jit(solution)/shard_map/ppermute | solution.py:42
  47.4 1.1 collective-permute-start.15
  48.5 7.2 %collective-permute-done.15 = bf16[32,4096]{1,0:T(8,128)(2,1)S(1)} collective-permute-done((bf16[32,4096]{1,0:T(8,128)(2,1)S(1)}, bf16[32,4096]{1,0:T(8,128)(2,1)S(1)}, u32[]{:S(2)}, u32[]{:S(2)}) %collective-permute-start.15) | collective-permute-done | bytes 262176 | tf_op jit(solution)/shard_map/ppermute | solution.py:42
  55.7 0.6 collective-permute-start.40
  56.3 4.4 %collective-permute-start.38 = (bf16[128,4096]{1,0:T(8,128)(2,1)S(1)}, bf16[128,4096]{1,0:T(8,128)(2,1)S(1)}, u32[]{:S(2)}, u32[]{:S(2)}) collective-permute-start(bf16[128,4096]{1,0:T(8,128)(2,1)S(1)} %constant_dynamic-update-slice_fusion.14.refs_12_), channel_id=1, source_target_pairs={{0,1},{1,0},{2,3},{3,2},{4,5},{5,4},{6,7},{7,6},{8,9},{9,8},{10,11... | collective-permute-start | bytes 3145736 | tf_op jit(solution)/shard_map/ppermute | solution.py:46
  60.9 0.9 collective-permute-start.36
  61.8 2.3 %collective-permute-start.34 = (bf16[128,4096]{1,0:T(8,128)(2,1)S(1)}, bf16[128,4096]{1,0:T(8,128)(2,1)S(1)}, u32[]{:S(2)}, u32[]{:S(2)}) collective-permute-start(bf16[128,4096]{1,0:T(8,128)(2,1)S(1)} %constant_dynamic-update-slice_fusion.7.refs_6_.refs_8_), channel_id=1, source_target_pairs={{0,1},{1,0},{2,3},{3,2},{4,5},{5,4},{6,7},{7,6},{8,9},{9,8},{10,11... | collective-permute-start | bytes 3145736 | tf_op jit(solution)/shard_map/ppermute | solution.py:46
  64.1 12.3 %collective-permute-done.40.refs_16_ = bf16[128,4096]{1,0:T(8,128)(2,1)S(1)} collective-permute-done((bf16[128,4096]{1,0:T(8,128)(2,1)S(1)}, bf16[128,4096]{1,0:T(8,128)(2,1)S(1)}, u32[]{:S(2)}, u32[]{:S(2)}) %collective-permute-start.40) | collective-permute-done | bytes 1048608 | tf_op jit(solution)/shard_map/ppermute | solution.py:42
  76.4 5.8 %collective-permute-start.18 = (bf16[128,4096]{1,0:T(8,128)(2,1)S(1)}, bf16[128,4096]{1,0:T(8,128)(2,1)S(1)}, u32[]{:S(2)}, u32[]{:S(2)}) collective-permute-start(bf16[128,4096]{1,0:T(8,128)(2,1)S(1)} %constant_dynamic-update-slice_fusion.7.refs_6_.refs_8_), channel_id=1, source_target_pairs={{0,32},{1,97},{2,34},{3,99},{4,36},{5,101},{6,38},{7,103},{8,40},{... | collective-permute-start | bytes 3145736 | tf_op jit(solution)/shard_map/ppermute | solution.py:42
  82.2 3.6 %collective-permute-start.32 = (bf16[128,4096]{1,0:T(8,128)(2,1)S(1)}, bf16[128,4096]{1,0:T(8,128)(2,1)}, u32[]{:S(2)}, u32[]{:S(2)}) collective-permute-start(bf16[128,4096]{1,0:T(8,128)(2,1)S(1)} %constant_dynamic-update-slice_fusion.refs_0_), channel_id=1, source_target_pairs={{0,12},{1,5},{2,14},{3,7},{4,0},{5,9},{6,2},{7,11},{8,4},{9,13},{1... | collective-permute-start | bytes 3145736 | tf_op jit(solution)/shard_map/ppermute | solution.py:42
  85.8 2.1 collective-permute-start.30
  87.9 1.0 copy-done.2
  88.9 1.5 collective-permute-start.41
  90.4 3.5 %collective-permute-done.18.refs_8_.refs_9_ = bf16[128,4096]{1,0:T(8,128)(2,1)S(1)} collective-permute-done((bf16[128,4096]{1,0:T(8,128)(2,1)S(1)}, bf16[128,4096]{1,0:T(8,128)(2,1)S(1)}, u32[]{:S(2)}, u32[]{:S(2)}) %collective-permute-start.18) | collective-permute-done | bytes 1048608 | tf_op jit(solution)/shard_map/ppermute | solution.py:42
  93.9 6.5 %collective-permute-start.39 = (bf16[128,4096]{1,0:T(8,128)(2,1)S(1)}, bf16[128,4096]{1,0:T(8,128)(2,1)S(1)}, u32[]{:S(2)}, u32[]{:S(2)}) collective-permute-start(bf16[128,4096]{1,0:T(8,128)(2,1)S(1)} %collective-permute-done.27.refs_14_), channel_id=1, source_target_pairs={{0,1},{1,0},{2,3},{3,2},{4,5},{5,4},{6,7},{7,6},{8,9},{9,8},{10,11... | collective-permute-start | bytes 3145736 | tf_op jit(solution)/shard_map/ppermute | solution.py:46
  100.4 4.7 %collective-permute-done.32.refs_4_.refs_2_ = bf16[128,4096]{1,0:T(8,128)(2,1)} collective-permute-done((bf16[128,4096]{1,0:T(8,128)(2,1)S(1)}, bf16[128,4096]{1,0:T(8,128)(2,1)}, u32[]{:S(2)}, u32[]{:S(2)}) %collective-permute-start.32) | collective-permute-done | bytes 1048608 | tf_op jit(solution)/shard_map/ppermute | solution.py:42
  105.1 1.0 copy-done.5
  106.0 8.3 %collective-permute-start.37 = (bf16[128,4096]{1,0:T(8,128)(2,1)S(1)}, bf16[128,4096]{1,0:T(8,128)(2,1)S(1)}, u32[]{:S(2)}, u32[]{:S(2)}) collective-permute-start(bf16[128,4096]{1,0:T(8,128)(2,1)S(1)} %collective-permute-done.36.refs_10_), channel_id=1, source_target_pairs={{0,1},{1,0},{2,3},{3,2},{4,5},{5,4},{6,7},{7,6},{8,9},{9,8},{10,11... | collective-permute-start | bytes 3145736 | tf_op jit(solution)/shard_map/ppermute | solution.py:46
  114.7 1.9 collective-permute-start.10
  116.7 2.4 %collective-permute-done.28.refs_4_ = bf16[128,4096]{1,0:T(8,128)(2,1)} collective-permute-done((bf16[128,4096]{1,0:T(8,128)(2,1)S(1)}, bf16[128,4096]{1,0:T(8,128)(2,1)}, u32[]{:S(2)}, u32[]{:S(2)}) %collective-permute-start.28) | collective-permute-done | bytes 1048608 | tf_op jit(solution)/shard_map/ppermute | solution.py:42
  119.1 10.4 %collective-permute-start.33 = (bf16[128,4096]{1,0:T(8,128)(2,1)}, bf16[128,4096]{1,0:T(8,128)(2,1)}, u32[]{:S(2)}, u32[]{:S(2)}) collective-permute-start(bf16[128,4096]{1,0:T(8,128)(2,1)} %collective-permute-done.32.refs_4_.refs_2_), channel_id=1, source_target_pairs={{0,1},{1,0},{2,3},{3,2},{4,5},{5,4},{6,7},{7,6},{8,9},{9,8},{10,11... | collective-permute-start | bytes 3145736 | tf_op jit(solution)/shard_map/ppermute | solution.py:46
  129.5 1.0 copy-done.15
  130.5 0.6 collective-permute-start.29
  132.1 1.5 collective-permute-done.31.refs_3_.refs_5_
  133.6 1.2 copy-done.3
  134.8 1.2 copy-done.6
  136.0 22.0 %shard_map.95.refs_8_ = f32[2,1024,512]{2,1,0:T(8,128)} custom-call(s32[384]{0:T(512)S(1)} %fusion.17.table, bf16[128,4096]{1,0:T(8,128)(2,1)S(1)} %copy-done.3, bf16[128,4096]{1,0:T(8,128)(2,1)S(1)} %copy-done.6, bf16[128,4096]{1,0:T(8,128)(2,1)} %collective-permute-done.9.refs_2_.refs_1_, bf16[128,4096]{1,0:T(8,128)(2,1)} %collective-permute-done.31.refs_3_.refs_5_, ...), custom_call_target="tpu_custom_call" | custom-call | flops 9663676416 | bytes 35651584 | tf_op jit(solution)/shard_map/pallas_call | solution.py:225
  158.1 17.3 %shard_map.96 = (f32[2,1024,512]{2,1,0:T(8,128)}, f32[8,1024]{1,0:T(8,128)S(1)}) custom-call(s32[384]{0:T(512)S(1)} %fusion.17.table, bf16[128,4096]{1,0:T(8,128)(2,1)S(1)} %collective-permute-done.10.refs_0_.refs_3_, bf16[128,4096]{1,0:T(8,128)(2,1)} %collective-permute-done.11.refs_1_.refs_7_, ...), custom_call_target="tpu_custom_call" | custom-call | flops 3221225472 | bytes 23068672 | tf_op jit(solution)/shard_map/pallas_call | solution.py:225
  175.9 0.9 collective-permute-done.42
  176.9 1.5 collective-permute-start.44
  178.9 2.2 %collective-permute-done.45 = f32[8,1024]{1,0:T(8,128)S(1)} collective-permute-done((f32[8,1024]{1,0:T(8,128)S(1)}, f32[8,1024]{1,0:T(8,128)S(1)}, u32[]{:S(2)}, u32[]{:S(2)}) %collective-permute-start.45) | collective-permute-done | bytes 32800 | tf_op jit(solution)/shard_map/ppermute | solution.py:42
  181.1 1.3 collective-permute-done.43
  182.4 1.9 collective-permute-start.48
  184.6 1.2 collective-permute-start.46
  185.8 1.0 collective-permute-done.48
  186.8 0.6 collective-permute-done.47
  187.4 1.2 collective-permute-done.46
  188.7 2.0 collective-permute-start.51
  190.9 1.2 collective-permute-start.49
  192.1 0.8 collective-permute-done.51
  193.4 1.5 collective-permute-done.49
  195.0 0.6 fusion.44
  195.6 1.2 copy-done.4
  196.8 1.2 copy-done.7
  198.0 19.2 %shard_map.97 = bf16[8192,512]{1,0:T(8,128)(2,1)} custom-call(s32[384]{0:T(512)S(1)} %fusion.17.table, bf16[128,4096]{1,0:T(8,128)(2,1)S(1)} %copy-done.4, bf16[128,4096]{1,0:T(8,128)(2,1)} %collective-permute-done.9.refs_2_.refs_1_, bf16[128,4096]{1,0:T(8,128)(2,1)} %collective-permute-done.32.refs_4_.refs_2_, ...), custom_call_target="tpu_custom_call" | custom-call | flops 8589934592 | bytes 27262976 | tf_op jit(solution)/shard_map/pallas_call | solution.py:249
  (127 shorter events, 5.8 us)
Async XLA Ops:
  1.5 10.3 %collective-permute-start.2 = (bf16[8,2048]{1,0:T(8,128)(2,1)S(1)}, bf16[8,2048]{1,0:T(8,128)(2,1)S(1)}, u32[]{:S(2)}, u32[]{:S(2)}) collective-permute-start(bf16[8,2048]{1,0:T(8,128)(2,1)S(1)} %get-tuple-element.16), channel_id=1, source_target_pairs={{0,1},{1,0},{2,3},{3,2},{4,5},{5,4},{6,7},{7,6},{8,9},{9,8},{10,11... | collective-permute-start | bytes 98312 | tf_op jit(solution)/shard_map/ppermute | solution.py:46
  2.9 11.2 %collective-permute-start.1 = (bf16[8,2048]{1,0:T(8,128)(2,1)S(1)}, bf16[8,2048]{1,0:T(8,128)(2,1)S(1)}, u32[]{:S(2)}, u32[]{:S(2)}) collective-permute-start(bf16[8,2048]{1,0:T(8,128)(2,1)S(1)} %get-tuple-element.17), channel_id=1, source_target_pairs={{0,2},{1,3},{2,0},{3,1},{4,6},{5,7},{6,4},{7,5},{8,10},{9,11},{10,... | collective-permute-start | bytes 98312 | tf_op jit(solution)/shard_map/ppermute | solution.py:46
  6.6 7.5 %collective-permute-start = (bf16[8,2048]{1,0:T(8,128)(2,1)S(1)}, bf16[8,2048]{1,0:T(8,128)(2,1)S(1)}, u32[]{:S(2)}, u32[]{:S(2)}) collective-permute-start(bf16[8,2048]{1,0:T(8,128)(2,1)S(1)} %get-tuple-element.18), channel_id=1, source_target_pairs={{0,3},{1,2},{2,1},{3,0},{4,7},{5,6},{6,5},{7,4},{8,11},{9,10},{10,... | collective-permute-start | bytes 98312 | tf_op jit(solution)/shard_map/ppermute | solution.py:46
  8.6 14.8 %collective-permute-start.23 = (bf16[8,4096]{1,0:T(8,128)(2,1)S(1)}, bf16[8,4096]{1,0:T(8,128)(2,1)S(1)}, u32[]{:S(2)}, u32[]{:S(2)}) collective-permute-start(bf16[8,4096]{1,0:T(8,128)(2,1)S(1)} %get-tuple-element.7), channel_id=1, source_target_pairs={{0,8},{1,9},{2,10},{3,11},{4,12},{5,13},{6,14},{7,15},{8,0},{9,1},... | collective-permute-start | bytes 196616 | tf_op jit(solution)/shard_map/ppermute | solution.py:42
  11.5 11.5 %collective-permute-start.22 = (bf16[8,4096]{1,0:T(8,128)(2,1)S(1)}, bf16[8,4096]{1,0:T(8,128)(2,1)S(1)}, u32[]{:S(2)}, u32[]{:S(2)}) collective-permute-start(bf16[8,4096]{1,0:T(8,128)(2,1)S(1)} %get-tuple-element.7), channel_id=1, source_target_pairs={{0,12},{1,5},{2,14},{3,7},{4,0},{5,9},{6,2},{7,11},{8,4},{9,13},{1... | collective-permute-start | bytes 196616 | tf_op jit(solution)/shard_map/ppermute | solution.py:42
  11.8 8.3 %collective-permute-start.21 = (bf16[8,4096]{1,0:T(8,128)(2,1)S(1)}, bf16[8,4096]{1,0:T(8,128)(2,1)S(1)}, u32[]{:S(2)}, u32[]{:S(2)}) collective-permute-start(bf16[8,4096]{1,0:T(8,128)(2,1)S(1)} %get-tuple-element.7), channel_id=1, source_target_pairs={{0,4},{1,13},{2,6},{3,15},{4,8},{5,1},{6,10},{7,3},{8,12},{9,5},{1... | collective-permute-start | bytes 196616 | tf_op jit(solution)/shard_map/ppermute | solution.py:42
  15.0 115.5 %copy-start.9 = (s32[1024]{0:T(1024)S(1)}, s32[1024]{0:T(1024)}, u32[]{:S(2)}) copy-start(s32[1024]{0:T(1024)} %param.15) | copy-start | bytes 12292
  15.0 115.5 %copy-start.10 = (s32[1024]{0:T(1024)S(1)}, s32[1024]{0:T(1024)}, u32[]{:S(2)}) copy-start(s32[1024]{0:T(1024)} %param.14) | copy-start | bytes 12292
  16.1 17.0 %collective-permute-start.14 = (bf16[8,4096]{1,0:T(8,128)(2,1)S(1)}, bf16[8,4096]{1,0:T(8,128)(2,1)S(1)}, u32[]{:S(2)}, u32[]{:S(2)}) collective-permute-start(bf16[8,4096]{1,0:T(8,128)(2,1)S(1)} %get-tuple-element.12), channel_id=1, source_target_pairs={{0,2},{1,3},{2,0},{3,1},{4,6},{5,7},{6,4},{7,5},{8,10},{9,11},{10,... | collective-permute-start | bytes 196616 | tf_op jit(solution)/shard_map/ppermute | solution.py:42
  19.3 13.7 %collective-permute-start.13 = (bf16[8,4096]{1,0:T(8,128)(2,1)S(1)}, bf16[8,4096]{1,0:T(8,128)(2,1)S(1)}, u32[]{:S(2)}, u32[]{:S(2)}) collective-permute-start(bf16[8,4096]{1,0:T(8,128)(2,1)S(1)} %get-tuple-element.12), channel_id=1, source_target_pairs={{0,18},{1,17},{2,16},{3,19},{4,22},{5,21},{6,20},{7,23},{8,26},{9,... | collective-permute-start | bytes 196616 | tf_op jit(solution)/shard_map/ppermute | solution.py:42
  20.0 5.8 %collective-permute-start.5 = (bf16[8,4096]{1,0:T(8,128)(2,1)S(1)}, bf16[8,4096]{1,0:T(8,128)(2,1)S(1)}, u32[]{:S(2)}, u32[]{:S(2)}) collective-permute-start(bf16[8,4096]{1,0:T(8,128)(2,1)S(1)} %get-tuple-element.15), channel_id=1, source_target_pairs={{0,64},{1,65},{2,66},{3,67},{4,68},{5,69},{6,70},{7,71},{8,72},{9,... | collective-permute-start | bytes 196616 | tf_op jit(solution)/shard_map/ppermute | solution.py:42
  23.0 4.9 %collective-permute-start.4 = (bf16[8,4096]{1,0:T(8,128)(2,1)S(1)}, bf16[8,4096]{1,0:T(8,128)(2,1)S(1)}, u32[]{:S(2)}, u32[]{:S(2)}) collective-permute-start(bf16[8,4096]{1,0:T(8,128)(2,1)S(1)} %get-tuple-element.15), channel_id=1, source_target_pairs={{0,96},{1,33},{2,98},{3,35},{4,100},{5,37},{6,102},{7,39},{8,104},... | collective-permute-start | bytes 196616 | tf_op jit(solution)/shard_map/ppermute | solution.py:42
  23.5 6.8 %collective-permute-start.3 = (bf16[8,4096]{1,0:T(8,128)(2,1)S(1)}, bf16[8,4096]{1,0:T(8,128)(2,1)S(1)}, u32[]{:S(2)}, u32[]{:S(2)}) collective-permute-start(bf16[8,4096]{1,0:T(8,128)(2,1)S(1)} %get-tuple-element.15), channel_id=1, source_target_pairs={{0,32},{1,97},{2,34},{3,99},{4,36},{5,101},{6,38},{7,103},{8,40},{... | collective-permute-start | bytes 196616 | tf_op jit(solution)/shard_map/ppermute | solution.py:42
  25.8 4.8 %collective-permute-start.12 = (bf16[8,4096]{1,0:T(8,128)(2,1)S(1)}, bf16[8,4096]{1,0:T(8,128)(2,1)S(1)}, u32[]{:S(2)}, u32[]{:S(2)}) collective-permute-start(bf16[8,4096]{1,0:T(8,128)(2,1)S(1)} %get-tuple-element.12), channel_id=1, source_target_pairs={{0,16},{1,19},{2,18},{3,17},{4,20},{5,23},{6,22},{7,21},{8,24},{9,... | collective-permute-start | bytes 196616 | tf_op jit(solution)/shard_map/ppermute | solution.py:42
  27.9 15.4 %collective-permute-start.26 = (bf16[32,4096]{1,0:T(8,128)(2,1)S(1)}, bf16[32,4096]{1,0:T(8,128)(2,1)S(1)}, u32[]{:S(2)}, u32[]{:S(2)}) collective-permute-start(bf16[32,4096]{1,0:T(8,128)(2,1)S(1)} %pad_maximum_fusion.2), channel_id=1, source_target_pairs={{0,64},{1,65},{2,66},{3,67},{4,68},{5,69},{6,70},{7,71},{8,72},{9,... | collective-permute-start | bytes 786440 | tf_op jit(solution)/shard_map/ppermute | solution.py:42
  30.2 13.0 %collective-permute-start.25 = (bf16[32,4096]{1,0:T(8,128)(2,1)S(1)}, bf16[32,4096]{1,0:T(8,128)(2,1)S(1)}, u32[]{:S(2)}, u32[]{:S(2)}) collective-permute-start(bf16[32,4096]{1,0:T(8,128)(2,1)S(1)} %pad_maximum_fusion.2), channel_id=1, source_target_pairs={{0,96},{1,33},{2,98},{3,35},{4,100},{5,37},{6,102},{7,39},{8,104},... | collective-permute-start | bytes 786440 | tf_op jit(solution)/shard_map/ppermute | solution.py:42
  30.6 11.5 %collective-permute-start.24 = (bf16[32,4096]{1,0:T(8,128)(2,1)S(1)}, bf16[32,4096]{1,0:T(8,128)(2,1)S(1)}, u32[]{:S(2)}, u32[]{:S(2)}) collective-permute-start(bf16[32,4096]{1,0:T(8,128)(2,1)S(1)} %pad_maximum_fusion.2), channel_id=1, source_target_pairs={{0,32},{1,97},{2,34},{3,99},{4,36},{5,101},{6,38},{7,103},{8,40},{... | collective-permute-start | bytes 786440 | tf_op jit(solution)/shard_map/ppermute | solution.py:42
  33.0 28.8 %collective-permute-start.8 = (bf16[32,4096]{1,0:T(8,128)(2,1)S(1)}, bf16[32,4096]{1,0:T(8,128)(2,1)S(1)}, u32[]{:S(2)}, u32[]{:S(2)}) collective-permute-start(bf16[32,4096]{1,0:T(8,128)(2,1)S(1)} %pad_maximum_fusion), channel_id=1, source_target_pairs={{0,2},{1,3},{2,0},{3,1},{4,6},{5,7},{6,4},{7,5},{8,10},{9,11},{10,... | collective-permute-start | bytes 786440 | tf_op jit(solution)/shard_map/ppermute | solution.py:42
  33.1 27.7 %collective-permute-start.7 = (bf16[32,4096]{1,0:T(8,128)(2,1)S(1)}, bf16[32,4096]{1,0:T(8,128)(2,1)S(1)}, u32[]{:S(2)}, u32[]{:S(2)}) collective-permute-start(bf16[32,4096]{1,0:T(8,128)(2,1)S(1)} %pad_maximum_fusion), channel_id=1, source_target_pairs={{0,18},{1,17},{2,16},{3,19},{4,22},{5,21},{6,20},{7,23},{8,26},{9,... | collective-permute-start | bytes 786440 | tf_op jit(solution)/shard_map/ppermute | solution.py:42
  42.2 5.2 %collective-permute-start.6 = (bf16[32,4096]{1,0:T(8,128)(2,1)S(1)}, bf16[32,4096]{1,0:T(8,128)(2,1)S(1)}, u32[]{:S(2)}, u32[]{:S(2)}) collective-permute-start(bf16[32,4096]{1,0:T(8,128)(2,1)S(1)} %pad_maximum_fusion), channel_id=1, source_target_pairs={{0,16},{1,19},{2,18},{3,17},{4,20},{5,23},{6,22},{7,21},{8,24},{9,... | collective-permute-start | bytes 786440 | tf_op jit(solution)/shard_map/ppermute | solution.py:42
  43.2 17.5 %collective-permute-start.17 = (bf16[32,4096]{1,0:T(8,128)(2,1)S(1)}, bf16[32,4096]{1,0:T(8,128)(2,1)S(1)}, u32[]{:S(2)}, u32[]{:S(2)}) collective-permute-start(bf16[32,4096]{1,0:T(8,128)(2,1)S(1)} %pad_maximum_fusion.1), channel_id=1, source_target_pairs={{0,8},{1,9},{2,10},{3,11},{4,12},{5,13},{6,14},{7,15},{8,0},{9,1},... | collective-permute-start | bytes 786440 | tf_op jit(solution)/shard_map/ppermute | solution.py:42
  43.2 13.1 %collective-permute-start.16 = (bf16[32,4096]{1,0:T(8,128)(2,1)S(1)}, bf16[32,4096]{1,0:T(8,128)(2,1)S(1)}, u32[]{:S(2)}, u32[]{:S(2)}) collective-permute-start(bf16[32,4096]{1,0:T(8,128)(2,1)S(1)} %pad_maximum_fusion.1), channel_id=1, source_target_pairs={{0,12},{1,5},{2,14},{3,7},{4,0},{5,9},{6,2},{7,11},{8,4},{9,13},{1... | collective-permute-start | bytes 786440 | tf_op jit(solution)/shard_map/ppermute | solution.py:42
  43.4 71.0 %copy-start.8 = (bf16[128,4096]{1,0:T(8,128)(2,1)}, bf16[128,4096]{1,0:T(8,128)(2,1)S(1)}, u32[]{:S(2)}) copy-start(bf16[128,4096]{1,0:T(8,128)(2,1)S(1)} %constant_dynamic-update-slice_fusion.14.refs_12_) | copy-start | bytes 3145732
  47.4 8.3 %collective-permute-start.15 = (bf16[32,4096]{1,0:T(8,128)(2,1)S(1)}, bf16[32,4096]{1,0:T(8,128)(2,1)S(1)}, u32[]{:S(2)}, u32[]{:S(2)}) collective-permute-start(bf16[32,4096]{1,0:T(8,128)(2,1)S(1)} %pad_maximum_fusion.1), channel_id=1, source_target_pairs={{0,4},{1,13},{2,6},{3,15},{4,8},{5,1},{6,10},{7,3},{8,12},{9,5},{1... | collective-permute-start | bytes 786440 | tf_op jit(solution)/shard_map/ppermute | solution.py:42
  55.7 20.7 %collective-permute-start.40 = (bf16[128,4096]{1,0:T(8,128)(2,1)S(1)}, bf16[128,4096]{1,0:T(8,128)(2,1)S(1)}, u32[]{:S(2)}, u32[]{:S(2)}) collective-permute-start(bf16[128,4096]{1,0:T(8,128)(2,1)S(1)} %constant_dynamic-update-slice_fusion.14.refs_12_), channel_id=1, source_target_pairs={{0,18},{1,17},{2,16},{3,19},{4,22},{5,21},{6,20},{7,23},{8,26},{9,... | collective-permute-start | bytes 3145736 | tf_op jit(solution)/shard_map/ppermute | solution.py:42
  56.3 25.9 %collective-permute-start.38 = (bf16[128,4096]{1,0:T(8,128)(2,1)S(1)}, bf16[128,4096]{1,0:T(8,128)(2,1)S(1)}, u32[]{:S(2)}, u32[]{:S(2)}) collective-permute-start(bf16[128,4096]{1,0:T(8,128)(2,1)S(1)} %constant_dynamic-update-slice_fusion.14.refs_12_), channel_id=1, source_target_pairs={{0,1},{1,0},{2,3},{3,2},{4,5},{5,4},{6,7},{7,6},{8,9},{9,8},{10,11... | collective-permute-start | bytes 3145736 | tf_op jit(solution)/shard_map/ppermute | solution.py:46
  60.7 25.1 %collective-permute-start.27 = (bf16[128,4096]{1,0:T(8,128)(2,1)S(1)}, bf16[128,4096]{1,0:T(8,128)(2,1)S(1)}, u32[]{:S(2)}, u32[]{:S(2)}) collective-permute-start(bf16[128,4096]{1,0:T(8,128)(2,1)S(1)} %constant_dynamic-update-slice_fusion.14.refs_12_), channel_id=1, source_target_pairs={{0,16},{1,19},{2,18},{3,17},{4,20},{5,23},{6,22},{7,21},{8,24},{9,... | collective-permute-start | bytes 3145736 | tf_op jit(solution)/shard_map/ppermute | solution.py:42
  60.8 53.9 %copy-start.11 = (bf16[128,4096]{1,0:T(8,128)(2,1)}, bf16[128,4096]{1,0:T(8,128)(2,1)S(1)}, u32[]{:S(2)}) copy-start(bf16[128,4096]{1,0:T(8,128)(2,1)S(1)} %constant_dynamic-update-slice_fusion.7.refs_6_.refs_8_) | copy-start | bytes 3145732
  60.9 27.0 %collective-permute-start.36 = (bf16[128,4096]{1,0:T(8,128)(2,1)S(1)}, bf16[128,4096]{1,0:T(8,128)(2,1)S(1)}, u32[]{:S(2)}, u32[]{:S(2)}) collective-permute-start(bf16[128,4096]{1,0:T(8,128)(2,1)S(1)} %constant_dynamic-update-slice_fusion.7.refs_6_.refs_8_), channel_id=1, source_target_pairs={{0,96},{1,33},{2,98},{3,35},{4,100},{5,37},{6,102},{7,39},{8,104},... | collective-permute-start | bytes 3145736 | tf_op jit(solution)/shard_map/ppermute | solution.py:42
  61.8 27.1 %collective-permute-start.34 = (bf16[128,4096]{1,0:T(8,128)(2,1)S(1)}, bf16[128,4096]{1,0:T(8,128)(2,1)S(1)}, u32[]{:S(2)}, u32[]{:S(2)}) collective-permute-start(bf16[128,4096]{1,0:T(8,128)(2,1)S(1)} %constant_dynamic-update-slice_fusion.7.refs_6_.refs_8_), channel_id=1, source_target_pairs={{0,1},{1,0},{2,3},{3,2},{4,5},{5,4},{6,7},{7,6},{8,9},{9,8},{10,11... | collective-permute-start | bytes 3145736 | tf_op jit(solution)/shard_map/ppermute | solution.py:46
  76.4 53.1 %copy-start.16 = (bf16[128,4096]{1,0:T(8,128)(2,1)}, bf16[128,4096]{1,0:T(8,128)(2,1)S(1)}, u32[]{:S(2)}) copy-start(bf16[128,4096]{1,0:T(8,128)(2,1)S(1)} %collective-permute-done.40.refs_16_) | copy-start | bytes 3145732
  76.4 17.5 %collective-permute-start.18 = (bf16[128,4096]{1,0:T(8,128)(2,1)S(1)}, bf16[128,4096]{1,0:T(8,128)(2,1)S(1)}, u32[]{:S(2)}, u32[]{:S(2)}) collective-permute-start(bf16[128,4096]{1,0:T(8,128)(2,1)S(1)} %constant_dynamic-update-slice_fusion.7.refs_6_.refs_8_), channel_id=1, source_target_pairs={{0,32},{1,97},{2,34},{3,99},{4,36},{5,101},{6,38},{7,103},{8,40},{... | collective-permute-start | bytes 3145736 | tf_op jit(solution)/shard_map/ppermute | solution.py:42
  82.2 47.2 %copy-start.17 = (bf16[128,4096]{1,0:T(8,128)(2,1)}, bf16[128,4096]{1,0:T(8,128)(2,1)S(1)}, u32[]{:S(2)}) copy-start(bf16[128,4096]{1,0:T(8,128)(2,1)S(1)} %collective-permute-done.38.refs_13_) | copy-start | bytes 3145732
  82.2 22.8 %collective-permute-start.32 = (bf16[128,4096]{1,0:T(8,128)(2,1)S(1)}, bf16[128,4096]{1,0:T(8,128)(2,1)}, u32[]{:S(2)}, u32[]{:S(2)}) collective-permute-start(bf16[128,4096]{1,0:T(8,128)(2,1)S(1)} %constant_dynamic-update-slice_fusion.refs_0_), channel_id=1, source_target_pairs={{0,12},{1,5},{2,14},{3,7},{4,0},{5,9},{6,2},{7,11},{8,4},{9,13},{1... | collective-permute-start | bytes 3145736 | tf_op jit(solution)/shard_map/ppermute | solution.py:42
  85.8 43.7 %copy-start.18 = (bf16[128,4096]{1,0:T(8,128)(2,1)}, bf16[128,4096]{1,0:T(8,128)(2,1)S(1)}, u32[]{:S(2)}) copy-start(bf16[128,4096]{1,0:T(8,128)(2,1)S(1)} %collective-permute-done.27.refs_14_) | copy-start | bytes 3145732
  85.8 19.2 %collective-permute-start.30 = (bf16[128,4096]{1,0:T(8,128)(2,1)S(1)}, bf16[128,4096]{1,0:T(8,128)(2,1)S(1)}, u32[]{:S(2)}, u32[]{:S(2)}) collective-permute-start(bf16[128,4096]{1,0:T(8,128)(2,1)S(1)} %constant_dynamic-update-slice_fusion.refs_0_), channel_id=1, source_target_pairs={{0,1},{1,0},{2,3},{3,2},{4,5},{5,4},{6,7},{7,6},{8,9},{9,8},{10,11... | collective-permute-start | bytes 3145736 | tf_op jit(solution)/shard_map/ppermute | solution.py:46
  87.9 26.8 %copy-start.12 = (bf16[128,4096]{1,0:T(8,128)(2,1)}, bf16[128,4096]{1,0:T(8,128)(2,1)S(1)}, u32[]{:S(2)}) copy-start(bf16[128,4096]{1,0:T(8,128)(2,1)S(1)} %collective-permute-done.36.refs_10_) | copy-start | bytes 3145732
  87.9 26.4 %collective-permute-start.9 = (bf16[128,4096]{1,0:T(8,128)(2,1)S(1)}, bf16[128,4096]{1,0:T(8,128)(2,1)}, u32[]{:S(2)}, u32[]{:S(2)}) collective-permute-start(bf16[128,4096]{1,0:T(8,128)(2,1)S(1)} %constant_dynamic-update-slice_fusion.refs_0_), channel_id=1, source_target_pairs={{0,4},{1,13},{2,6},{3,15},{4,8},{5,1},{6,10},{7,3},{8,12},{9,5},{1... | collective-permute-start | bytes 3145736 | tf_op jit(solution)/shard_map/ppermute | solution.py:42
  88.9 40.5 %copy-start.13 = (bf16[128,4096]{1,0:T(8,128)(2,1)}, bf16[128,4096]{1,0:T(8,128)(2,1)S(1)}, u32[]{:S(2)}) copy-start(bf16[128,4096]{1,0:T(8,128)(2,1)S(1)} %collective-permute-done.34.refs_7_.refs_12_) | copy-start | bytes 3145732
  88.9 25.4 %collective-permute-start.41 = (bf16[128,4096]{1,0:T(8,128)(2,1)S(1)}, bf16[128,4096]{1,0:T(8,128)(2,1)S(1)}, u32[]{:S(2)}, u32[]{:S(2)}) collective-permute-start(bf16[128,4096]{1,0:T(8,128)(2,1)S(1)} %collective-permute-done.40.refs_16_), channel_id=1, source_target_pairs={{0,1},{1,0},{2,3},{3,2},{4,5},{5,4},{6,7},{7,6},{8,9},{9,8},{10,11... | collective-permute-start | bytes 3145736 | tf_op jit(solution)/shard_map/ppermute | solution.py:46
  93.9 37.2 %copy-start.14 = (bf16[128,4096]{1,0:T(8,128)(2,1)}, bf16[128,4096]{1,0:T(8,128)(2,1)S(1)}, u32[]{:S(2)}) copy-start(bf16[128,4096]{1,0:T(8,128)(2,1)S(1)} %collective-permute-done.18.refs_8_.refs_9_) | copy-start | bytes 3145732
  93.9 20.8 %collective-permute-start.39 = (bf16[128,4096]{1,0:T(8,128)(2,1)S(1)}, bf16[128,4096]{1,0:T(8,128)(2,1)S(1)}, u32[]{:S(2)}, u32[]{:S(2)}) collective-permute-start(bf16[128,4096]{1,0:T(8,128)(2,1)S(1)} %collective-permute-done.27.refs_14_), channel_id=1, source_target_pairs={{0,1},{1,0},{2,3},{3,2},{4,5},{5,4},{6,7},{7,6},{8,9},{9,8},{10,11... | collective-permute-start | bytes 3145736 | tf_op jit(solution)/shard_map/ppermute | solution.py:46
  105.0 14.0 %collective-permute-start.28 = (bf16[128,4096]{1,0:T(8,128)(2,1)S(1)}, bf16[128,4096]{1,0:T(8,128)(2,1)}, u32[]{:S(2)}, u32[]{:S(2)}) collective-permute-start(bf16[128,4096]{1,0:T(8,128)(2,1)S(1)} %collective-permute-done.27.refs_14_), channel_id=1, source_target_pairs={{0,16},{1,19},{2,18},{3,17},{4,20},{5,23},{6,22},{7,21},{8,24},{9,... | collective-permute-start | bytes 3145736 | tf_op jit(solution)/shard_map/ppermute | solution.py:42
  106.0 23.4 %collective-permute-start.37 = (bf16[128,4096]{1,0:T(8,128)(2,1)S(1)}, bf16[128,4096]{1,0:T(8,128)(2,1)S(1)}, u32[]{:S(2)}, u32[]{:S(2)}) collective-permute-start(bf16[128,4096]{1,0:T(8,128)(2,1)S(1)} %collective-permute-done.36.refs_10_), channel_id=1, source_target_pairs={{0,1},{1,0},{2,3},{3,2},{4,5},{5,4},{6,7},{7,6},{8,9},{9,8},{10,11... | collective-permute-start | bytes 3145736 | tf_op jit(solution)/shard_map/ppermute | solution.py:46
  114.3 16.2 %collective-permute-start.35 = (bf16[128,4096]{1,0:T(8,128)(2,1)S(1)}, bf16[128,4096]{1,0:T(8,128)(2,1)}, u32[]{:S(2)}, u32[]{:S(2)}) collective-permute-start(bf16[128,4096]{1,0:T(8,128)(2,1)S(1)} %collective-permute-done.18.refs_8_.refs_9_), channel_id=1, source_target_pairs={{0,1},{1,0},{2,3},{3,2},{4,5},{5,4},{6,7},{7,6},{8,9},{9,8},{10,11... | collective-permute-start | bytes 3145736 | tf_op jit(solution)/shard_map/ppermute | solution.py:46
  114.4 16.8 %collective-permute-start.19 = (bf16[128,4096]{1,0:T(8,128)(2,1)S(1)}, bf16[128,4096]{1,0:T(8,128)(2,1)S(1)}, u32[]{:S(2)}, u32[]{:S(2)}) collective-permute-start(bf16[128,4096]{1,0:T(8,128)(2,1)S(1)} %collective-permute-done.18.refs_8_.refs_9_), channel_id=1, source_target_pairs={{0,32},{1,97},{2,34},{3,99},{4,36},{5,101},{6,38},{7,103},{8,40},{... | collective-permute-start | bytes 3145736 | tf_op jit(solution)/shard_map/ppermute | solution.py:42
  114.7 16.5 %collective-permute-start.10 = (bf16[128,4096]{1,0:T(8,128)(2,1)}, bf16[128,4096]{1,0:T(8,128)(2,1)S(1)}, u32[]{:S(2)}, u32[]{:S(2)}) collective-permute-start(bf16[128,4096]{1,0:T(8,128)(2,1)} %collective-permute-done.9.refs_2_.refs_1_), channel_id=1, source_target_pairs={{0,4},{1,13},{2,6},{3,15},{4,8},{5,1},{6,10},{7,3},{8,12},{9,5},{1... | collective-permute-start | bytes 3145736 | tf_op jit(solution)/shard_map/ppermute | solution.py:42
  119.1 13.0 %collective-permute-start.33 = (bf16[128,4096]{1,0:T(8,128)(2,1)}, bf16[128,4096]{1,0:T(8,128)(2,1)}, u32[]{:S(2)}, u32[]{:S(2)}) collective-permute-start(bf16[128,4096]{1,0:T(8,128)(2,1)} %collective-permute-done.32.refs_4_.refs_2_), channel_id=1, source_target_pairs={{0,1},{1,0},{2,3},{3,2},{4,5},{5,4},{6,7},{7,6},{8,9},{9,8},{10,11... | collective-permute-start | bytes 3145736 | tf_op jit(solution)/shard_map/ppermute | solution.py:46
  130.5 3.1 %collective-permute-start.31 = (bf16[128,4096]{1,0:T(8,128)(2,1)}, bf16[128,4096]{1,0:T(8,128)(2,1)}, u32[]{:S(2)}, u32[]{:S(2)}) collective-permute-start(bf16[128,4096]{1,0:T(8,128)(2,1)} %collective-permute-done.9.refs_2_.refs_1_), channel_id=1, source_target_pairs={{0,1},{1,0},{2,3},{3,2},{4,5},{5,4},{6,7},{7,6},{8,9},{9,8},{10,11... | collective-permute-start | bytes 3145736 | tf_op jit(solution)/shard_map/ppermute | solution.py:46
  130.5 27.5 %collective-permute-start.29 = (bf16[128,4096]{1,0:T(8,128)(2,1)}, bf16[128,4096]{1,0:T(8,128)(2,1)}, u32[]{:S(2)}, u32[]{:S(2)}) collective-permute-start(bf16[128,4096]{1,0:T(8,128)(2,1)} %collective-permute-done.28.refs_4_), channel_id=1, source_target_pairs={{0,1},{1,0},{2,3},{3,2},{4,5},{5,4},{6,7},{7,6},{8,9},{9,8},{10,11... | collective-permute-start | bytes 3145736 | tf_op jit(solution)/shard_map/ppermute | solution.py:46
  131.1 26.9 %copy-start = (bf16[128,4096]{1,0:T(8,128)(2,1)}, bf16[128,4096]{1,0:T(8,128)(2,1)S(1)}, u32[]{:S(2)}) copy-start(bf16[128,4096]{1,0:T(8,128)(2,1)S(1)} %collective-permute-done.19.refs_2_.refs_11_) | copy-start | bytes 3145732
  131.1 26.9 %collective-permute-start.20 = (bf16[128,4096]{1,0:T(8,128)(2,1)S(1)}, bf16[128,4096]{1,0:T(8,128)(2,1)S(1)}, u32[]{:S(2)}, u32[]{:S(2)}) collective-permute-start(bf16[128,4096]{1,0:T(8,128)(2,1)S(1)} %collective-permute-done.19.refs_2_.refs_11_), channel_id=1, source_target_pairs={{0,1},{1,0},{2,3},{3,2},{4,5},{5,4},{6,7},{7,6},{8,9},{9,8},{10,11... | collective-permute-start | bytes 3145736 | tf_op jit(solution)/shard_map/ppermute | solution.py:46
  131.2 26.8 %collective-permute-start.11 = (bf16[128,4096]{1,0:T(8,128)(2,1)S(1)}, bf16[128,4096]{1,0:T(8,128)(2,1)}, u32[]{:S(2)}, u32[]{:S(2)}) collective-permute-start(bf16[128,4096]{1,0:T(8,128)(2,1)S(1)} %collective-permute-done.10.refs_0_.refs_3_), channel_id=1, source_target_pairs={{0,1},{1,0},{2,3},{3,2},{4,5},{5,4},{6,7},{7,6},{8,9},{9,8},{10,11... | collective-permute-start | bytes 3145736 | tf_op jit(solution)/shard_map/ppermute | solution.py:46
  158.0 17.4 %copy-start.1 = (bf16[128,4096]{1,0:T(8,128)(2,1)}, bf16[128,4096]{1,0:T(8,128)(2,1)S(1)}, u32[]{:S(2)}) copy-start(bf16[128,4096]{1,0:T(8,128)(2,1)S(1)} %collective-permute-done.20.refs_3_.refs_15_) | copy-start | bytes 3145732
  175.4 1.3 collective-permute-start.42
  176.8 4.3 %collective-permute-start.45 = (f32[8,1024]{1,0:T(8,128)S(1)}, f32[8,1024]{1,0:T(8,128)S(1)}, u32[]{:S(2)}, u32[]{:S(2)}) collective-permute-start(f32[8,1024]{1,0:T(8,128)S(1)} %add_select_fusion.3), channel_id=1, source_target_pairs={{0,8},{1,9},{2,10},{3,11},{4,12},{5,13},{6,14},{7,15},{8,0},{9,1},... | collective-permute-start | bytes 98312 | tf_op jit(solution)/shard_map/ppermute | solution.py:42
  176.9 4.3 %collective-permute-start.44 = (f32[8,1024]{1,0:T(8,128)S(1)}, f32[8,1024]{1,0:T(8,128)S(1)}, u32[]{:S(2)}, u32[]{:S(2)}) collective-permute-start(f32[8,1024]{1,0:T(8,128)S(1)} %add_select_fusion.3), channel_id=1, source_target_pairs={{0,12},{1,13},{2,14},{3,15},{4,0},{5,1},{6,2},{7,3},{8,4},{9,5},{1... | collective-permute-start | bytes 98312 | tf_op jit(solution)/shard_map/ppermute | solution.py:42
  178.4 4.0 %collective-permute-start.43 = (f32[8,1024]{1,0:T(8,128)S(1)}, f32[8,1024]{1,0:T(8,128)S(1)}, u32[]{:S(2)}, u32[]{:S(2)}) collective-permute-start(f32[8,1024]{1,0:T(8,128)S(1)} %add_select_fusion.3), channel_id=1, source_target_pairs={{0,4},{1,5},{2,6},{3,7},{4,8},{5,9},{6,10},{7,11},{8,12},{9,13},{1... | collective-permute-start | bytes 98312 | tf_op jit(solution)/shard_map/ppermute | solution.py:42
  182.4 4.3 %collective-permute-start.48 = (f32[8,1024]{1,0:T(8,128)S(1)}, f32[8,1024]{1,0:T(8,128)S(1)}, u32[]{:S(2)}, u32[]{:S(2)}) collective-permute-start(f32[8,1024]{1,0:T(8,128)S(1)} %add_select_fusion.2), channel_id=1, source_target_pairs={{0,64},{1,65},{2,66},{3,67},{4,68},{5,69},{6,70},{7,71},{8,72},{9,... | collective-permute-start | bytes 98312 | tf_op jit(solution)/shard_map/ppermute | solution.py:42
  184.3 3.1 %collective-permute-start.47 = (f32[8,1024]{1,0:T(8,128)S(1)}, f32[8,1024]{1,0:T(8,128)S(1)}, u32[]{:S(2)}, u32[]{:S(2)}) collective-permute-start(f32[8,1024]{1,0:T(8,128)S(1)} %add_select_fusion.2), channel_id=1, source_target_pairs={{0,96},{1,97},{2,98},{3,99},{4,100},{5,101},{6,102},{7,103},{8,104... | collective-permute-start | bytes 98312 | tf_op jit(solution)/shard_map/ppermute | solution.py:42
  184.6 4.0 %collective-permute-start.46 = (f32[8,1024]{1,0:T(8,128)S(1)}, f32[8,1024]{1,0:T(8,128)S(1)}, u32[]{:S(2)}, u32[]{:S(2)}) collective-permute-start(f32[8,1024]{1,0:T(8,128)S(1)} %add_select_fusion.2), channel_id=1, source_target_pairs={{0,32},{1,33},{2,34},{3,35},{4,36},{5,37},{6,38},{7,39},{8,40},{9,... | collective-permute-start | bytes 98312 | tf_op jit(solution)/shard_map/ppermute | solution.py:42
  188.7 4.3 %collective-permute-start.51 = (f32[8,1024]{1,0:T(8,128)S(1)}, f32[8,1024]{1,0:T(8,128)S(1)}, u32[]{:S(2)}, u32[]{:S(2)}) collective-permute-start(f32[8,1024]{1,0:T(8,128)S(1)} %add_select_fusion.1), channel_id=1, source_target_pairs={{0,2},{1,3},{2,0},{3,1},{4,6},{5,7},{6,4},{7,5},{8,10},{9,11},{10,... | collective-permute-start | bytes 98312 | tf_op jit(solution)/shard_map/ppermute | solution.py:42
  190.7 2.8 %collective-permute-start.50 = (f32[8,1024]{1,0:T(8,128)S(1)}, f32[8,1024]{1,0:T(8,128)S(1)}, u32[]{:S(2)}, u32[]{:S(2)}) collective-permute-start(f32[8,1024]{1,0:T(8,128)S(1)} %add_select_fusion.1), channel_id=1, source_target_pairs={{0,18},{1,19},{2,16},{3,17},{4,22},{5,23},{6,20},{7,21},{8,26},{9,... | collective-permute-start | bytes 98312 | tf_op jit(solution)/shard_map/ppermute | solution.py:42
  190.9 4.0 %collective-permute-start.49 = (f32[8,1024]{1,0:T(8,128)S(1)}, f32[8,1024]{1,0:T(8,128)S(1)}, u32[]{:S(2)}, u32[]{:S(2)}) collective-permute-start(f32[8,1024]{1,0:T(8,128)S(1)} %add_select_fusion.1), channel_id=1, source_target_pairs={{0,16},{1,17},{2,18},{3,19},{4,20},{5,21},{6,22},{7,23},{8,24},{9,... | collective-permute-start | bytes 98312 | tf_op jit(solution)/shard_map/ppermute | solution.py:42
  (9 other events, 37.8 us)

commit v2 on v0

v2 whole, which is shorter than its diff:
```python
import jax
import jax.numpy as jnp
from jax import lax
from jax.experimental import pallas as pl
from jax.experimental.pallas import tpu as pltpu
from jax.sharding import Mesh
from jax.sharding import PartitionSpec as P

EPSILON = 1e-05
FSDP = ("y", "zl", "x")
TP = ("zh", "c")
ALL = (*FSDP, *TP)
CHIPS = ALL[:-1]
WIDE = 4096
HALF = 512
BLOCK = 1024
MIB = 1 << 20
NEAR, BACK = (1, -1), (-1, 1)


def flat(x, y, z, core):
    return (((y % 4) * 2 + (z % 4) % 2) * 4 + (x % 4)) * 4 + ((z % 4) // 2) * 2 + core


def place(index):
    x = (index // 4) % 4
    y = index // 32
    z = ((index // 2) % 2) * 2 + (index // 16) % 2
    return x, y, z, index % 2


def send(values, axis, steps):
    pairs = []
    for index in range(128):
        x, y, z, core = place(index)
        at = {"x": x, "y": y, "z": z}
        at[axis] += steps[core]
        pairs.append((index, flat(at["x"], at["y"], at["z"], core)))
    return lax.ppermute(values, ALL, pairs)


def swap(values):
    return lax.ppermute(values, ALL, [(index, index ^ 1) for index in range(128)])


def ring(rows, axis):
    return jnp.concatenate(
        [rows, *(send(rows, axis, steps) for steps in (NEAR, BACK, (2, 2)))], axis=0
    )


def fence(*values):
    return lax.optimization_barrier(values)


def normalize(values, gain):
    widened = values.astype(jnp.float32)
    factor = lax.rsqrt(jnp.mean(widened * widened, axis=1, keepdims=True) + EPSILON)
    return (widened * factor * gain).astype(jnp.bfloat16)


def row_table(me):
    x, y, z, mine = place(me)
    t = jnp.arange(3 * 8 * 16, dtype=jnp.int32)
    part, slot, group = t // 128, (t // 16) % 8, t % 16
    core = jnp.where(slot >= 4, 1 - mine, mine)

    def offset(j):
        return jnp.where(j == 0, 0, jnp.where(j == 3, 2, (2 * j - 3) * (1 - 2 * core))) + 4

    last, outer, inner = offset(slot % 4), offset(group // 4), offset(group % 4)
    at_x = (x + jnp.where(part == 0, last, outer)) % 4
    at_y = (y + jnp.where(part == 0, outer, jnp.where(part == 1, last, inner))) % 4
    at_z = (z + last) % 4
    low = jnp.where(part == 2, at_z % 2, group // 2 % 2)
    high = jnp.where(part == 2, at_z // 2, group % 2)
    return 8 * (((at_y * 2 + low) * 4 + at_x) * 2 + high)


def start_copies(sources, targets, sems):
    copies = [
        pltpu.make_async_copy(source, target, sems.at[number])
        for number, (source, target) in enumerate(zip(sources, targets))
    ]
    for copy in copies:
        copy.start()
    return copies


def put_rows(table, first, tmp, rows, total, lanes, add):
    for group in range(rows // 8):
        target = pl.ds(pl.multiple_of(table[first + group], 8), 8)
        values = tmp[8 * group : 8 * group + 8, :]
        if add:
            total[target, lanes] += values
        else:
            total[target, lanes] = values


def stats_of(total, info):
    def chunk(step):
        rows = pl.ds(pl.multiple_of(step * 128, 128), 128)
        told = jnp.transpose(info[:, rows])
        column = lax.broadcasted_iota(jnp.int32, (128, HALF), 1).astype(jnp.float32)
        sides = [total[rows, pl.ds(HALF * side, HALF)] for side in (0, 1)]
        peaks = [jnp.max(side, axis=1, keepdims=True) for side in sides]
        peak = jnp.maximum(*peaks)
        summed = sum(jnp.sum(jnp.exp(side - peak), axis=1, keepdims=True) for side in sides)
        hit = sum(
            jnp.sum(
                jnp.where(column == told[:, number : number + 1], side, 0.0), axis=1, keepdims=True
            )
            for number, side in enumerate(sides)
        )
        lane = lax.broadcasted_iota(jnp.int32, (128, 128), 1)
        block = jnp.where(lane == 0, peak + jnp.log(summed), jnp.where(lane == 1, hit, 0.0))
        return rows, jnp.transpose(block)[0:8, :]

    return chunk


def ref_kernel(table, *refs):
    pieces, (head, head_2, info, stats, xbuf, hbuf, tmp, total, sems) = refs[:4], refs[4:]
    copies = start_copies(
        [*pieces, head, head_2],
        [*(xbuf.at[pl.ds(128 * k, 128), :] for k in range(4)), hbuf.at[0], hbuf.at[1]],
        sems,
    )
    for copy in copies[:5]:
        copy.wait()
    for side in (0, 1):
        if side:
            copies[5].wait()
        for pair in (0, 1):
            tmp[...] = jnp.dot(
                xbuf[256 * pair : 256 * pair + 256, :],
                hbuf[side],
                preferred_element_type=jnp.float32,
            )
            lanes = pl.ds(HALF * side, HALF)
            put_rows(table, 256 + 32 * pair, tmp, 256, total, lanes, False)
    chunk = stats_of(total, info)

    def body(step, carry):
        rows, block = chunk(step)
        stats[:, rows] = block
        return carry

    lax.fori_loop(0, HALF // 128, body, 0)


def early_kernel(table, *refs):
    pieces, (head, head_2, total, xbuf, hbuf, tmp, sems) = refs[:6], refs[6:]
    copies = []
    for part in (0, 1):
        cut = pl.ds(WIDE * part, WIDE)
        sources = [*pieces[3 * part : 3 * part + 3], head.at[cut, :], head_2.at[cut, :]]
        targets = [xbuf.at[part, pl.ds(128 * k, 128), :] for k in range(3)]
        targets += [hbuf.at[part, 0], hbuf.at[part, 1]]
        copies.append(start_copies(sources, targets, sems.at[part]))
    total[...] = jnp.zeros_like(total)
    for part in (0, 1):
        for copy in copies[part][:4]:
            copy.wait()
        for side in (0, 1):
            if side:
                copies[part][4].wait()
            tmp[...] = jnp.dot(
                xbuf[part], hbuf[part, side], preferred_element_type=jnp.float32
            )
            put_rows(table, 128 * part, tmp, 384, total, pl.ds(HALF * side, HALF), True)


def late_kernel(table, *refs):
    pieces = refs[:2]
    head, head_2, before, info, mine, other, stats, xbuf, hbuf, tmp, total, sems = refs[2:]
    copies = []
    for part in (0, 1):
        cut = pl.ds(WIDE * part, WIDE)
        sources = [pieces[part], head.at[cut, :], head_2.at[cut, :]]
        targets = [xbuf.at[part], hbuf.at[part, 0], hbuf.at[part, 1]]
        copies.append(start_copies(sources, targets, sems.at[part]))
    copy = pltpu.make_async_copy(before, total, sems.at[2, 0])
    copy.start()
    for part in (0, 1):
        for number in (0, 1):
            copies[part][number].wait()
        for side in (0, 1):
            if side:
                copies[part][2].wait()
            tmp[...] = jnp.dot(
                xbuf[part], hbuf[part, side], preferred_element_type=jnp.float32
            )
            if part == 0 and side == 0:
                copy.wait()
            put_rows(table, 128 * part + 48, tmp, 128, total, pl.ds(HALF * side, HALF), True)
    chunk = stats_of(total, info)

    def body(step, carry):
        rows, block = chunk(step)
        stats[:, rows] = block
        mine[rows, :] = total[rows, pl.ds(0, HALF)]
        other[rows, :] = total[rows, pl.ds(HALF, HALF)]
        return carry

    lax.fori_loop(0, HALF // 128, body, 0)


def grad_kernel(table, *refs):
    pieces = refs[:16]
    mine, other, info, lses, out, xbuf, obuf, plain, ordered, scaled, sems, out_sems = refs[16:]
    copies = [
        start_copies(
            pieces[8 * part : 8 * part + 8],
            [xbuf.at[part, pl.ds(128 * k, 128), :] for k in range(8)],
            sems.at[part],
        )
        for part in (0, 1)
    ]

    for core, logits in enumerate((mine, other)):

        def chunk(number, carry):
            source = pl.ds(pl.multiple_of(number * 128, 128), 128)
            rows = pl.ds(pl.multiple_of(number * 128 + HALF * core, 128), 128)
            told = jnp.transpose(info[:, rows])
            lse = lses[pl.ds(number + 4 * core, 1), :]
            lse = jnp.transpose(jnp.broadcast_to(lse, (8, 128)))[:, 0:1]
            column = lax.broadcasted_iota(jnp.int32, (128, HALF), 1).astype(jnp.float32)
            hit = (column == told[:, 0:1]).astype(jnp.float32)
            plain[rows, :] = told[:, 2:3] * (jnp.exp(logits[source, :] - lse) - hit)
            return carry

        lax.fori_loop(0, HALF // 128, chunk, 0)
    for part in (0, 1):
        for core in (0, 1):

            def place_rows(group, carry):
                source = table[part * 128 + core * 64 + group] + HALF * core
                target = pl.multiple_of(HALF * core + 8 * group, 8)
                ordered[pl.ds(target, 8), :] = plain[pl.ds(pl.multiple_of(source, 8), 8), :]
                return carry

            lax.fori_loop(0, 64, place_rows, 0, unroll=16)
        scaled[part] = ordered[...].astype(jnp.bfloat16)
    steps = WIDE // BLOCK
    sent = []
    for part in (0, 1):
        for copy in copies[part]:
            copy.wait()
        for step in range(steps):
            number = part * steps + step
            if number >= 2:
                sent[number - 2].wait()
            obuf[number % 2] = lax.dot_general(
                xbuf[part, :, BLOCK * step : BLOCK * step + BLOCK],
                scaled[part],
                (((0,), (0,)), ((), ())),
                preferred_element_type=jnp.float32,
            ).astype(jnp.bfloat16)
            sent.append(
                pltpu.make_async_copy(
                    obuf.at[number % 2],
                    out.at[pl.ds(BLOCK * number, BLOCK), :],
                    out_sems.at[number % 2],
                )
            )
            sent[number].start()
    for copy in sent[-2:]:
        copy.wait()


ANY = pl.BlockSpec(memory_space=pl.ANY)
INSIDE = pl.BlockSpec(memory_space=pltpu.VMEM)
TABLE = pl.BlockSpec(memory_space=pltpu.SMEM)
DMA = pltpu.SemaphoreType.DMA


def floats(*shape):
    return jax.ShapeDtypeStruct(shape, jnp.float32)


def call(kernel, operands, specs, out_shape, out_specs, scratch, limit, flops, moved):
    return pl.pallas_call(
        kernel,
        out_shape=out_shape,
        in_specs=[TABLE, *specs],
        out_specs=out_specs,
        scratch_shapes=scratch,
        compiler_params=pltpu.CompilerParams(vmem_limit_bytes=limit * MIB),
        cost_estimate=pl.CostEstimate(
            flops=flops, bytes_accessed=moved * MIB, transcendentals=0
        ),
    )(*operands)


def ref_call(table, pieces, heads, info):
    scratch = [
        pltpu.VMEM((HALF, WIDE), jnp.bfloat16),
        pltpu.VMEM((2, WIDE, HALF), jnp.bfloat16),
        pltpu.VMEM((256, HALF), jnp.float32),
        pltpu.VMEM((HALF, 2 * HALF), jnp.float32),
        DMA((6,)),
    ]
    flops = 4 * HALF * HALF * WIDE
    specs = [ANY] * 6 + [INSIDE]
    operands = (table, *pieces, *heads, info)
    return call(ref_kernel, operands, specs, floats(8, HALF), INSIDE, scratch, 20, flops, 12)


def early_call(table, pieces, heads):
    scratch = [
        pltpu.VMEM((2, 384, WIDE), jnp.bfloat16),
        pltpu.VMEM((2, 2, WIDE, HALF), jnp.bfloat16),
        pltpu.VMEM((384, HALF), jnp.float32),
        DMA((2, 5)),
    ]
    flops = 8 * 384 * HALF * WIDE
    specs = [ANY] * 8
    operands = (table, *pieces, *heads)
    shape = floats(HALF, 2 * HALF)
    return call(early_kernel, operands, specs, shape, INSIDE, scratch, 28, flops, 24)


def late_call(table, pieces, heads, before, info):
    scratch = [
        pltpu.VMEM((2, 128, WIDE), jnp.bfloat16),
        pltpu.VMEM((2, 2, WIDE, HALF), jnp.bfloat16),
        pltpu.VMEM((128, HALF), jnp.float32),
        pltpu.VMEM((HALF, 2 * HALF), jnp.float32),
        DMA((3, 3)),
    ]
    flops = 8 * 128 * HALF * WIDE
    specs = [ANY] * 5 + [INSIDE]
    operands = (table, *pieces, *heads, before, info)
    shapes = (floats(HALF, HALF), floats(HALF, HALF), floats(8, HALF))
    return call(late_kernel, operands, specs, shapes, (INSIDE,) * 3, scratch, 26, flops, 20)


def grad_call(table, pieces, logits, info, lses):
    scratch = [
        pltpu.VMEM((2, 2 * HALF, WIDE), jnp.bfloat16),
        pltpu.VMEM((2, BLOCK, HALF), jnp.bfloat16),
        pltpu.VMEM((2 * HALF, HALF), jnp.float32),
        pltpu.VMEM((2 * HALF, HALF), jnp.float32),
        pltpu.VMEM((2, 2 * HALF, HALF), jnp.bfloat16),
        DMA((2, 8)),
        DMA((2,)),
    ]
    flops = 2 * 2 * HALF * 2 * WIDE * HALF
    specs = [ANY] * 16 + [INSIDE] * 4
    operands = (table, *pieces, *logits, info, lses)
    shape = jax.ShapeDtypeStruct((2 * WIDE, HALF), jnp.bfloat16)
    return call(grad_kernel, operands, specs, shape, ANY, scratch, 32, flops, 26)


def log_sum(terms, axis):
    peak = jnp.max(terms, axis=axis)
    return peak + jnp.log(jnp.sum(jnp.exp(terms - jnp.expand_dims(peak, axis)), axis=axis))


def core_tokens(values, core):
    values = values.reshape(64, 2, 8)
    return jnp.where(core == 0, values[:, 0], values[:, 1]).reshape(HALF)


def shards(
    ref_rows, ref_gain, trainee_rows, trainee_gain, ref_head, trainee_head, targets, selected
):
    me = lax.axis_index(ALL)
    core = lax.axis_index("c")
    chip = me // 2

    raw = trainee_rows.reshape(2, 2, 8, 2048).transpose(1, 0, 2, 3).reshape(1, 1, 2, 16, 2048)
    raw = jnp.broadcast_to(raw, (2, 2, 2, 16, 2048)).reshape(8, 16, 2048)
    raw = lax.all_to_all(raw, ("zl", "zh", "c"), 0, 0, tiled=True).reshape(2, 4, 16, 2048)
    own = normalize(raw.transpose(0, 2, 1, 3).reshape(32, 2 * WIDE), trainee_gain)
    ref = ring(ring(normalize(ref_rows, ref_gain), "y"), "x")
    ref_near, ref_back = send(ref, "z", NEAR), send(ref, "z", BACK)
    head_2, ref_head_2 = swap(trainee_head), swap(ref_head)
    own, head_2, ref_head_2 = fence(own, head_2, ref_head_2)

    low, top = ring(own[:, :WIDE], "y"), ring(own[:, WIDE:], "x")
    low, top = fence(low, top)

    low_near, top_near = send(low, "x", NEAR), send(top, "y", NEAR)
    low_back = send(low, "x", BACK)
    top, ref_near, ref_back = fence(top, ref_near, ref_back)
    top_back = send(top, "y", BACK)
    ref_far = send(ref_near, "z", NEAR)

    table = row_table(me)
    weight = selected.astype(jnp.float32)

    def info_of(which):
        wanted = core_tokens(targets, which)
        row = lax.broadcasted_iota(jnp.int32, (8, HALF), 0)
        beside = (wanted - HALF * (me ^ 1)).astype(jnp.float32)
        here = (wanted - HALF * me).astype(jnp.float32)
        rest = jnp.where(row == 1, beside[None], core_tokens(weight, which)[None])
        return jnp.where(row == 0, here[None], rest)

    info, info_2 = info_of(core), info_of(1 - core)
    ref_pieces = (ref, ref_near, ref_back, ref_far)
    ref_stats = ref_call(table, ref_pieces, (ref_head, ref_head_2), info)

    low, low_near, low_back, top, top_near, top_back, ref_stats = fence(
        low, low_near, low_back, top, top_near, top_back, ref_stats
    )
    low_far, top_far = send(low_near, "x", NEAR), send(top_near, "y", NEAR)
    early = (low, low_near, low_back, top, top_near, top_back)
    before = early_call(table, early, (trainee_head, head_2))
    low_2, top_2, low_near_2 = swap(low), swap(top), swap(low_near)
    low_far, top_far, before, low_2, top_2, low_near_2 = fence(
        low_far, top_far, before, low_2, top_2, low_near_2
    )
    mine, other, stats = late_call(
        table, (low_far, top_far), (trainee_head, head_2), before, info
    )

    rest = jnp.concatenate(
        [ref_stats[0].reshape(64, 8), (stats[1] - ref_stats[1]).reshape(64, 8)], axis=1
    )
    rest = jnp.pad(rest, ((0, 0), (0, 112)))
    message = jnp.concatenate(
        [jnp.broadcast_to(stats[0].reshape(1, 4, 128), (64, 4, 128)), rest[:, None]], axis=1
    )
    message, other, top_near, low_back, top_back, low_far, top_far = fence(
        message, other, top_near, low_back, top_back, low_far, top_far
    )
    arrived = lax.all_to_all(message, CHIPS, 0, 0, tiled=True)
    other_2 = swap(other)
    top_near_2, low_back_2, top_back_2 = swap(top_near), swap(low_back), swap(top_back)
    low_far_2, top_far_2 = swap(low_far), swap(top_far)
    lse = log_sum(arrived[:, :4], 0)
    lse_2 = swap(lse)
    found = log_sum(arrived[:, 4, :8], 0)
    hits = jnp.sum(arrived[:, 4, 8:16], axis=0)
    excess = lax.dynamic_slice_in_dim(lse.reshape(HALF), 8 * chip, 8) - found - hits

    pieces = (low, low_near, low_back, low_far, low_2, low_near_2, low_back_2, low_far_2)
    pieces += (top, top_near, top_back, top_far, top_2, top_near_2, top_back_2, top_far_2)
    head_grad = grad_call(
        table,
        pieces,
        (mine, other_2),
        jnp.concatenate([info, info_2], axis=1),
        jnp.concatenate([lse, lse_2], axis=0),
    )
    return excess, head_grad


def solution(mesh):
    grid = Mesh(mesh.devices.reshape(4, 2, 4, 2, 2), ALL)
    in_specs = (P(ALL, None), P(), P(FSDP, TP), P(), P(None, ALL), P(None, ALL), P(), P())
    out_specs = (P(ALL), P(None, ALL))
    return jax.shard_map(shards, mesh=grid, in_specs=in_specs, out_specs=out_specs, check_vma=False)
```

time: 583 us -> 181 us (0.31)
  waiting for transfers between devices: 371 us -> 44.3 us
  blocking collectives: 144 us -> 17.1 us
  matrix products: 45.7 us -> 0 us
  Pallas kernels: 0 us -> 42 us
  starting transfers between devices: 0.08 us -> 40.8 us
  local copies, waits for them, and re-layouts: 0.6 us -> 29.7 us
  between operations: 14.1 us -> 1.32 us
    all_gather x2 -> x0, waiting for transfers between devices: 371 us -> none  [the longest x1 193 us: shards(): lax.all_gather(ref_normed, ('fsdp', 'tp'), axis=0, tiled=True)]
    pmax x1 -> x0, blocking collectives: 68.4 us -> none  [shards(): ref_peak, own_peak = lax.pmax((ref_parts[0], own_high), ('fsdp', 'tp'))]
    psum x1 -> x0, blocking collectives: 64.7 us -> none  [shards(): lax.psum((ref_parts[1] * jnp.exp(ref_parts[0] - ref_peak), ref_parts[2],...]
    dot_general x3 -> x0, matrix products: 45.7 us -> none  [the longest x2 27.8 us: head_stats(): logits = jnp.dot(normed, head, preferred_element_type=jnp.float32)]
    ppermute x0 -> x33, waiting for transfers between devices: none -> 44.3 us  [the longest x21 38.4 us: send(): return lax.ppermute(values, ALL, pairs)]
    pallas_call x0 -> x4, Pallas kernels: none -> 42 us  [call(): pl.pallas_call(kernel, out_shape=out_shape, in_specs=[TABLE, *specs], out...]
    ppermute x0 -> x33, starting transfers between devices: none -> 35.4 us  [the longest x21 29.2 us: send(): return lax.ppermute(values, ALL, pairs)]
    unnamed x4 -> x57, local copies, waits for them, and re-layouts: 0.01 us -> 26.1 us
  transfers between devices with their start and end apart: 2 -> 34, of which waited for: 2 -> 14; matrix products, arithmetic and copies ran while one was open for 2% -> 5% of each run, Pallas kernels for 0% -> 10%
where the time goes in v2:
time: 181 us; the launch traced here: 180 us
  waiting for transfers between devices  44.3 us (24%)
  Pallas kernels  42 us (23%)
  starting transfers between devices  40.8 us (23%)
  local copies, waits for them, and re-layouts  29.7 us (16%)
  blocking collectives  17.1 us (9%)
  other arithmetic  4.64 us (3%)
    pallas_call x4, Pallas kernels, call(): pl.pallas_call(kernel, out_shape=out_shape, in_specs=[TABLE, *specs], out...  42 us
    ppermute x21, waiting for transfers between devices, send(): return lax.ppermute(values, ALL, pairs)  38.4 us
    ppermute x21, starting transfers between devices, send(): return lax.ppermute(values, ALL, pairs)  29.2 us
    unnamed x57, local copies, waits for them, and re-layouts  26.1 us
    all_to_all x1, blocking collectives, shards(): arrived = lax.all_to_all(message, CHIPS, 0, 0, tiled=True)  17.1 us
    ppermute x12, starting transfers between devices, swap(): lax.ppermute(values, ALL, [(index, index ^ 1) for index in range(128)])  6.22 us
    ppermute x12, waiting for transfers between devices, swap(): lax.ppermute(values, ALL, [(index, index ^ 1) for index in range(128)])  5.89 us
    all_to_all x1, starting transfers between devices, shards(): lax.all_to_all(raw, ('zl', 'zh', 'c'), 0, 0, tiled=True)  5.42 us
  transfers between devices with their start and end apart: 34, of which 14 were waited for; matrix products, arithmetic and copies ran while one was open for 5% of the time, Pallas kernels for 10%

profile of v2, /device:TPU:1, one launch (start us, length us, event | category | flops | bytes accessed | tf_op | source)
XLA Modules:
  0.0 179.8 jit_solution(3698107754713581107)
XLA Ops:
  0.6 1.5 collective-permute-start
  2.1 1.0 fusion
  3.1 0.9 constant_dynamic-update-slice_fusion.6
  4.1 3.1 %collective-permute-start.12 = (bf16[8,4096]{1,0:T(8,128)(2,1)S(1)}, bf16[8,4096]{1,0:T(8,128)(2,1)S(1)}, u32[]{:S(2)}, u32[]{:S(2)}) collective-permute-start(bf16[8,4096]{1,0:T(8,128)(2,1)S(1)} %get-tuple-element.75), channel_id=1, source_target_pairs={{0,64},{1,65},{2,66},{3,67},{4,68},{5,69},{6,70},{7,71},{8,72},{9,... | collective-permute-start | bytes 196616 | tf_op jit(solution)/shard_map/ppermute | solution.py:39
  7.2 0.4 collective-permute-start.11
  7.5 2.3 %collective-permute-start.10 = (bf16[8,4096]{1,0:T(8,128)(2,1)S(1)}, bf16[8,4096]{1,0:T(8,128)(2,1)S(1)}, u32[]{:S(2)}, u32[]{:S(2)}) collective-permute-start(bf16[8,4096]{1,0:T(8,128)(2,1)S(1)} %get-tuple-element.75), channel_id=1, source_target_pairs={{0,32},{1,97},{2,34},{3,99},{4,36},{5,101},{6,38},{7,103},{8,40},{... | collective-permute-start | bytes 196616 | tf_op jit(solution)/shard_map/ppermute | solution.py:39
  9.8 0.9 copy.59
  10.7 0.8 broadcast_in_dim.84
  11.6 5.4 %all-to-all-start = ((bf16[8,16,2048]{2,1,0:T(8,128)(2,1)}), bf16[8,16,2048]{2,1,0:T(8,128)(2,1)S(1)}, u32[]{:S(2)}, u32[]{:S(2)}) async-start(bf16[8,16,2048]{2,1,0:T(8,128)(2,1)} %bitcast.3), calls=%async_computation | async-start | bytes 1048576 | tf_op jit(solution)/shard_map/all_to_all | solution.py:376
  17.1 2.8 %collective-permute-start.15 = (bf16[32,4096]{1,0:T(8,128)(2,1)S(1)}, bf16[32,4096]{1,0:T(8,128)(2,1)S(1)}, u32[]{:S(2)}, u32[]{:S(2)}) collective-permute-start(bf16[32,4096]{1,0:T(8,128)(2,1)S(1)} %pad_maximum_fusion.2), channel_id=1, source_target_pairs={{0,8},{1,9},{2,10},{3,11},{4,12},{5,13},{6,14},{7,15},{8,0},{9,1},... | collective-permute-start | bytes 786440 | tf_op jit(solution)/shard_map/ppermute | solution.py:39
  20.2 2.4 %collective-permute-start.13 = (bf16[32,4096]{1,0:T(8,128)(2,1)S(1)}, bf16[32,4096]{1,0:T(8,128)(2,1)S(1)}, u32[]{:S(2)}, u32[]{:S(2)}) collective-permute-start(bf16[32,4096]{1,0:T(8,128)(2,1)S(1)} %pad_maximum_fusion.2), channel_id=1, source_target_pairs={{0,4},{1,13},{2,6},{3,15},{4,8},{5,1},{6,10},{7,3},{8,12},{9,5},{1... | collective-permute-start | bytes 786440 | tf_op jit(solution)/shard_map/ppermute | solution.py:39
  22.6 9.2 %collective-permute-done.13 = bf16[32,4096]{1,0:T(8,128)(2,1)S(1)} collective-permute-done((bf16[32,4096]{1,0:T(8,128)(2,1)S(1)}, bf16[32,4096]{1,0:T(8,128)(2,1)S(1)}, u32[]{:S(2)}, u32[]{:S(2)}) %collective-permute-start.13) | collective-permute-done | bytes 262176 | tf_op jit(solution)/shard_map/ppermute | solution.py:39
  31.8 0.7 collective-permute-done.14
  33.0 0.7 copy.46
  33.6 0.6 copy.57
  34.5 1.1 collective-permute-start.7
  35.6 2.1 %collective-permute-start.6 = (bf16[32,4096]{1,0:T(8,128)(2,1)S(1)}, bf16[32,4096]{1,0:T(8,128)(2,1)S(1)}, u32[]{:S(2)}, u32[]{:S(2)}) collective-permute-start(bf16[32,4096]{1,0:T(8,128)(2,1)S(1)} %get-tuple-element.76), channel_id=1, source_target_pairs={{0,12},{1,5},{2,14},{3,7},{4,0},{5,9},{6,2},{7,11},{8,4},{9,13},{1... | collective-permute-start | bytes 786440 | tf_op jit(solution)/shard_map/ppermute | solution.py:39
  37.7 0.6 collective-permute-start.5
  38.4 2.2 %collective-permute-start.17 = (bf16[128,4096]{1,0:T(8,128)(2,1)S(1)}, bf16[128,4096]{1,0:T(8,128)(2,1)S(1)}, u32[]{:S(2)}, u32[]{:S(2)}) collective-permute-start(bf16[128,4096]{1,0:T(8,128)(2,1)S(1)} %constant_dynamic-update-slice_fusion.refs_0_), channel_id=1, source_target_pairs={{0,18},{1,17},{2,16},{3,19},{4,22},{5,21},{6,20},{7,23},{8,26},{9,... | collective-permute-start | bytes 3145736 | tf_op jit(solution)/shard_map/ppermute | solution.py:39
  40.5 1.3 collective-permute-start.16
  41.8 1.5 collective-permute-done.7
  43.4 6.5 %collective-permute-done.6 = bf16[32,4096]{1,0:T(8,128)(2,1)S(1)} collective-permute-done((bf16[32,4096]{1,0:T(8,128)(2,1)S(1)}, bf16[32,4096]{1,0:T(8,128)(2,1)S(1)}, u32[]{:S(2)}, u32[]{:S(2)}) %collective-permute-start.6) | collective-permute-done | bytes 262176 | tf_op jit(solution)/shard_map/ppermute | solution.py:39
  49.9 2.7 %collective-permute-start.2 = (bf16[32,4096]{1,0:T(8,128)(2,1)S(1)}, bf16[32,4096]{1,0:T(8,128)(2,1)S(1)}, u32[]{:S(2)}, u32[]{:S(2)}) collective-permute-start(bf16[32,4096]{1,0:T(8,128)(2,1)S(1)} %get-tuple-element.77), channel_id=1, source_target_pairs={{0,32},{1,97},{2,34},{3,99},{4,36},{5,101},{6,38},{7,103},{8,40},{... | collective-permute-start | bytes 786440 | tf_op jit(solution)/shard_map/ppermute | solution.py:39
  52.7 4.0 %collective-permute-done.3 = bf16[32,4096]{1,0:T(8,128)(2,1)S(1)} collective-permute-done((bf16[32,4096]{1,0:T(8,128)(2,1)S(1)}, bf16[32,4096]{1,0:T(8,128)(2,1)S(1)}, u32[]{:S(2)}, u32[]{:S(2)}) %collective-permute-start.3) | collective-permute-done | bytes 262176 | tf_op jit(solution)/shard_map/ppermute | solution.py:39
  56.7 1.9 %collective-permute-done.2 = bf16[32,4096]{1,0:T(8,128)(2,1)S(1)} collective-permute-done((bf16[32,4096]{1,0:T(8,128)(2,1)S(1)}, bf16[32,4096]{1,0:T(8,128)(2,1)S(1)}, u32[]{:S(2)}, u32[]{:S(2)}) %collective-permute-start.2) | collective-permute-done | bytes 262176 | tf_op jit(solution)/shard_map/ppermute | solution.py:39
  58.7 2.7 %collective-permute-done.17.refs_2_ = bf16[128,4096]{1,0:T(8,128)(2,1)S(1)} collective-permute-done((bf16[128,4096]{1,0:T(8,128)(2,1)S(1)}, bf16[128,4096]{1,0:T(8,128)(2,1)S(1)}, u32[]{:S(2)}, u32[]{:S(2)}) %collective-permute-start.17) | collective-permute-done | bytes 1048608 | tf_op jit(solution)/shard_map/ppermute | solution.py:39
  61.4 1.0 copy-done.9
  62.4 2.8 %collective-permute-done.16.refs_1_ = bf16[128,4096]{1,0:T(8,128)(2,1)} collective-permute-done((bf16[128,4096]{1,0:T(8,128)(2,1)S(1)}, bf16[128,4096]{1,0:T(8,128)(2,1)}, u32[]{:S(2)}, u32[]{:S(2)}) %collective-permute-start.16) | collective-permute-done | bytes 1048608 | tf_op jit(solution)/shard_map/ppermute | solution.py:39
  65.2 1.9 %collective-permute-start.20 = (bf16[128,4096]{1,0:T(8,128)(2,1)}, bf16[128,4096]{1,0:T(8,128)(2,1)}, u32[]{:S(2)}, u32[]{:S(2)}) collective-permute-start(bf16[128,4096]{1,0:T(8,128)(2,1)} %collective-permute-done.16.refs_1_), channel_id=1, source_target_pairs={{0,16},{1,19},{2,18},{3,17},{4,20},{5,23},{6,22},{7,21},{8,24},{9,... | collective-permute-start | bytes 3145736 | tf_op jit(solution)/shard_map/ppermute | solution.py:39
  67.5 1.6 collective-permute-start.18
  69.1 2.7 %collective-permute-start.8 = (bf16[128,4096]{1,0:T(8,128)(2,1)S(1)}, bf16[128,4096]{1,0:T(8,128)(2,1)}, u32[]{:S(2)}, u32[]{:S(2)}) collective-permute-start(bf16[128,4096]{1,0:T(8,128)(2,1)S(1)} %pad_maximum_fusion.refs_0_), channel_id=1, source_target_pairs={{0,4},{1,13},{2,6},{3,15},{4,8},{5,1},{6,10},{7,3},{8,12},{9,5},{1... | collective-permute-start | bytes 3145736 | tf_op jit(solution)/shard_map/ppermute | solution.py:39
  71.8 0.4 fusion.4
  73.1 6.5 %collective-permute-done.20.refs_3_ = bf16[128,4096]{1,0:T(8,128)(2,1)} collective-permute-done((bf16[128,4096]{1,0:T(8,128)(2,1)}, bf16[128,4096]{1,0:T(8,128)(2,1)}, u32[]{:S(2)}, u32[]{:S(2)}) %collective-permute-start.20) | collective-permute-done | bytes 1048608 | tf_op jit(solution)/shard_map/ppermute | solution.py:39
  79.6 1.2 copy-done.7
  80.8 2.2 %copy-done.8 = bf16[4096,512]{1,0:T(8,128)(2,1)S(1)} copy-done((bf16[4096,512]{1,0:T(8,128)(2,1)S(1)}, bf16[4096,512]{1,0:T(8,128)(2,1)}, u32[]{:S(2)}) %copy-start.8) | copy-done | bytes 4194328
  83.0 1.2 copy-done.10
  84.2 9.0 %shard_map.95 = f32[8,512]{1,0:T(8,128)S(1)} custom-call(s32[384]{0:T(512)S(1)} %fusion.16.table, bf16[128,4096]{1,0:T(8,128)(2,1)S(1)} %copy-done.7, bf16[128,4096]{1,0:T(8,128)(2,1)} %collective-permute-done.16.refs_1_, bf16[128,4096]{1,0:T(8,128)(2,1)S(1)} %copy-done.10, bf16[128,4096]{1,0:T(8,128)(2,1)} %collective-permute-done.20.refs_3_, ...), custom_call_target="tpu_custom_call" | custom-call | flops 4294967296 | bytes 12582912 | tf_op jit(solution)/shard_map/pallas_call | solution.py:284
  93.2 2.4 %collective-permute-done.19.refs_5_.refs_10_ = bf16[128,4096]{1,0:T(8,128)(2,1)} collective-permute-done((bf16[128,4096]{1,0:T(8,128)(2,1)S(1)}, bf16[128,4096]{1,0:T(8,128)(2,1)}, u32[]{:S(2)}, u32[]{:S(2)}) %collective-permute-start.19) | collective-permute-done | bytes 1048608 | tf_op jit(solution)/shard_map/ppermute | solution.py:39
  95.9 0.9 collective-permute-start.23
  96.9 0.5 collective-permute-start.25
  97.4 1.5 collective-permute-start.21
  98.8 3.4 %copy-done = bf16[8192,512]{1,0:T(8,128)(2,1)S(1)} copy-done((bf16[8192,512]{1,0:T(8,128)(2,1)S(1)}, bf16[8192,512]{1,0:T(8,128)(2,1)}, u32[]{:S(2)}) %copy-start) | copy-done | bytes 8388632
  102.2 9.7 %shard_map.96.refs_4_ = f32[512,1024]{1,0:T(8,128)S(1)} custom-call(s32[384]{0:T(512)S(1)} %fusion.16.table, bf16[128,4096]{1,0:T(8,128)(2,1)S(1)} %pad_maximum_fusion.refs_0_, bf16[128,4096]{1,0:T(8,128)(2,1)} %collective-permute-done.8.refs_1_, bf16[128,4096]{1,0:T(8,128)(2,1)} %collective-permute-done.9.refs_2_, ...), custom_call_target="tpu_custom_call" | custom-call | flops 6442450944 | bytes 25165824 | tf_op jit(solution)/shard_map/pallas_call | solution.py:284
  112.1 4.8 %copy-done.1 = bf16[8192,512]{1,0:T(8,128)(2,1)S(1)} copy-done((bf16[8192,512]{1,0:T(8,128)(2,1)S(1)}, bf16[8192,512]{1,0:T(8,128)(2,1)}, u32[]{:S(2)}) %copy-start.1) | copy-done | bytes 8388632
  116.9 7.6 %shard_map.97 = (f32[512,512]{1,0:T(8,128)S(1)}, f32[512,512]{1,0:T(8,128)S(1)}, f32[8,512]{1,0:T(8,128)S(1)}) custom-call(s32[384]{0:T(512)S(1)} %fusion.16.table, bf16[128,4096]{1,0:T(8,128)(2,1)S(1)} %collective-permute-done.21.refs_0_.refs_3_, bf16[128,4096]{1,0:T(8,128)(2,1)S(1)} %collective-permute-done.22.refs_1_.refs_11_, ...), custom_call_target="tpu_custom_call" | custom-call | flops 2147483648 | bytes 20971520 | tf_op jit(solution)/shard_map/pallas_call | solution.py:284
  124.5 1.0 copy-done.17
  125.5 1.0 copy-done.21
  126.9 0.7 collective-permute-start.31
  127.6 17.1 %all_to_all.10 = f32[64,5,128]{2,1,0:T(8,128)S(1)} all-to-all(f32[64,5,128]{2,1,0:T(8,128)S(1)} %pad_maximum_fusion.3), channel_id=1, replica_groups=mesh['y'=4,'zl'=2,'x'=4,'zh'=2,'c'=2] {'y','zl','x','zh'}, dimensions={0} | all-to-all | bytes 327680 | tf_op jit(solution)/shard_map/all_to_all | solution.py:431
  144.8 1.5 collective-permute-start.32
  146.4 0.4 collective-permute-start.27
  147.4 1.0 copy-done.19
  149.0 0.6 subtract_subtract_fusion
  149.6 2.7 %collective-permute-done.27.refs_7_ = bf16[128,4096]{1,0:T(8,128)(2,1)} collective-permute-done((bf16[128,4096]{1,0:T(8,128)(2,1)}, bf16[128,4096]{1,0:T(8,128)(2,1)}, u32[]{:S(2)}, u32[]{:S(2)}) %collective-permute-start.27) | collective-permute-done | bytes 1048608 | tf_op jit(solution)/shard_map/ppermute | solution.py:43
  152.3 1.5 collective-permute-done.29.refs_14_
  153.8 1.5 collective-permute-done.30.refs_15_
  155.3 1.2 copy-done.3
  156.5 1.2 copy-done.5
  157.7 1.2 copy-done.12
  159.0 1.2 copy-done.14
  160.2 1.2 copy-done.16
  161.4 1.2 copy-done.18
  162.6 1.2 copy-done.20
  163.9 15.8 %shard_map.98 = bf16[8192,512]{1,0:T(8,128)(2,1)} custom-call(s32[384]{0:T(512)S(1)} %fusion.16.table, bf16[128,4096]{1,0:T(8,128)(2,1)S(1)} %pad_maximum_fusion.refs_0_, bf16[128,4096]{1,0:T(8,128)(2,1)} %collective-permute-done.8.refs_1_, bf16[128,4096]{1,0:T(8,128)(2,1)} %collective-permute-done.9.refs_2_, bf16[128,4096]{1,0:T(8,128)(2,1)S(1)} %copy-done.5, ...), custom_call_target="tpu_custom_call" | custom-call | flops 8589934592 | bytes 27262976 | tf_op jit(solution)/shard_map/pallas_call | solution.py:284
  (112 shorter events, 4.6 us)
Async XLA Ops:
  0.6 33.8 %collective-permute-start = (bf16[8192,512]{1,0:T(8,128)(2,1)}, bf16[8192,512]{1,0:T(8,128)(2,1)}, u32[]{:S(2)}, u32[]{:S(2)}) collective-permute-start(bf16[8192,512]{1,0:T(8,128)(2,1)} %refs_2_.1), channel_id=1, source_target_pairs={{0,1},{1,0},{2,3},{3,2},{4,5},{5,4},{6,7},{7,6},{8,9},{9,8},{10,11... | collective-permute-start | bytes 25165832 | tf_op jit(solution)/shard_map/ppermute | solution.py:43
  4.1 12.9 %collective-permute-start.12 = (bf16[8,4096]{1,0:T(8,128)(2,1)S(1)}, bf16[8,4096]{1,0:T(8,128)(2,1)S(1)}, u32[]{:S(2)}, u32[]{:S(2)}) collective-permute-start(bf16[8,4096]{1,0:T(8,128)(2,1)S(1)} %get-tuple-element.75), channel_id=1, source_target_pairs={{0,64},{1,65},{2,66},{3,67},{4,68},{5,69},{6,70},{7,71},{8,72},{9,... | collective-permute-start | bytes 196616 | tf_op jit(solution)/shard_map/ppermute | solution.py:39
  7.2 9.9 %collective-permute-start.11 = (bf16[8,4096]{1,0:T(8,128)(2,1)S(1)}, bf16[8,4096]{1,0:T(8,128)(2,1)S(1)}, u32[]{:S(2)}, u32[]{:S(2)}) collective-permute-start(bf16[8,4096]{1,0:T(8,128)(2,1)S(1)} %get-tuple-element.75), channel_id=1, source_target_pairs={{0,96},{1,33},{2,98},{3,35},{4,100},{5,37},{6,102},{7,39},{8,104},... | collective-permute-start | bytes 196616 | tf_op jit(solution)/shard_map/ppermute | solution.py:39
  7.5 9.5 %collective-permute-start.10 = (bf16[8,4096]{1,0:T(8,128)(2,1)S(1)}, bf16[8,4096]{1,0:T(8,128)(2,1)S(1)}, u32[]{:S(2)}, u32[]{:S(2)}) collective-permute-start(bf16[8,4096]{1,0:T(8,128)(2,1)S(1)} %get-tuple-element.75), channel_id=1, source_target_pairs={{0,32},{1,97},{2,34},{3,99},{4,36},{5,101},{6,38},{7,103},{8,40},{... | collective-permute-start | bytes 196616 | tf_op jit(solution)/shard_map/ppermute | solution.py:39
  11.6 20.9 %all-to-all-start = ((bf16[8,16,2048]{2,1,0:T(8,128)(2,1)}), bf16[8,16,2048]{2,1,0:T(8,128)(2,1)S(1)}, u32[]{:S(2)}, u32[]{:S(2)}) async-start(bf16[8,16,2048]{2,1,0:T(8,128)(2,1)} %bitcast.3), calls=%async_computation | async-start | bytes 1048576 | tf_op jit(solution)/shard_map/all_to_all | solution.py:376
  17.0 17.4 %collective-permute-start.1 = (bf16[4096,512]{1,0:T(8,128)(2,1)}, bf16[4096,512]{1,0:T(8,128)(2,1)}, u32[]{:S(2)}, u32[]{:S(2)}) collective-permute-start(bf16[4096,512]{1,0:T(8,128)(2,1)} %refs_4_.1), channel_id=1, source_target_pairs={{0,1},{1,0},{2,3},{3,2},{4,5},{5,4},{6,7},{7,6},{8,9},{9,8},{10,11... | collective-permute-start | bytes 12582920 | tf_op jit(solution)/shard_map/ppermute | solution.py:43
  17.1 21.2 %collective-permute-start.15 = (bf16[32,4096]{1,0:T(8,128)(2,1)S(1)}, bf16[32,4096]{1,0:T(8,128)(2,1)S(1)}, u32[]{:S(2)}, u32[]{:S(2)}) collective-permute-start(bf16[32,4096]{1,0:T(8,128)(2,1)S(1)} %pad_maximum_fusion.2), channel_id=1, source_target_pairs={{0,8},{1,9},{2,10},{3,11},{4,12},{5,13},{6,14},{7,15},{8,0},{9,1},... | collective-permute-start | bytes 786440 | tf_op jit(solution)/shard_map/ppermute | solution.py:39
  19.9 12.6 %collective-permute-start.14 = (bf16[32,4096]{1,0:T(8,128)(2,1)S(1)}, bf16[32,4096]{1,0:T(8,128)(2,1)S(1)}, u32[]{:S(2)}, u32[]{:S(2)}) collective-permute-start(bf16[32,4096]{1,0:T(8,128)(2,1)S(1)} %pad_maximum_fusion.2), channel_id=1, source_target_pairs={{0,12},{1,5},{2,14},{3,7},{4,0},{5,9},{6,2},{7,11},{8,4},{9,13},{1... | collective-permute-start | bytes 786440 | tf_op jit(solution)/shard_map/ppermute | solution.py:39
  20.2 11.6 %collective-permute-start.13 = (bf16[32,4096]{1,0:T(8,128)(2,1)S(1)}, bf16[32,4096]{1,0:T(8,128)(2,1)S(1)}, u32[]{:S(2)}, u32[]{:S(2)}) collective-permute-start(bf16[32,4096]{1,0:T(8,128)(2,1)S(1)} %pad_maximum_fusion.2), channel_id=1, source_target_pairs={{0,4},{1,13},{2,6},{3,15},{4,8},{5,1},{6,10},{7,3},{8,12},{9,5},{1... | collective-permute-start | bytes 786440 | tf_op jit(solution)/shard_map/ppermute | solution.py:39
  32.9 1.3 copy-start.22
  34.5 8.9 %collective-permute-start.7 = (bf16[32,4096]{1,0:T(8,128)(2,1)S(1)}, bf16[32,4096]{1,0:T(8,128)(2,1)S(1)}, u32[]{:S(2)}, u32[]{:S(2)}) collective-permute-start(bf16[32,4096]{1,0:T(8,128)(2,1)S(1)} %get-tuple-element.76), channel_id=1, source_target_pairs={{0,8},{1,9},{2,10},{3,11},{4,12},{5,13},{6,14},{7,15},{8,0},{9,1},... | collective-permute-start | bytes 786440 | tf_op jit(solution)/shard_map/ppermute | solution.py:39
  35.6 14.3 %collective-permute-start.6 = (bf16[32,4096]{1,0:T(8,128)(2,1)S(1)}, bf16[32,4096]{1,0:T(8,128)(2,1)S(1)}, u32[]{:S(2)}, u32[]{:S(2)}) collective-permute-start(bf16[32,4096]{1,0:T(8,128)(2,1)S(1)} %get-tuple-element.76), channel_id=1, source_target_pairs={{0,12},{1,5},{2,14},{3,7},{4,0},{5,9},{6,2},{7,11},{8,4},{9,13},{1... | collective-permute-start | bytes 786440 | tf_op jit(solution)/shard_map/ppermute | solution.py:39
  37.7 12.2 %collective-permute-start.5 = (bf16[32,4096]{1,0:T(8,128)(2,1)S(1)}, bf16[32,4096]{1,0:T(8,128)(2,1)S(1)}, u32[]{:S(2)}, u32[]{:S(2)}) collective-permute-start(bf16[32,4096]{1,0:T(8,128)(2,1)S(1)} %get-tuple-element.76), channel_id=1, source_target_pairs={{0,4},{1,13},{2,6},{3,15},{4,8},{5,1},{6,10},{7,3},{8,12},{9,5},{1... | collective-permute-start | bytes 786440 | tf_op jit(solution)/shard_map/ppermute | solution.py:39
  38.3 20.4 %copy-start.6 = (bf16[128,4096]{1,0:T(8,128)(2,1)}, bf16[128,4096]{1,0:T(8,128)(2,1)S(1)}, u32[]{:S(2)}) copy-start(bf16[128,4096]{1,0:T(8,128)(2,1)S(1)} %constant_dynamic-update-slice_fusion.refs_0_) | copy-start | bytes 3145732
  38.4 23.1 %collective-permute-start.17 = (bf16[128,4096]{1,0:T(8,128)(2,1)S(1)}, bf16[128,4096]{1,0:T(8,128)(2,1)S(1)}, u32[]{:S(2)}, u32[]{:S(2)}) collective-permute-start(bf16[128,4096]{1,0:T(8,128)(2,1)S(1)} %constant_dynamic-update-slice_fusion.refs_0_), channel_id=1, source_target_pairs={{0,18},{1,17},{2,16},{3,19},{4,22},{5,21},{6,20},{7,23},{8,26},{9,... | collective-permute-start | bytes 3145736 | tf_op jit(solution)/shard_map/ppermute | solution.py:39
  40.5 24.7 %collective-permute-start.16 = (bf16[128,4096]{1,0:T(8,128)(2,1)S(1)}, bf16[128,4096]{1,0:T(8,128)(2,1)}, u32[]{:S(2)}, u32[]{:S(2)}) collective-permute-start(bf16[128,4096]{1,0:T(8,128)(2,1)S(1)} %constant_dynamic-update-slice_fusion.refs_0_), channel_id=1, source_target_pairs={{0,16},{1,19},{2,18},{3,17},{4,20},{5,23},{6,22},{7,21},{8,24},{9,... | collective-permute-start | bytes 3145736 | tf_op jit(solution)/shard_map/ppermute | solution.py:39
  43.4 23.8 %copy-start.24 = (s32[1024]{0:T(1024)S(1)}, s32[1024]{0:T(1024)}, u32[]{:S(2)}) copy-start(s32[1024]{0:T(1024)} %param.15) | copy-start | bytes 12292
  43.4 24.0 %copy-start.23 = (s32[1024]{0:T(1024)S(1)}, s32[1024]{0:T(1024)}, u32[]{:S(2)}) copy-start(s32[1024]{0:T(1024)} %param.14) | copy-start | bytes 12292
  43.4 9.3 %collective-permute-start.4 = (bf16[32,4096]{1,0:T(8,128)(2,1)S(1)}, bf16[32,4096]{1,0:T(8,128)(2,1)S(1)}, u32[]{:S(2)}, u32[]{:S(2)}) collective-permute-start(bf16[32,4096]{1,0:T(8,128)(2,1)S(1)} %get-tuple-element.77), channel_id=1, source_target_pairs={{0,64},{1,65},{2,66},{3,67},{4,68},{5,69},{6,70},{7,71},{8,72},{9,... | collective-permute-start | bytes 786440 | tf_op jit(solution)/shard_map/ppermute | solution.py:39
  49.9 6.8 %collective-permute-start.3 = (bf16[32,4096]{1,0:T(8,128)(2,1)S(1)}, bf16[32,4096]{1,0:T(8,128)(2,1)S(1)}, u32[]{:S(2)}, u32[]{:S(2)}) collective-permute-start(bf16[32,4096]{1,0:T(8,128)(2,1)S(1)} %get-tuple-element.77), channel_id=1, source_target_pairs={{0,96},{1,33},{2,98},{3,35},{4,100},{5,37},{6,102},{7,39},{8,104},... | collective-permute-start | bytes 786440 | tf_op jit(solution)/shard_map/ppermute | solution.py:39
  49.9 8.8 %collective-permute-start.2 = (bf16[32,4096]{1,0:T(8,128)(2,1)S(1)}, bf16[32,4096]{1,0:T(8,128)(2,1)S(1)}, u32[]{:S(2)}, u32[]{:S(2)}) collective-permute-start(bf16[32,4096]{1,0:T(8,128)(2,1)S(1)} %get-tuple-element.77), channel_id=1, source_target_pairs={{0,32},{1,97},{2,34},{3,99},{4,36},{5,101},{6,38},{7,103},{8,40},{... | collective-permute-start | bytes 786440 | tf_op jit(solution)/shard_map/ppermute | solution.py:39
  61.4 1.0 copy-start.9
  65.2 14.4 %collective-permute-start.20 = (bf16[128,4096]{1,0:T(8,128)(2,1)}, bf16[128,4096]{1,0:T(8,128)(2,1)}, u32[]{:S(2)}, u32[]{:S(2)}) collective-permute-start(bf16[128,4096]{1,0:T(8,128)(2,1)} %collective-permute-done.16.refs_1_), channel_id=1, source_target_pairs={{0,16},{1,19},{2,18},{3,17},{4,20},{5,23},{6,22},{7,21},{8,24},{9,... | collective-permute-start | bytes 3145736 | tf_op jit(solution)/shard_map/ppermute | solution.py:39
  67.5 28.1 %collective-permute-start.18 = (bf16[128,4096]{1,0:T(8,128)(2,1)S(1)}, bf16[128,4096]{1,0:T(8,128)(2,1)S(1)}, u32[]{:S(2)}, u32[]{:S(2)}) collective-permute-start(bf16[128,4096]{1,0:T(8,128)(2,1)S(1)} %pad_maximum_fusion.1.refs_3_.refs_8_), channel_id=1, source_target_pairs={{0,32},{1,97},{2,34},{3,99},{4,36},{5,101},{6,38},{7,103},{8,40},{... | collective-permute-start | bytes 3145736 | tf_op jit(solution)/shard_map/ppermute | solution.py:39
  69.1 26.5 %collective-permute-start.9 = (bf16[128,4096]{1,0:T(8,128)(2,1)S(1)}, bf16[128,4096]{1,0:T(8,128)(2,1)}, u32[]{:S(2)}, u32[]{:S(2)}) collective-permute-start(bf16[128,4096]{1,0:T(8,128)(2,1)S(1)} %pad_maximum_fusion.refs_0_), channel_id=1, source_target_pairs={{0,12},{1,5},{2,14},{3,7},{4,0},{5,9},{6,2},{7,11},{8,4},{9,13},{1... | collective-permute-start | bytes 3145736 | tf_op jit(solution)/shard_map/ppermute | solution.py:39
  69.1 26.5 %collective-permute-start.8 = (bf16[128,4096]{1,0:T(8,128)(2,1)S(1)}, bf16[128,4096]{1,0:T(8,128)(2,1)}, u32[]{:S(2)}, u32[]{:S(2)}) collective-permute-start(bf16[128,4096]{1,0:T(8,128)(2,1)S(1)} %pad_maximum_fusion.refs_0_), channel_id=1, source_target_pairs={{0,4},{1,13},{2,6},{3,15},{4,8},{5,1},{6,10},{7,3},{8,12},{9,5},{1... | collective-permute-start | bytes 3145736 | tf_op jit(solution)/shard_map/ppermute | solution.py:39
  71.8 23.8 %collective-permute-start.19 = (bf16[128,4096]{1,0:T(8,128)(2,1)S(1)}, bf16[128,4096]{1,0:T(8,128)(2,1)}, u32[]{:S(2)}, u32[]{:S(2)}) collective-permute-start(bf16[128,4096]{1,0:T(8,128)(2,1)S(1)} %pad_maximum_fusion.1.refs_3_.refs_8_), channel_id=1, source_target_pairs={{0,96},{1,33},{2,98},{3,35},{4,100},{5,37},{6,102},{7,39},{8,104},... | collective-permute-start | bytes 3145736 | tf_op jit(solution)/shard_map/ppermute | solution.py:39
  79.6 1.2 copy-start.7
  80.8 2.2 %copy-start.8 = (bf16[4096,512]{1,0:T(8,128)(2,1)S(1)}, bf16[4096,512]{1,0:T(8,128)(2,1)}, u32[]{:S(2)}) copy-start(bf16[4096,512]{1,0:T(8,128)(2,1)} %refs_4_.1) | copy-start | bytes 12582916
  83.0 1.2 copy-start.10
  95.6 16.4 %collective-permute-start.22 = (bf16[128,4096]{1,0:T(8,128)(2,1)S(1)}, bf16[128,4096]{1,0:T(8,128)(2,1)S(1)}, u32[]{:S(2)}, u32[]{:S(2)}) collective-permute-start(bf16[128,4096]{1,0:T(8,128)(2,1)S(1)} %collective-permute-done.18.refs_4_.refs_9_), channel_id=1, source_target_pairs={{0,32},{1,97},{2,34},{3,99},{4,36},{5,101},{6,38},{7,103},{8,40},{... | collective-permute-start | bytes 3145736 | tf_op jit(solution)/shard_map/ppermute | solution.py:39
  95.9 16.1 %collective-permute-start.23 = (bf16[128,4096]{1,0:T(8,128)(2,1)S(1)}, bf16[128,4096]{1,0:T(8,128)(2,1)S(1)}, u32[]{:S(2)}, u32[]{:S(2)}) collective-permute-start(bf16[128,4096]{1,0:T(8,128)(2,1)S(1)} %pad_maximum_fusion.refs_0_), channel_id=1, source_target_pairs={{0,1},{1,0},{2,3},{3,2},{4,5},{5,4},{6,7},{7,6},{8,9},{9,8},{10,11... | collective-permute-start | bytes 3145736 | tf_op jit(solution)/shard_map/ppermute | solution.py:43
  96.9 15.2 %collective-permute-start.24 = (bf16[128,4096]{1,0:T(8,128)(2,1)S(1)}, bf16[128,4096]{1,0:T(8,128)(2,1)S(1)}, u32[]{:S(2)}, u32[]{:S(2)}) collective-permute-start(bf16[128,4096]{1,0:T(8,128)(2,1)S(1)} %pad_maximum_fusion.1.refs_3_.refs_8_), channel_id=1, source_target_pairs={{0,1},{1,0},{2,3},{3,2},{4,5},{5,4},{6,7},{7,6},{8,9},{9,8},{10,11... | collective-permute-start | bytes 3145736 | tf_op jit(solution)/shard_map/ppermute | solution.py:43
  96.9 15.2 %collective-permute-start.25 = (bf16[128,4096]{1,0:T(8,128)(2,1)}, bf16[128,4096]{1,0:T(8,128)(2,1)S(1)}, u32[]{:S(2)}, u32[]{:S(2)}) collective-permute-start(bf16[128,4096]{1,0:T(8,128)(2,1)} %collective-permute-done.8.refs_1_), channel_id=1, source_target_pairs={{0,1},{1,0},{2,3},{3,2},{4,5},{5,4},{6,7},{7,6},{8,9},{9,8},{10,11... | collective-permute-start | bytes 3145736 | tf_op jit(solution)/shard_map/ppermute | solution.py:43
  97.4 14.7 %collective-permute-start.21 = (bf16[128,4096]{1,0:T(8,128)(2,1)}, bf16[128,4096]{1,0:T(8,128)(2,1)S(1)}, u32[]{:S(2)}, u32[]{:S(2)}) collective-permute-start(bf16[128,4096]{1,0:T(8,128)(2,1)} %collective-permute-done.8.refs_1_), channel_id=1, source_target_pairs={{0,4},{1,13},{2,6},{3,15},{4,8},{5,1},{6,10},{7,3},{8,12},{9,5},{1... | collective-permute-start | bytes 3145736 | tf_op jit(solution)/shard_map/ppermute | solution.py:39
  98.8 3.4 %copy-start = (bf16[8192,512]{1,0:T(8,128)(2,1)S(1)}, bf16[8192,512]{1,0:T(8,128)(2,1)}, u32[]{:S(2)}) copy-start(bf16[8192,512]{1,0:T(8,128)(2,1)} %refs_2_.1) | copy-start | bytes 25165828
  112.0 12.5 %copy-start.2 = (bf16[128,4096]{1,0:T(8,128)(2,1)}, bf16[128,4096]{1,0:T(8,128)(2,1)S(1)}, u32[]{:S(2)}) copy-start(bf16[128,4096]{1,0:T(8,128)(2,1)S(1)} %collective-permute-done.22.refs_1_.refs_11_) | copy-start | bytes 3145732
  112.0 12.5 %copy-start.11 = (bf16[128,4096]{1,0:T(8,128)(2,1)}, bf16[128,4096]{1,0:T(8,128)(2,1)S(1)}, u32[]{:S(2)}) copy-start(bf16[128,4096]{1,0:T(8,128)(2,1)S(1)} %collective-permute-done.23.refs_4_) | copy-start | bytes 3145732
  112.0 12.5 %copy-start.13 = (bf16[128,4096]{1,0:T(8,128)(2,1)}, bf16[128,4096]{1,0:T(8,128)(2,1)S(1)}, u32[]{:S(2)}) copy-start(bf16[128,4096]{1,0:T(8,128)(2,1)S(1)} %collective-permute-done.24.refs_12_) | copy-start | bytes 3145732
  112.0 12.5 %copy-start.15 = (bf16[128,4096]{1,0:T(8,128)(2,1)}, bf16[128,4096]{1,0:T(8,128)(2,1)S(1)}, u32[]{:S(2)}) copy-start(bf16[128,4096]{1,0:T(8,128)(2,1)S(1)} %collective-permute-done.25.refs_5_) | copy-start | bytes 3145732
  112.1 4.8 %copy-start.1 = (bf16[8192,512]{1,0:T(8,128)(2,1)S(1)}, bf16[8192,512]{1,0:T(8,128)(2,1)}, u32[]{:S(2)}) copy-start(bf16[8192,512]{1,0:T(8,128)(2,1)} %refs_2_.1) | copy-start | bytes 25165828
  116.9 7.6 %copy-start.4 = (bf16[128,4096]{1,0:T(8,128)(2,1)}, bf16[128,4096]{1,0:T(8,128)(2,1)S(1)}, u32[]{:S(2)}) copy-start(bf16[128,4096]{1,0:T(8,128)(2,1)S(1)} %collective-permute-done.21.refs_0_.refs_3_) | copy-start | bytes 3145732
  124.5 1.0 copy-start.17
  125.5 1.0 copy-start.21
  126.9 20.6 %collective-permute-start.31 = (f32[512,512]{1,0:T(8,128)}, f32[512,512]{1,0:T(8,128)S(1)}, u32[]{:S(2)}, u32[]{:S(2)}) collective-permute-start(f32[512,512]{1,0:T(8,128)} %copy-done.21), channel_id=1, source_target_pairs={{0,1},{1,0},{2,3},{3,2},{4,5},{5,4},{6,7},{7,6},{8,9},{9,8},{10,11... | collective-permute-start | bytes 3145736 | tf_op jit(solution)/shard_map/ppermute | solution.py:43
  144.8 2.3 %collective-permute-start.32 = (f32[4,128]{1,0:T(4,128)S(1)}, f32[4,128]{1,0:T(4,128)S(1)}, u32[]{:S(2)}, u32[]{:S(2)}) collective-permute-start(f32[4,128]{1,0:T(4,128)S(1)} %log_add_fusion), channel_id=1, source_target_pairs={{0,1},{1,0},{2,3},{3,2},{4,5},{5,4},{6,7},{7,6},{8,9},{9,8},{10,11... | collective-permute-start | bytes 6152 | tf_op jit(solution)/shard_map/ppermute | solution.py:43
  146.3 3.3 %collective-permute-start.26 = (bf16[128,4096]{1,0:T(8,128)(2,1)}, bf16[128,4096]{1,0:T(8,128)(2,1)}, u32[]{:S(2)}, u32[]{:S(2)}) collective-permute-start(bf16[128,4096]{1,0:T(8,128)(2,1)} %collective-permute-done.9.refs_2_), channel_id=1, source_target_pairs={{0,1},{1,0},{2,3},{3,2},{4,5},{5,4},{6,7},{7,6},{8,9},{9,8},{10,11... | collective-permute-start | bytes 3145736 | tf_op jit(solution)/shard_map/ppermute | solution.py:43
  146.4 5.9 %collective-permute-start.27 = (bf16[128,4096]{1,0:T(8,128)(2,1)}, bf16[128,4096]{1,0:T(8,128)(2,1)}, u32[]{:S(2)}, u32[]{:S(2)}) collective-permute-start(bf16[128,4096]{1,0:T(8,128)(2,1)} %copy-done.4), channel_id=1, source_target_pairs={{0,1},{1,0},{2,3},{3,2},{4,5},{5,4},{6,7},{7,6},{8,9},{9,8},{10,11... | collective-permute-start | bytes 3145736 | tf_op jit(solution)/shard_map/ppermute | solution.py:43
  146.8 5.5 %collective-permute-start.28 = (bf16[128,4096]{1,0:T(8,128)(2,1)S(1)}, bf16[128,4096]{1,0:T(8,128)(2,1)}, u32[]{:S(2)}, u32[]{:S(2)}) collective-permute-start(bf16[128,4096]{1,0:T(8,128)(2,1)S(1)} %collective-permute-done.18.refs_4_.refs_9_), channel_id=1, source_target_pairs={{0,1},{1,0},{2,3},{3,2},{4,5},{5,4},{6,7},{7,6},{8,9},{9,8},{10,11... | collective-permute-start | bytes 3145736 | tf_op jit(solution)/shard_map/ppermute | solution.py:43
  147.1 6.7 %collective-permute-start.29 = (bf16[128,4096]{1,0:T(8,128)(2,1)}, bf16[128,4096]{1,0:T(8,128)(2,1)}, u32[]{:S(2)}, u32[]{:S(2)}) collective-permute-start(bf16[128,4096]{1,0:T(8,128)(2,1)} %collective-permute-done.19.refs_5_.refs_10_), channel_id=1, source_target_pairs={{0,1},{1,0},{2,3},{3,2},{4,5},{5,4},{6,7},{7,6},{8,9},{9,8},{10,11... | collective-permute-start | bytes 3145736 | tf_op jit(solution)/shard_map/ppermute | solution.py:43
  147.4 1.0 copy-start.19
  148.4 6.9 %collective-permute-start.30 = (bf16[128,4096]{1,0:T(8,128)(2,1)}, bf16[128,4096]{1,0:T(8,128)(2,1)}, u32[]{:S(2)}, u32[]{:S(2)}) collective-permute-start(bf16[128,4096]{1,0:T(8,128)(2,1)} %copy-done.2), channel_id=1, source_target_pairs={{0,1},{1,0},{2,3},{3,2},{4,5},{5,4},{6,7},{7,6},{8,9},{9,8},{10,11... | collective-permute-start | bytes 3145736 | tf_op jit(solution)/shard_map/ppermute | solution.py:43
  155.3 1.2 copy-start.3
  156.5 1.2 copy-start.5
  157.7 1.2 copy-start.12
  158.9 1.2 copy-start.14
  160.2 1.2 copy-start.16
  161.4 1.2 copy-start.18
  162.6 1.2 copy-start.20

commit v3 on v0

v3 whole, which is shorter than its diff:
```python
import jax
import jax.numpy as jnp
from jax import lax
from jax.experimental import pallas as pl
from jax.experimental.pallas import tpu as pltpu
from jax.sharding import Mesh
from jax.sharding import PartitionSpec as P

EPSILON = 1e-05
FSDP = ("y", "zl", "x")
TP = ("zh", "c")
ALL = (*FSDP, *TP)
CHIPS = ALL[:-1]
WIDE = 4096
HALF = 512
BLOCK = 1024
MIB = 1 << 20


def flat(x, y, z, core):
    return (((y % 4) * 2 + (z % 4) % 2) * 4 + (x % 4)) * 4 + ((z % 4) // 2) * 2 + core


def place(index):
    x = (index // 4) % 4
    y = index // 32
    z = ((index // 2) % 2) * 2 + (index // 16) % 2
    return x, y, z, index % 2


def send(values, axes, steps):
    pairs = []
    for index in range(128):
        x, y, z, core = place(index)
        at = {"x": x, "y": y, "z": z}
        at[axes[core]] += steps[core]
        pairs.append((index, flat(at["x"], at["y"], at["z"], core)))
    return lax.ppermute(values, ALL, pairs)


def swap(values):
    return lax.ppermute(values, ALL, [(index, index ^ 1) for index in range(128)])


def ring(rows, axes):
    return [rows, *(send(rows, axes, (steps, steps)) for steps in (1, -1, 2))]


def stack(pieces, cut=slice(None)):
    return jnp.concatenate([piece[:, cut] for piece in pieces], axis=0)


def fence(*values):
    return lax.optimization_barrier(values)


def normalize(values, gain):
    widened = values.astype(jnp.float32)
    factor = lax.rsqrt(jnp.mean(widened * widened, axis=1, keepdims=True) + EPSILON)
    return (widened * factor * gain).astype(jnp.bfloat16)


def row_table(me):
    x, y, z, mine = place(me)
    t = jnp.arange(2 * 8 * 16, dtype=jnp.int32)
    part, slot, group = t // 128, (t // 16) % 8, t % 16
    core = jnp.where(slot >= 4, 1 - mine, mine)

    def offset(j):
        return jnp.where(j == 0, 0, jnp.where(j == 3, 2, 2 * j - 3)) + 4

    last, outer, inner = offset(slot % 4), offset(group // 4), offset(group % 4)
    first, second = jnp.where(part == 0, outer, inner), jnp.where(part == 0, last, outer)
    at_x = (x + jnp.where(core == 0, first, second)) % 4
    at_y = (y + jnp.where(core == 0, second, first)) % 4
    at_z = (z + jnp.where(core == 0, last, 8 - last)) % 4
    low = jnp.where(part == 1, at_z % 2, group // 2 % 2)
    high = jnp.where(part == 1, at_z // 2, group % 2)
    return 8 * (((at_y * 2 + low) * 4 + at_x) * 2 + high)


def put_rows(table, first, values, total):
    for group in range(16):
        target = pl.ds(pl.multiple_of(table[first + group], 8), 8)
        total[target, :] = values[8 * group : 8 * group + 8, :]


def write_stats(sides, info, stats):
    column = lax.broadcasted_iota(jnp.int32, (128, HALF), 1).astype(jnp.float32)
    lane = lax.broadcasted_iota(jnp.int32, (128, 128), 1)
    for step in range(HALF // 128):
        rows = slice(128 * step, 128 * step + 128)
        told = jnp.transpose(info[:, rows])
        values = [side[rows, :] for side in sides]
        peaks = [jnp.max(value, axis=1, keepdims=True) for value in values]
        peak = jnp.maximum(*peaks)
        summed = jnp.sum(sum(jnp.exp(value - peak) for value in values), axis=1, keepdims=True)
        hits = [
            jnp.where(column == told[:, number : number + 1], value, 0.0)
            for number, value in enumerate(values)
        ]
        hit = jnp.sum(sum(hits), axis=1, keepdims=True)
        block = jnp.where(lane == 0, peak + jnp.log(summed), jnp.where(lane == 1, hit, 0.0))
        stats[:, rows] = jnp.transpose(block)[0:8, :]


def start(copies):
    for copy in copies:
        copy.start()


def wait(copies):
    for copy in copies:
        copy.wait()


def copies_of(sources, targets, sems):
    return [
        pltpu.make_async_copy(source, target, sems.at[k])
        for k, (source, target) in enumerate(zip(sources, targets))
    ]


def put_slots(table, first, tmp, total):
    for slot in range(tmp.shape[0] // 128):
        put_rows(table, first + 16 * slot, tmp[128 * slot : 128 * slot + 128, :], total)


def early_kernel(table, *refs):
    pieces, (head, head_2, mine, other, xbuf, tmp, sems) = refs[:6], refs[6:]
    places = [pl.ds(128 * k, 128) for k in range(3)]
    arrive = [
        copies_of(pieces[part::2], [xbuf.at[part, place, :] for place in places], sems.at[part])
        for part in (0, 1)
    ]
    start(arrive[0])
    start(arrive[1])
    wait(arrive[0])
    for side, columns in enumerate((head, head_2)):
        tmp[side] = jnp.dot(xbuf[0], columns[0:WIDE, :], preferred_element_type=jnp.float32)
    wait(arrive[1])
    for side, (columns, total) in enumerate(((head, mine), (head_2, other))):
        tmp[side] += jnp.dot(
            xbuf[1], columns[WIDE : 2 * WIDE, :], preferred_element_type=jnp.float32
        )
        put_slots(table, 0, tmp.at[side], total)


def ref_kernel(table, *refs):
    pieces, (head, head_2, mine, other, xbuf, hbuf, tmp, sems) = refs[:3], refs[3:]
    targets = [xbuf.at[pl.ds(128 * k, 128), :] for k in range(3)]
    arrive = copies_of((*pieces, head, head_2), (*targets, hbuf.at[0], hbuf.at[1]), sems)
    start(arrive)
    wait(arrive[:4])
    for side, total in enumerate((mine, other)):
        if side:
            wait(arrive[4:])
        tmp[...] = jnp.dot(xbuf[...], hbuf[side], preferred_element_type=jnp.float32)
        put_slots(table, 128, tmp, total)


def ref_late_kernel(table, *refs):
    far, head, head_2, mine, other, info, stats, xbuf, hbuf, totals, tmp, sems = refs
    sources = (far, head, mine, other, head_2)
    arrive = copies_of(sources, (xbuf, hbuf.at[0], totals.at[0], totals.at[1], hbuf.at[1]), sems)
    start(arrive)
    wait(arrive[:4])
    for side in (0, 1):
        if side:
            wait(arrive[4:])
        tmp[...] = jnp.dot(xbuf[...], hbuf[side], preferred_element_type=jnp.float32)
        put_slots(table, 176, tmp, totals.at[side])
    write_stats((totals.at[0], totals.at[1]), info, stats)


def late_kernel(table, *refs):
    low, top, head, head_2, mine_0, other_0, info, mine, other, stats, xbuf, tmp, sems = refs
    arrive = copies_of((low, top), (xbuf.at[0], xbuf.at[1]), sems)
    start(arrive)
    mine[...], other[...] = mine_0[...], other_0[...]
    wait(arrive)
    for columns, total in ((head, mine), (head_2, other)):
        tmp[...] = jnp.dot(xbuf[0], columns[0:WIDE, :], preferred_element_type=jnp.float32)
        tmp[...] += jnp.dot(
            xbuf[1], columns[WIDE : 2 * WIDE, :], preferred_element_type=jnp.float32
        )
        put_slots(table, 48, tmp, total)
    write_stats((mine, other), info, stats)


def grad_kernel(table, *refs):
    pieces, (mine, other, lse, lse_2, info, out) = refs[:16], refs[16:22]
    xbuf, obuf, plain, ordered, scaled, sems, out_sems = refs[22:]
    logits = [
        pltpu.make_async_copy(source, plain.at[pl.ds(HALF * k, HALF), :], sems.at[2, k])
        for k, source in enumerate((mine, other))
    ]
    start(logits)
    arrive = []
    for part in (0, 1):
        sources = pieces[part::2]
        arrive.append(
            [
                pltpu.make_async_copy(
                    source, xbuf.at[part, pl.ds(128 * k, 128), :], sems.at[part, k]
                )
                for k, source in enumerate(sources)
            ]
        )
    start(arrive[0])
    wait(logits)
    column = lax.broadcasted_iota(jnp.int32, (128, HALF), 1).astype(jnp.float32)
    for step in range(2 * HALF // 128):
        rows = slice(128 * step, 128 * step + 128)
        told = jnp.transpose(info[:, rows])
        joined = lse[step : step + 1, :] if step < 4 else lse_2[step - 4 : step - 3, :]
        joined = jnp.transpose(jnp.broadcast_to(joined, (8, 128)))[:, 0:1]
        hit = (column == told[:, 0:1]).astype(jnp.float32)
        plain[rows, :] = told[:, 2:3] * (jnp.exp(plain[rows, :] - joined) - hit)
    for group in range(128):
        source = pl.multiple_of(table[group] + HALF * (group // 64), 8)
        ordered[8 * group : 8 * group + 8, :] = plain[pl.ds(source, 8), :]
    scaled[...] = ordered[...].astype(jnp.bfloat16)
    steps = WIDE // BLOCK
    sent = []
    for part in (0, 1):
        wait(arrive[part])
        if part == 0:
            start(arrive[1])
        for step in range(steps):
            number = part * steps + step
            if number >= 2:
                sent[number - 2].wait()
            obuf[number % 2] = lax.dot_general(
                xbuf[part, :, BLOCK * step : BLOCK * step + BLOCK],
                scaled[...],
                (((0,), (0,)), ((), ())),
                preferred_element_type=jnp.float32,
            ).astype(jnp.bfloat16)
            sent.append(
                pltpu.make_async_copy(
                    obuf.at[number % 2],
                    out.at[pl.ds(BLOCK * number, BLOCK), :],
                    out_sems.at[number % 2],
                )
            )
            sent[number].start()
    wait(sent[-2:])


ANY = pl.BlockSpec(memory_space=pl.ANY)
INSIDE = pl.BlockSpec(memory_space=pltpu.VMEM)
TABLE = pl.BlockSpec(memory_space=pltpu.SMEM)
DMA = pltpu.SemaphoreType.DMA


def floats(*shape):
    return jax.ShapeDtypeStruct(shape, jnp.float32)


def call(kernel, operands, out_shape, out_specs, scratch, rows, specs, limit=40):
    return pl.pallas_call(
        kernel,
        out_shape=out_shape,
        in_specs=[TABLE, *specs],
        out_specs=out_specs,
        scratch_shapes=scratch,
        compiler_params=pltpu.CompilerParams(vmem_limit_bytes=limit * MIB),
        cost_estimate=pl.CostEstimate(
            flops=4 * rows * HALF * WIDE, bytes_accessed=12 * MIB, transcendentals=0
        ),
    )(*operands)


TOTALS = (floats(HALF, HALF), floats(HALF, HALF))
PRODUCT = pltpu.VMEM((128, HALF), jnp.float32)


def early_call(table, pieces, heads):
    operands = (table, *pieces, *heads)
    specs = [ANY] * 6 + [INSIDE] * 2
    scratch = [
        pltpu.VMEM((2, 384, WIDE), jnp.bfloat16),
        pltpu.VMEM((2, 384, HALF), jnp.float32),
        DMA((2, 3)),
    ]
    return call(early_kernel, operands, TOTALS, (INSIDE,) * 2, scratch, 768, specs)


def ref_call(table, pieces, heads):
    operands = (table, *pieces, *heads)
    scratch = [
        pltpu.VMEM((384, WIDE), jnp.bfloat16),
        pltpu.VMEM((2, WIDE, HALF), jnp.bfloat16),
        pltpu.VMEM((384, HALF), jnp.float32),
        DMA((5,)),
    ]
    return call(ref_kernel, operands, TOTALS, (INSIDE,) * 2, scratch, 384, [ANY] * 5)


def ref_late_call(table, far, heads, totals, info):
    operands = (table, far, *heads, *totals, info)
    scratch = [
        pltpu.VMEM((128, WIDE), jnp.bfloat16),
        pltpu.VMEM((2, WIDE, HALF), jnp.bfloat16),
        pltpu.VMEM((2, HALF, HALF), jnp.float32),
        PRODUCT,
        DMA((5,)),
    ]
    specs = [ANY] * 5 + [INSIDE]
    return call(ref_late_kernel, operands, floats(8, HALF), INSIDE, scratch, 128, specs)


def late_call(table, fars, heads, totals, info):
    operands = (table, *fars, *heads, *totals, info)
    shapes = (*TOTALS, floats(8, HALF))
    scratch = [pltpu.VMEM((2, 128, WIDE), jnp.bfloat16), PRODUCT, DMA((2,))]
    specs = [ANY] * 2 + [INSIDE] * 5
    return call(late_kernel, operands, shapes, (INSIDE,) * 3, scratch, 256, specs)


def grad_call(table, pieces, logits, lses, info):
    scratch = [
        pltpu.VMEM((2, 2 * HALF, WIDE), jnp.bfloat16),
        pltpu.VMEM((2, BLOCK, HALF), jnp.bfloat16),
        pltpu.VMEM((2 * HALF, HALF), jnp.float32),
        pltpu.VMEM((2 * HALF, HALF), jnp.float32),
        pltpu.VMEM((2 * HALF, HALF), jnp.bfloat16),
        DMA((3, 8)),
        DMA((2,)),
    ]
    operands = (table, *pieces, *logits, *lses, info)
    specs = [ANY] * 18 + [INSIDE] * 3
    shape = jax.ShapeDtypeStruct((2 * WIDE, HALF), jnp.bfloat16)
    return call(grad_kernel, operands, shape, ANY, scratch, 1024, specs, 60)


def log_sum(terms, axis):
    peak = jnp.max(terms, axis=axis)
    return peak + jnp.log(jnp.sum(jnp.exp(terms - jnp.expand_dims(peak, axis)), axis=axis))


def core_tokens(values, core):
    values = values.reshape(64, 2, 8)
    return jnp.where(core == 0, values[:, 0], values[:, 1]).reshape(HALF)


def shards(
    ref_rows, ref_gain, trainee_rows, trainee_gain, ref_head, trainee_head, targets, selected
):
    me = lax.axis_index(ALL)
    core = lax.axis_index("c")
    chip = me // 2

    table = row_table(me)
    weight = selected.astype(jnp.float32)

    def info_of(which):
        wanted = core_tokens(targets, which)
        row = lax.broadcasted_iota(jnp.int32, (8, HALF), 0)
        beside = (wanted - HALF * (me ^ 1)).astype(jnp.float32)
        here = (wanted - HALF * me).astype(jnp.float32)
        rest = jnp.where(row == 1, beside[None], core_tokens(weight, which)[None])
        return jnp.where(row == 0, here[None], rest)

    info, info_2 = info_of(core), info_of(1 - core)

    raw = trainee_rows.reshape(2, 2, 8, 2048).transpose(1, 0, 2, 3).reshape(1, 1, 2, 16, 2048)
    raw = jnp.broadcast_to(raw, (2, 2, 2, 16, 2048)).reshape(8, 16, 2048)
    raw, ref = fence(raw, normalize(ref_rows, ref_gain))
    raw = lax.all_to_all(raw, ("zl", "zh", "c"), 0, 0, tiled=True).reshape(2, 4, 16, 2048)
    own = normalize(raw.transpose(0, 2, 1, 3).reshape(32, 2 * WIDE), trainee_gain)
    ref = stack(ring(stack(ring(ref, "xy")), "yx"))
    head_2, ref_head_2 = swap(trainee_head), swap(ref_head)
    own, ref, head_2, ref_head_2 = fence(own, ref, head_2, ref_head_2)
    heads, ref_heads = (trainee_head, head_2), (ref_head, ref_head_2)

    ref_near, ref_back = send(ref, "zz", (1, -1)), send(ref, "zz", (-1, 1))
    own = ring(own, "xy")
    low, top = fence(stack(own, slice(0, WIDE)), stack(own, slice(WIDE, None)))

    low_near, low_back = send(low, "yx", (1, 1)), send(low, "yx", (-1, -1))
    top_near, top_back = send(top, "yx", (1, 1)), send(top, "yx", (-1, -1))
    ref_near, ref_back = fence(ref_near, ref_back)
    ref_far = send(ref_near, "zz", (1, -1))
    ref_totals = ref_call(table, (ref, ref_near, ref_back), ref_heads)
    low, top, low_near, top_near, low_back, top_back, ref_far, *ref_totals = fence(
        low, top, low_near, top_near, low_back, top_back, ref_far, *ref_totals
    )

    low_far, top_far = send(low_near, "yx", (1, 1)), send(top_back, "yx", (-1, -1))
    pieces = (low, top, low_near, top_near, low_back, top_back)
    totals = early_call(table, pieces, heads)
    ref_stats = ref_late_call(table, ref_far, ref_heads, ref_totals, info)
    near_2 = swap(low_near), swap(top_near)
    low_back_2 = swap(low_back)
    low_far, top_far, low_back_2, ref_stats, top_back, low, top, *rest = fence(
        low_far, top_far, low_back_2, ref_stats, top_back, low, top, *totals, *near_2
    )
    totals, near_2 = rest[:2], rest[2:]
    swapped = [swap(piece) for piece in (low, top, top_back, low_far, top_far)]
    mine, other, stats = late_call(table, (low_far, top_far), heads, totals, info)

    rest = jnp.concatenate(
        [ref_stats[0].reshape(64, 8), (stats[1] - ref_stats[1]).reshape(64, 8)], axis=1
    )
    rest = jnp.pad(rest, ((0, 0), (0, 112)))
    message = jnp.concatenate(
        [jnp.broadcast_to(stats[0].reshape(1, 4, 128), (64, 4, 128)), rest[:, None]], axis=1
    )
    message, other, *swapped = fence(message, other, *swapped)
    low_2, top_2, top_back_2, low_far_2, top_far_2 = swapped
    arrived = lax.all_to_all(message, CHIPS, 0, 0, tiled=True)
    other_2 = swap(other)
    lse = log_sum(arrived[:, :4], 0)
    lse_2 = swap(lse)
    found = log_sum(arrived[:, 4, :8], 0)
    hits = jnp.sum(arrived[:, 4, 8:16], axis=0)
    excess = lax.dynamic_slice_in_dim(lse.reshape(HALF), 8 * chip, 8) - found - hits

    pieces = (low, top, low_near, top_near, low_back, top_back, low_far, top_far)
    pieces += (low_2, top_2, *near_2, low_back_2, top_back_2, low_far_2, top_far_2)
    both = jnp.concatenate([info, info_2], axis=1)
    head_grad = grad_call(table, pieces, (mine, other_2), (lse, lse_2), both)
    return excess, head_grad


def solution(mesh):
    grid = Mesh(mesh.devices.reshape(4, 2, 4, 2, 2), ALL)
    in_specs = (P(ALL, None), P(), P(FSDP, TP), P(), P(None, ALL), P(None, ALL), P(), P())
    out_specs = (P(ALL), P(None, ALL))
    return jax.shard_map(shards, mesh=grid, in_specs=in_specs, out_specs=out_specs, check_vma=False)
```

time: 583 us -> 160 us (0.27)
  waiting for transfers between devices: 371 us -> 35.9 us
  blocking collectives: 144 us -> 0 us
  Pallas kernels: 0 us -> 49.9 us
  starting transfers between devices: 0.08 us -> 47.6 us
  matrix products: 45.7 us -> 0 us
  local copies, waits for them, and re-layouts: 0.6 us -> 17.4 us
  between operations: 14.1 us -> 1.32 us
    all_gather x2 -> x0, waiting for transfers between devices: 371 us -> none  [the longest x1 193 us: shards(): lax.all_gather(ref_normed, ('fsdp', 'tp'), axis=0, tiled=True)]
    pmax x1 -> x0, blocking collectives: 68.4 us -> none  [shards(): ref_peak, own_peak = lax.pmax((ref_parts[0], own_high), ('fsdp', 'tp'))]
    psum x1 -> x0, blocking collectives: 64.7 us -> none  [shards(): lax.psum((ref_parts[1] * jnp.exp(ref_parts[0] - ref_peak), ref_parts[2],...]
    pallas_call x0 -> x5, Pallas kernels: none -> 49.9 us  [call(): pl.pallas_call(kernel, out_shape=out_shape, in_specs=[TABLE, *specs], out...]
    dot_general x3 -> x0, matrix products: 45.7 us -> none  [the longest x2 27.8 us: head_stats(): logits = jnp.dot(normed, head, preferred_element_type=jnp.float32)]
    ppermute x0 -> x30, starting transfers between devices: none -> 34.4 us  [the longest x18 24 us: send(): return lax.ppermute(values, ALL, pairs)]
    ppermute x0 -> x30, waiting for transfers between devices: none -> 25.5 us  [the longest x18 25.5 us: send(): return lax.ppermute(values, ALL, pairs)]
    unnamed x4 -> x43, local copies, waits for them, and re-layouts: 0.01 us -> 13.7 us
  transfers between devices with their start and end apart: 2 -> 32, of which waited for: 2 -> 10; matrix products, arithmetic and copies ran while one was open for 2% -> 7% of each run, Pallas kernels for 0% -> 21%
where the time goes in v3:
time: 160 us; the launch traced here: 159 us
  Pallas kernels  49.9 us (31%)
  starting transfers between devices  47.6 us (30%)
  waiting for transfers between devices  35.9 us (22%)
  local copies, waits for them, and re-layouts  17.4 us (11%)
  other arithmetic  7.21 us (5%)
    pallas_call x5, Pallas kernels, call(): pl.pallas_call(kernel, out_shape=out_shape, in_specs=[TABLE, *specs], out...  49.9 us
    ppermute x18, waiting for transfers between devices, send(): return lax.ppermute(values, ALL, pairs)  25.5 us
    ppermute x18, starting transfers between devices, send(): return lax.ppermute(values, ALL, pairs)  24 us
    unnamed x43, local copies, waits for them, and re-layouts  13.7 us
    ppermute x12, starting transfers between devices, swap(): lax.ppermute(values, ALL, [(index, index ^ 1) for index in range(128)])  10.3 us
    all_to_all x1, waiting for transfers between devices, shards(): arrived = lax.all_to_all(message, CHIPS, 0, 0, tiled=True)  8.77 us
    all_to_all x1, starting transfers between devices, shards(): lax.all_to_all(raw, ('zl', 'zh', 'c'), 0, 0, tiled=True)  7.32 us
    all_to_all x1, starting transfers between devices, shards(): arrived = lax.all_to_all(message, CHIPS, 0, 0, tiled=True)  5.89 us
  transfers between devices with their start and end apart: 32, of which 10 were waited for; matrix products, arithmetic and copies ran while one was open for 7% of the time, Pallas kernels for 21%

profile of v3, /device:TPU:1, one launch (start us, length us, event | category | flops | bytes accessed | tf_op | source)
XLA Modules:
  0.0 159.2 jit_solution(4395763542015651118)
XLA Ops:
  0.6 1.5 collective-permute-start.6
  2.1 0.9 copy.59
  3.0 1.0 fusion
  4.0 0.9 fusion.2
  5.0 0.8 broadcast_in_dim.87
  5.8 3.0 %collective-permute-start.2 = (bf16[8,4096]{1,0:T(8,128)(2,1)S(1)}, bf16[8,4096]{1,0:T(8,128)(2,1)S(1)}, u32[]{:S(2)}, u32[]{:S(2)}) collective-permute-start(bf16[8,4096]{1,0:T(8,128)(2,1)S(1)} %fusion.2), channel_id=1, source_target_pairs={{0,8},{1,65},{2,10},{3,67},{4,12},{5,69},{6,14},{7,71},{8,0},{9,73... | collective-permute-start | bytes 196616 | tf_op jit(solution)/shard_map/ppermute | solution.py:38
  8.8 0.8 collective-permute-start.1
  9.6 0.7 collective-permute-start
  10.3 0.7 collective-permute-start.7
  11.0 2.9 %collective-permute-done = bf16[8,4096]{1,0:T(8,128)(2,1)S(1)} collective-permute-done((bf16[8,4096]{1,0:T(8,128)(2,1)S(1)}, bf16[8,4096]{1,0:T(8,128)(2,1)S(1)}, u32[]{:S(2)}, u32[]{:S(2)}) %collective-permute-start) | collective-permute-done | bytes 65568 | tf_op jit(solution)/shard_map/ppermute | solution.py:38
  14.0 1.3 collective-permute-start.3
  15.3 7.3 %all-to-all-start = ((bf16[8,16,2048]{2,1,0:T(8,128)(2,1)}), bf16[8,16,2048]{2,1,0:T(8,128)(2,1)S(1)}, u32[]{:S(2)}, u32[]{:S(2)}) async-start(bf16[8,16,2048]{2,1,0:T(8,128)(2,1)} %bitcast.3), calls=%async_computation | async-start | bytes 1048576 | tf_op jit(solution)/shard_map/all_to_all | solution.py:371
  22.6 0.6 collective-permute-start.5
  23.1 1.2 collective-permute-start.4
  24.4 5.3 %collective-permute-done.4 = bf16[32,4096]{1,0:T(8,128)(2,1)S(1)} collective-permute-done((bf16[32,4096]{1,0:T(8,128)(2,1)S(1)}, bf16[32,4096]{1,0:T(8,128)(2,1)S(1)}, u32[]{:S(2)}, u32[]{:S(2)}) %collective-permute-start.4) | collective-permute-done | bytes 262176 | tf_op jit(solution)/shard_map/ppermute | solution.py:38
  29.8 1.5 all-to-all-done
  31.8 0.7 copy.46
  32.4 0.6 copy.57
  33.3 2.7 %collective-permute-start.10 = (bf16[32,8192]{1,0:T(8,128)(2,1)S(1)}, bf16[32,8192]{1,0:T(8,128)(2,1)S(1)}, u32[]{:S(2)}, u32[]{:S(2)}) collective-permute-start(bf16[32,8192]{1,0:T(8,128)(2,1)S(1)} %multiply_convert_fusion), channel_id=1, source_target_pairs={{0,8},{1,65},{2,10},{3,67},{4,12},{5,69},{6,14},{7,71},{8,0},{9,73... | collective-permute-start | bytes 1572872 | tf_op jit(solution)/shard_map/ppermute | solution.py:38
  36.0 1.1 collective-permute-start.9
  37.0 0.4 collective-permute-start.8
  37.4 2.7 %collective-permute-start.15 = (bf16[128,4096]{1,0:T(8,128)(2,1)S(1)}, bf16[128,4096]{1,0:T(8,128)(2,1)}, u32[]{:S(2)}, u32[]{:S(2)}) collective-permute-start(bf16[128,4096]{1,0:T(8,128)(2,1)S(1)} %constant_dynamic-update-slice_fusion.4.refs_0_), channel_id=1, source_target_pairs={{0,16},{1,19},{2,18},{3,17},{4,20},{5,23},{6,22},{7,21},{8,24},{9,... | collective-permute-start | bytes 3145736 | tf_op jit(solution)/shard_map/ppermute | solution.py:38
  40.1 3.1 %collective-permute-done.10 = bf16[32,8192]{1,0:T(8,128)(2,1)S(1)} collective-permute-done((bf16[32,8192]{1,0:T(8,128)(2,1)S(1)}, bf16[32,8192]{1,0:T(8,128)(2,1)S(1)}, u32[]{:S(2)}, u32[]{:S(2)}) %collective-permute-start.10) | collective-permute-done | bytes 524320 | tf_op jit(solution)/shard_map/ppermute | solution.py:38
  43.2 4.7 %collective-permute-done.9 = bf16[32,8192]{1,0:T(8,128)(2,1)S(1)} collective-permute-done((bf16[32,8192]{1,0:T(8,128)(2,1)S(1)}, bf16[32,8192]{1,0:T(8,128)(2,1)S(1)}, u32[]{:S(2)}, u32[]{:S(2)}) %collective-permute-start.9) | collective-permute-done | bytes 524320 | tf_op jit(solution)/shard_map/ppermute | solution.py:38
  48.0 0.9 collective-permute-done.8
  49.0 1.5 pad_maximum_fusion
  50.4 0.7 collective-permute-start.13
  51.1 0.8 collective-permute-start.11
  51.9 1.9 %collective-permute-start.14 = (bf16[128,4096]{1,0:T(8,128)(2,1)}, bf16[128,4096]{1,0:T(8,128)(2,1)}, u32[]{:S(2)}, u32[]{:S(2)}) collective-permute-start(bf16[128,4096]{1,0:T(8,128)(2,1)} %get-tuple-element.77.refs_1_), channel_id=1, source_target_pairs={{0,96},{1,13},{2,98},{3,15},{4,100},{5,1},{6,102},{7,3},{8,104},{9... | collective-permute-start | bytes 3145736 | tf_op jit(solution)/shard_map/ppermute | solution.py:38
  53.8 7.1 %collective-permute-done.16.refs_2_ = bf16[128,4096]{1,0:T(8,128)(2,1)S(1)} collective-permute-done((bf16[128,4096]{1,0:T(8,128)(2,1)S(1)}, bf16[128,4096]{1,0:T(8,128)(2,1)S(1)}, u32[]{:S(2)}, u32[]{:S(2)}) %collective-permute-start.16) | collective-permute-done | bytes 1048608 | tf_op jit(solution)/shard_map/ppermute | solution.py:38
  60.9 1.0 copy-done.9
  62.0 1.1 collective-permute-done.15.refs_1_
  63.1 3.5 %collective-permute-start.17 = (bf16[128,4096]{1,0:T(8,128)(2,1)}, bf16[128,4096]{1,0:T(8,128)(2,1)S(1)}, u32[]{:S(2)}, u32[]{:S(2)}) collective-permute-start(bf16[128,4096]{1,0:T(8,128)(2,1)} %collective-permute-done.15.refs_1_), channel_id=1, source_target_pairs={{0,16},{1,19},{2,18},{3,17},{4,20},{5,23},{6,22},{7,21},{8,24},{9,... | collective-permute-start | bytes 3145736 | tf_op jit(solution)/shard_map/ppermute | solution.py:38
  67.0 0.4 fusion.4
  67.5 2.2 %copy-done = bf16[4096,512]{1,0:T(8,128)(2,1)S(1)} copy-done((bf16[4096,512]{1,0:T(8,128)(2,1)S(1)}, bf16[4096,512]{1,0:T(8,128)(2,1)}, u32[]{:S(2)}) %copy-start) | copy-done | bytes 4194328
  69.6 1.2 copy-done.10
  70.9 5.5 %shard_map.95 = (f32[512,512]{1,0:T(8,128)S(1)}, f32[512,512]{1,0:T(8,128)S(1)}) custom-call(s32[256]{0:T(256)S(1)} %add_multiply_fusion.table, bf16[128,4096]{1,0:T(8,128)(2,1)S(1)} %constant_dynamic-update-slice_fusion.4.refs_0_, bf16[128,4096]{1,0:T(8,128)(2,1)} %collective-permute-done.15.refs_1_, bf16[128,4096]{1,0:T(8,128)(2,1)S(1)} %copy-done.10, ...), custom_call_target="tpu_custom_call" | custom-call | flops 3221225472 | bytes 12582912 | tf_op jit(solution)/shard_map/pallas_call | solution.py:262
  76.3 1.0 copy-done.4
  77.3 1.0 copy-done.6
  78.3 0.3 collective-permute-done.17.refs_0_
  78.6 3.8 %collective-permute-start.21 = (bf16[128,4096]{1,0:T(8,128)(2,1)}, bf16[128,4096]{1,0:T(8,128)(2,1)}, u32[]{:S(2)}, u32[]{:S(2)}) collective-permute-start(bf16[128,4096]{1,0:T(8,128)(2,1)} %collective-permute-done.11.refs_2_), channel_id=1, source_target_pairs={{0,1},{1,0},{2,3},{3,2},{4,5},{5,4},{6,7},{7,6},{8,9},{9,8},{10,11... | collective-permute-start | bytes 3145736 | tf_op jit(solution)/shard_map/ppermute | solution.py:42
  82.4 2.7 %collective-permute-start.19 = (bf16[128,4096]{1,0:T(8,128)(2,1)}, bf16[128,4096]{1,0:T(8,128)(2,1)S(1)}, u32[]{:S(2)}, u32[]{:S(2)}) collective-permute-start(bf16[128,4096]{1,0:T(8,128)(2,1)} %collective-permute-done.14.refs_5_), channel_id=1, source_target_pairs={{0,96},{1,13},{2,98},{3,15},{4,100},{5,1},{6,102},{7,3},{8,104},{9... | collective-permute-start | bytes 3145736 | tf_op jit(solution)/shard_map/ppermute | solution.py:38
  85.1 0.6 collective-permute-start.20
  85.7 0.2 convert_reduce_fusion.3
  86.5 2.2 %copy-done.1 = bf16[4096,512]{1,0:T(8,128)(2,1)S(1)} copy-done((bf16[4096,512]{1,0:T(8,128)(2,1)S(1)}, bf16[4096,512]{1,0:T(8,128)(2,1)}, u32[]{:S(2)}) %copy-start.1) | copy-done | bytes 4194328
  88.7 1.2 copy-done.5
  89.9 1.2 copy-done.7
  91.1 4.8 %shard_map.96 = f32[8,512]{1,0:T(8,128)S(1)} custom-call(s32[256]{0:T(256)S(1)} %add_multiply_fusion.table, bf16[128,4096]{1,0:T(8,128)(2,1)S(1)} %collective-permute-done.17.refs_0_, bf16[4096,512]{1,0:T(8,128)(2,1)S(1)} %copy-done.1, bf16[4096,512]{1,0:T(8,128)(2,1)} %collective-permute-done.7.refs_4_.refs_2_, f32[512,512]{1,0:T(8,128)S(1)} %copy-done.5, ...), custom_call_target="tpu_custom_call" | custom-call | flops 1073741824 | bytes 12582912 | tf_op jit(solution)/shard_map/pallas_call | solution.py:262
  95.9 14.4 %shard_map.97 = (f32[512,512]{1,0:T(8,128)S(1)}, f32[512,512]{1,0:T(8,128)S(1)}) custom-call(s32[256]{0:T(256)S(1)} %add_multiply_fusion.table, bf16[128,4096]{1,0:T(8,128)(2,1)} %get-tuple-element.76.refs_0_, bf16[128,4096]{1,0:T(8,128)(2,1)} %get-tuple-element.77.refs_1_, bf16[128,4096]{1,0:T(8,128)(2,1)} %collective-permute-done.11.refs_2_, ...), custom_call_target="tpu_custom_call" | custom-call | flops 6442450944 | bytes 12582912 | tf_op jit(solution)/shard_map/pallas_call | solution.py:262
  110.4 0.6 collective-permute-start.23
  111.1 0.4 collective-permute-start.25
  111.6 0.4 collective-permute-start.27
  112.0 9.1 %shard_map.98 = (f32[512,512]{1,0:T(8,128)S(1)}, f32[512,512]{1,0:T(8,128)S(1)}, f32[8,512]{1,0:T(8,128)S(1)}) custom-call(s32[256]{0:T(256)S(1)} %add_multiply_fusion.table, bf16[128,4096]{1,0:T(8,128)(2,1)S(1)} %collective-permute-done.18.refs_0_.refs_6_, bf16[128,4096]{1,0:T(8,128)(2,1)S(1)} %collective-permute-done.19.refs_1_.refs_7_, ...), custom_call_target="tpu_custom_call" | custom-call | flops 2147483648 | bytes 12582912 | tf_op jit(solution)/shard_map/pallas_call | solution.py:262
  121.1 1.0 copy-done.11
  122.4 0.8 pad_maximum_fusion.2
  123.2 5.9 %all-to-all-start.1 = ((f32[64,5,128]{2,1,0:T(8,128)}), f32[64,5,128]{2,1,0:T(8,128)S(1)}, u32[]{:S(2)}, u32[]{:S(2)}) async-start(f32[64,5,128]{2,1,0:T(8,128)} %pad_maximum_fusion.2), calls=%async_computation.1 | async-start | bytes 524288 | tf_op jit(solution)/shard_map/all_to_all | solution.py:413
  129.1 0.6 collective-permute-start.28
  129.8 0.6 pad_maximum_fusion.3.refs_20_
  130.4 8.8 %all-to-all-done.1 = f32[64,5,128]{2,1,0:T(8,128)S(1)} async-done(((f32[64,5,128]{2,1,0:T(8,128)}), f32[64,5,128]{2,1,0:T(8,128)S(1)}, u32[]{:S(2)}, u32[]{:S(2)}) %all-to-all-start.1) | async-done | bytes 163872 | tf_op jit(solution)/shard_map/all_to_all | solution.py:413
  139.5 1.5 collective-permute-start.29
  141.3 0.6 subtract_subtract_fusion
  141.9 0.5 copy-done.17
  142.4 0.4 copy-done.16
  142.9 16.1 %shard_map.99 = bf16[8192,512]{1,0:T(8,128)(2,1)} custom-call(s32[256]{0:T(256)} %copy-done.8, bf16[128,4096]{1,0:T(8,128)(2,1)} %get-tuple-element.76.refs_0_, bf16[128,4096]{1,0:T(8,128)(2,1)} %get-tuple-element.77.refs_1_, bf16[128,4096]{1,0:T(8,128)(2,1)} %collective-permute-done.11.refs_2_, bf16[128,4096]{1,0:T(8,128)(2,1)} %collective-permute-done.12.refs_3_, ...), custom_call_target="tpu_custom_call" | custom-call | flops 8589934592 | bytes 12582912 | tf_op jit(solution)/shard_map/pallas_call | solution.py:262
  (95 shorter events, 3.1 us)
Async XLA Ops:
  0.6 32.6 %collective-permute-start.6 = (bf16[8192,512]{1,0:T(8,128)(2,1)}, bf16[8192,512]{1,0:T(8,128)(2,1)}, u32[]{:S(2)}, u32[]{:S(2)}) collective-permute-start(bf16[8192,512]{1,0:T(8,128)(2,1)} %refs_2_.1), channel_id=1, source_target_pairs={{0,1},{1,0},{2,3},{3,2},{4,5},{5,4},{6,7},{7,6},{8,9},{9,8},{10,11... | collective-permute-start | bytes 25165832 | tf_op jit(solution)/shard_map/ppermute | solution.py:42
  5.8 8.1 %collective-permute-start.2 = (bf16[8,4096]{1,0:T(8,128)(2,1)S(1)}, bf16[8,4096]{1,0:T(8,128)(2,1)S(1)}, u32[]{:S(2)}, u32[]{:S(2)}) collective-permute-start(bf16[8,4096]{1,0:T(8,128)(2,1)S(1)} %fusion.2), channel_id=1, source_target_pairs={{0,8},{1,65},{2,10},{3,67},{4,12},{5,69},{6,14},{7,71},{8,0},{9,73... | collective-permute-start | bytes 196616 | tf_op jit(solution)/shard_map/ppermute | solution.py:38
  8.8 5.1 %collective-permute-start.1 = (bf16[8,4096]{1,0:T(8,128)(2,1)S(1)}, bf16[8,4096]{1,0:T(8,128)(2,1)S(1)}, u32[]{:S(2)}, u32[]{:S(2)}) collective-permute-start(bf16[8,4096]{1,0:T(8,128)(2,1)S(1)} %fusion.2), channel_id=1, source_target_pairs={{0,12},{1,97},{2,14},{3,99},{4,0},{5,101},{6,2},{7,103},{8,4},{9,1... | collective-permute-start | bytes 196616 | tf_op jit(solution)/shard_map/ppermute | solution.py:38
  9.6 4.3 %collective-permute-start = (bf16[8,4096]{1,0:T(8,128)(2,1)S(1)}, bf16[8,4096]{1,0:T(8,128)(2,1)S(1)}, u32[]{:S(2)}, u32[]{:S(2)}) collective-permute-start(bf16[8,4096]{1,0:T(8,128)(2,1)S(1)} %fusion.2), channel_id=1, source_target_pairs={{0,4},{1,33},{2,6},{3,35},{4,8},{5,37},{6,10},{7,39},{8,12},{9,41}... | collective-permute-start | bytes 196616 | tf_op jit(solution)/shard_map/ppermute | solution.py:38
  10.3 23.0 %collective-permute-start.7 = (bf16[4096,512]{1,0:T(8,128)(2,1)}, bf16[4096,512]{1,0:T(8,128)(2,1)}, u32[]{:S(2)}, u32[]{:S(2)}) collective-permute-start(bf16[4096,512]{1,0:T(8,128)(2,1)} %refs_1_.1), channel_id=1, source_target_pairs={{0,1},{1,0},{2,3},{3,2},{4,5},{5,4},{6,7},{7,6},{8,9},{9,8},{10,11... | collective-permute-start | bytes 12582920 | tf_op jit(solution)/shard_map/ppermute | solution.py:42
  14.0 10.4 %collective-permute-start.3 = (bf16[32,4096]{1,0:T(8,128)(2,1)S(1)}, bf16[32,4096]{1,0:T(8,128)(2,1)S(1)}, u32[]{:S(2)}, u32[]{:S(2)}) collective-permute-start(bf16[32,4096]{1,0:T(8,128)(2,1)S(1)} %get-tuple-element.111), channel_id=1, source_target_pairs={{0,32},{1,5},{2,34},{3,7},{4,36},{5,9},{6,38},{7,11},{8,40},{9,13}... | collective-permute-start | bytes 786440 | tf_op jit(solution)/shard_map/ppermute | solution.py:38
  15.3 16.1 %all-to-all-start = ((bf16[8,16,2048]{2,1,0:T(8,128)(2,1)}), bf16[8,16,2048]{2,1,0:T(8,128)(2,1)S(1)}, u32[]{:S(2)}, u32[]{:S(2)}) async-start(bf16[8,16,2048]{2,1,0:T(8,128)(2,1)} %bitcast.3), calls=%async_computation | async-start | bytes 1048576 | tf_op jit(solution)/shard_map/all_to_all | solution.py:371
  22.6 7.2 %collective-permute-start.5 = (bf16[32,4096]{1,0:T(8,128)(2,1)S(1)}, bf16[32,4096]{1,0:T(8,128)(2,1)S(1)}, u32[]{:S(2)}, u32[]{:S(2)}) collective-permute-start(bf16[32,4096]{1,0:T(8,128)(2,1)S(1)} %get-tuple-element.111), channel_id=1, source_target_pairs={{0,64},{1,9},{2,66},{3,11},{4,68},{5,13},{6,70},{7,15},{8,72},{9,1... | collective-permute-start | bytes 786440 | tf_op jit(solution)/shard_map/ppermute | solution.py:38
  23.1 6.6 %collective-permute-start.4 = (bf16[32,4096]{1,0:T(8,128)(2,1)S(1)}, bf16[32,4096]{1,0:T(8,128)(2,1)S(1)}, u32[]{:S(2)}, u32[]{:S(2)}) collective-permute-start(bf16[32,4096]{1,0:T(8,128)(2,1)S(1)} %get-tuple-element.111), channel_id=1, source_target_pairs={{0,96},{1,13},{2,98},{3,15},{4,100},{5,1},{6,102},{7,3},{8,104},{9... | collective-permute-start | bytes 786440 | tf_op jit(solution)/shard_map/ppermute | solution.py:38
  31.7 1.3 copy-start.12
  33.3 10.0 %collective-permute-start.10 = (bf16[32,8192]{1,0:T(8,128)(2,1)S(1)}, bf16[32,8192]{1,0:T(8,128)(2,1)S(1)}, u32[]{:S(2)}, u32[]{:S(2)}) collective-permute-start(bf16[32,8192]{1,0:T(8,128)(2,1)S(1)} %multiply_convert_fusion), channel_id=1, source_target_pairs={{0,8},{1,65},{2,10},{3,67},{4,12},{5,69},{6,14},{7,71},{8,0},{9,73... | collective-permute-start | bytes 1572872 | tf_op jit(solution)/shard_map/ppermute | solution.py:38
  36.0 12.0 %collective-permute-start.9 = (bf16[32,8192]{1,0:T(8,128)(2,1)S(1)}, bf16[32,8192]{1,0:T(8,128)(2,1)S(1)}, u32[]{:S(2)}, u32[]{:S(2)}) collective-permute-start(bf16[32,8192]{1,0:T(8,128)(2,1)S(1)} %multiply_convert_fusion), channel_id=1, source_target_pairs={{0,12},{1,97},{2,14},{3,99},{4,0},{5,101},{6,2},{7,103},{8,4},{9,1... | collective-permute-start | bytes 1572872 | tf_op jit(solution)/shard_map/ppermute | solution.py:38
  37.0 11.9 %collective-permute-start.8 = (bf16[32,8192]{1,0:T(8,128)(2,1)S(1)}, bf16[32,8192]{1,0:T(8,128)(2,1)S(1)}, u32[]{:S(2)}, u32[]{:S(2)}) collective-permute-start(bf16[32,8192]{1,0:T(8,128)(2,1)S(1)} %multiply_convert_fusion), channel_id=1, source_target_pairs={{0,4},{1,33},{2,6},{3,35},{4,8},{5,37},{6,10},{7,39},{8,12},{9,41}... | collective-permute-start | bytes 1572872 | tf_op jit(solution)/shard_map/ppermute | solution.py:38
  37.4 23.5 %collective-permute-start.16 = (bf16[128,4096]{1,0:T(8,128)(2,1)S(1)}, bf16[128,4096]{1,0:T(8,128)(2,1)S(1)}, u32[]{:S(2)}, u32[]{:S(2)}) collective-permute-start(bf16[128,4096]{1,0:T(8,128)(2,1)S(1)} %constant_dynamic-update-slice_fusion.4.refs_0_), channel_id=1, source_target_pairs={{0,18},{1,17},{2,16},{3,19},{4,22},{5,21},{6,20},{7,23},{8,26},{9,... | collective-permute-start | bytes 3145736 | tf_op jit(solution)/shard_map/ppermute | solution.py:38
  37.4 25.6 %collective-permute-start.15 = (bf16[128,4096]{1,0:T(8,128)(2,1)S(1)}, bf16[128,4096]{1,0:T(8,128)(2,1)}, u32[]{:S(2)}, u32[]{:S(2)}) collective-permute-start(bf16[128,4096]{1,0:T(8,128)(2,1)S(1)} %constant_dynamic-update-slice_fusion.4.refs_0_), channel_id=1, source_target_pairs={{0,16},{1,19},{2,18},{3,17},{4,20},{5,23},{6,22},{7,21},{8,24},{9,... | collective-permute-start | bytes 3145736 | tf_op jit(solution)/shard_map/ppermute | solution.py:38
  48.9 17.7 %copy-start.14 = (s32[1024]{0:T(1024)S(1)}, s32[1024]{0:T(1024)}, u32[]{:S(2)}) copy-start(s32[1024]{0:T(1024)} %param.15) | copy-start | bytes 12292
  48.9 17.8 %copy-start.13 = (s32[1024]{0:T(1024)S(1)}, s32[1024]{0:T(1024)}, u32[]{:S(2)}) copy-start(s32[1024]{0:T(1024)} %param.14) | copy-start | bytes 12292
  50.4 27.9 %collective-permute-start.13 = (bf16[128,4096]{1,0:T(8,128)(2,1)}, bf16[128,4096]{1,0:T(8,128)(2,1)}, u32[]{:S(2)}, u32[]{:S(2)}) collective-permute-start(bf16[128,4096]{1,0:T(8,128)(2,1)} %get-tuple-element.76.refs_0_), channel_id=1, source_target_pairs={{0,96},{1,13},{2,98},{3,15},{4,100},{5,1},{6,102},{7,3},{8,104},{9... | collective-permute-start | bytes 3145736 | tf_op jit(solution)/shard_map/ppermute | solution.py:38
  51.1 27.2 %collective-permute-start.11 = (bf16[128,4096]{1,0:T(8,128)(2,1)}, bf16[128,4096]{1,0:T(8,128)(2,1)}, u32[]{:S(2)}, u32[]{:S(2)}) collective-permute-start(bf16[128,4096]{1,0:T(8,128)(2,1)} %get-tuple-element.76.refs_0_), channel_id=1, source_target_pairs={{0,32},{1,5},{2,34},{3,7},{4,36},{5,9},{6,38},{7,11},{8,40},{9,13}... | collective-permute-start | bytes 3145736 | tf_op jit(solution)/shard_map/ppermute | solution.py:38
  51.9 26.4 %collective-permute-start.14 = (bf16[128,4096]{1,0:T(8,128)(2,1)}, bf16[128,4096]{1,0:T(8,128)(2,1)}, u32[]{:S(2)}, u32[]{:S(2)}) collective-permute-start(bf16[128,4096]{1,0:T(8,128)(2,1)} %get-tuple-element.77.refs_1_), channel_id=1, source_target_pairs={{0,96},{1,13},{2,98},{3,15},{4,100},{5,1},{6,102},{7,3},{8,104},{9... | collective-permute-start | bytes 3145736 | tf_op jit(solution)/shard_map/ppermute | solution.py:38
  60.9 1.0 copy-start.9
  61.8 16.5 %collective-permute-start.12 = (bf16[128,4096]{1,0:T(8,128)(2,1)}, bf16[128,4096]{1,0:T(8,128)(2,1)}, u32[]{:S(2)}, u32[]{:S(2)}) collective-permute-start(bf16[128,4096]{1,0:T(8,128)(2,1)} %get-tuple-element.77.refs_1_), channel_id=1, source_target_pairs={{0,32},{1,5},{2,34},{3,7},{4,36},{5,9},{6,38},{7,11},{8,40},{9,13}... | collective-permute-start | bytes 3145736 | tf_op jit(solution)/shard_map/ppermute | solution.py:38
  63.1 15.6 %collective-permute-start.17 = (bf16[128,4096]{1,0:T(8,128)(2,1)}, bf16[128,4096]{1,0:T(8,128)(2,1)S(1)}, u32[]{:S(2)}, u32[]{:S(2)}) collective-permute-start(bf16[128,4096]{1,0:T(8,128)(2,1)} %collective-permute-done.15.refs_1_), channel_id=1, source_target_pairs={{0,16},{1,19},{2,18},{3,17},{4,20},{5,23},{6,22},{7,21},{8,24},{9,... | collective-permute-start | bytes 3145736 | tf_op jit(solution)/shard_map/ppermute | solution.py:38
  67.0 45.0 %copy-start.8 = (s32[256]{0:T(256)}, s32[256]{0:T(256)S(1)}, u32[]{:S(2)}) copy-start(s32[256]{0:T(256)S(1)} %add_multiply_fusion.table) | copy-start | bytes 3076
  67.4 2.2 %copy-start = (bf16[4096,512]{1,0:T(8,128)(2,1)S(1)}, bf16[4096,512]{1,0:T(8,128)(2,1)}, u32[]{:S(2)}) copy-start(bf16[4096,512]{1,0:T(8,128)(2,1)} %refs_1_.1) | copy-start | bytes 12582916
  69.6 1.2 copy-start.10
  76.3 1.0 copy-start.4
  77.3 1.0 copy-start.6
  78.6 31.7 %collective-permute-start.21 = (bf16[128,4096]{1,0:T(8,128)(2,1)}, bf16[128,4096]{1,0:T(8,128)(2,1)}, u32[]{:S(2)}, u32[]{:S(2)}) collective-permute-start(bf16[128,4096]{1,0:T(8,128)(2,1)} %collective-permute-done.11.refs_2_), channel_id=1, source_target_pairs={{0,1},{1,0},{2,3},{3,2},{4,5},{5,4},{6,7},{7,6},{8,9},{9,8},{10,11... | collective-permute-start | bytes 3145736 | tf_op jit(solution)/shard_map/ppermute | solution.py:42
  82.4 28.0 %collective-permute-start.18 = (bf16[128,4096]{1,0:T(8,128)(2,1)}, bf16[128,4096]{1,0:T(8,128)(2,1)S(1)}, u32[]{:S(2)}, u32[]{:S(2)}) collective-permute-start(bf16[128,4096]{1,0:T(8,128)(2,1)} %collective-permute-done.11.refs_2_), channel_id=1, source_target_pairs={{0,32},{1,5},{2,34},{3,7},{4,36},{5,9},{6,38},{7,11},{8,40},{9,13}... | collective-permute-start | bytes 3145736 | tf_op jit(solution)/shard_map/ppermute | solution.py:38
  82.4 27.9 %collective-permute-start.19 = (bf16[128,4096]{1,0:T(8,128)(2,1)}, bf16[128,4096]{1,0:T(8,128)(2,1)S(1)}, u32[]{:S(2)}, u32[]{:S(2)}) collective-permute-start(bf16[128,4096]{1,0:T(8,128)(2,1)} %collective-permute-done.14.refs_5_), channel_id=1, source_target_pairs={{0,96},{1,13},{2,98},{3,15},{4,100},{5,1},{6,102},{7,3},{8,104},{9... | collective-permute-start | bytes 3145736 | tf_op jit(solution)/shard_map/ppermute | solution.py:38
  85.1 25.2 %collective-permute-start.20 = (bf16[128,4096]{1,0:T(8,128)(2,1)}, bf16[128,4096]{1,0:T(8,128)(2,1)}, u32[]{:S(2)}, u32[]{:S(2)}) collective-permute-start(bf16[128,4096]{1,0:T(8,128)(2,1)} %collective-permute-done.13.refs_4_), channel_id=1, source_target_pairs={{0,1},{1,0},{2,3},{3,2},{4,5},{5,4},{6,7},{7,6},{8,9},{9,8},{10,11... | collective-permute-start | bytes 3145736 | tf_op jit(solution)/shard_map/ppermute | solution.py:42
  85.7 24.7 %collective-permute-start.22 = (bf16[128,4096]{1,0:T(8,128)(2,1)}, bf16[128,4096]{1,0:T(8,128)(2,1)}, u32[]{:S(2)}, u32[]{:S(2)}) collective-permute-start(bf16[128,4096]{1,0:T(8,128)(2,1)} %collective-permute-done.12.refs_3_), channel_id=1, source_target_pairs={{0,1},{1,0},{2,3},{3,2},{4,5},{5,4},{6,7},{7,6},{8,9},{9,8},{10,11... | collective-permute-start | bytes 3145736 | tf_op jit(solution)/shard_map/ppermute | solution.py:42
  86.5 2.2 %copy-start.1 = (bf16[4096,512]{1,0:T(8,128)(2,1)S(1)}, bf16[4096,512]{1,0:T(8,128)(2,1)}, u32[]{:S(2)}) copy-start(bf16[4096,512]{1,0:T(8,128)(2,1)} %refs_1_.1) | copy-start | bytes 12582916
  88.7 1.2 copy-start.5
  89.9 1.2 copy-start.7
  110.3 10.8 %copy-start.3 = (bf16[128,4096]{1,0:T(8,128)(2,1)}, bf16[128,4096]{1,0:T(8,128)(2,1)S(1)}, u32[]{:S(2)}) copy-start(bf16[128,4096]{1,0:T(8,128)(2,1)S(1)} %collective-permute-done.19.refs_1_.refs_7_) | copy-start | bytes 3145732
  110.4 10.7 %copy-start.2 = (bf16[128,4096]{1,0:T(8,128)(2,1)}, bf16[128,4096]{1,0:T(8,128)(2,1)S(1)}, u32[]{:S(2)}) copy-start(bf16[128,4096]{1,0:T(8,128)(2,1)S(1)} %collective-permute-done.18.refs_0_.refs_6_) | copy-start | bytes 3145732
  110.4 12.8 %collective-permute-start.23 = (bf16[128,4096]{1,0:T(8,128)(2,1)}, bf16[128,4096]{1,0:T(8,128)(2,1)}, u32[]{:S(2)}, u32[]{:S(2)}) collective-permute-start(bf16[128,4096]{1,0:T(8,128)(2,1)} %get-tuple-element.76.refs_0_), channel_id=1, source_target_pairs={{0,1},{1,0},{2,3},{3,2},{4,5},{5,4},{6,7},{7,6},{8,9},{9,8},{10,11... | collective-permute-start | bytes 3145736 | tf_op jit(solution)/shard_map/ppermute | solution.py:42
  111.0 12.2 %collective-permute-start.24 = (bf16[128,4096]{1,0:T(8,128)(2,1)}, bf16[128,4096]{1,0:T(8,128)(2,1)}, u32[]{:S(2)}, u32[]{:S(2)}) collective-permute-start(bf16[128,4096]{1,0:T(8,128)(2,1)} %get-tuple-element.77.refs_1_), channel_id=1, source_target_pairs={{0,1},{1,0},{2,3},{3,2},{4,5},{5,4},{6,7},{7,6},{8,9},{9,8},{10,11... | collective-permute-start | bytes 3145736 | tf_op jit(solution)/shard_map/ppermute | solution.py:42
  111.1 12.1 %collective-permute-start.25 = (bf16[128,4096]{1,0:T(8,128)(2,1)}, bf16[128,4096]{1,0:T(8,128)(2,1)}, u32[]{:S(2)}, u32[]{:S(2)}) collective-permute-start(bf16[128,4096]{1,0:T(8,128)(2,1)} %collective-permute-done.14.refs_5_), channel_id=1, source_target_pairs={{0,1},{1,0},{2,3},{3,2},{4,5},{5,4},{6,7},{7,6},{8,9},{9,8},{10,11... | collective-permute-start | bytes 3145736 | tf_op jit(solution)/shard_map/ppermute | solution.py:42
  111.5 11.7 %collective-permute-start.26 = (bf16[128,4096]{1,0:T(8,128)(2,1)S(1)}, bf16[128,4096]{1,0:T(8,128)(2,1)}, u32[]{:S(2)}, u32[]{:S(2)}) collective-permute-start(bf16[128,4096]{1,0:T(8,128)(2,1)S(1)} %collective-permute-done.18.refs_0_.refs_6_), channel_id=1, source_target_pairs={{0,1},{1,0},{2,3},{3,2},{4,5},{5,4},{6,7},{7,6},{8,9},{9,8},{10,11... | collective-permute-start | bytes 3145736 | tf_op jit(solution)/shard_map/ppermute | solution.py:42
  111.6 11.6 %collective-permute-start.27 = (bf16[128,4096]{1,0:T(8,128)(2,1)S(1)}, bf16[128,4096]{1,0:T(8,128)(2,1)}, u32[]{:S(2)}, u32[]{:S(2)}) collective-permute-start(bf16[128,4096]{1,0:T(8,128)(2,1)S(1)} %collective-permute-done.19.refs_1_.refs_7_), channel_id=1, source_target_pairs={{0,1},{1,0},{2,3},{3,2},{4,5},{5,4},{6,7},{7,6},{8,9},{9,8},{10,11... | collective-permute-start | bytes 3145736 | tf_op jit(solution)/shard_map/ppermute | solution.py:42
  121.1 1.0 copy-start.11
  123.2 15.9 %all-to-all-start.1 = ((f32[64,5,128]{2,1,0:T(8,128)}), f32[64,5,128]{2,1,0:T(8,128)S(1)}, u32[]{:S(2)}, u32[]{:S(2)}) async-start(f32[64,5,128]{2,1,0:T(8,128)} %pad_maximum_fusion.2), calls=%async_computation.1 | async-start | bytes 524288 | tf_op jit(solution)/shard_map/all_to_all | solution.py:413
  129.1 12.8 %collective-permute-start.28 = (f32[512,512]{1,0:T(8,128)S(1)}, f32[512,512]{1,0:T(8,128)S(1)}, u32[]{:S(2)}, u32[]{:S(2)}) collective-permute-start(f32[512,512]{1,0:T(8,128)S(1)} %get-tuple-element.89), channel_id=1, source_target_pairs={{0,1},{1,0},{2,3},{3,2},{4,5},{5,4},{6,7},{7,6},{8,9},{9,8},{10,11... | collective-permute-start | bytes 3145736 | tf_op jit(solution)/shard_map/ppermute | solution.py:42
  139.5 2.4 %copy-start.15 = (f32[4,128]{1,0:T(4,128)}, f32[4,128]{1,0:T(4,128)S(1)}, u32[]{:S(2)}) copy-start(f32[4,128]{1,0:T(4,128)S(1)} %log_add_fusion.refs_18_) | copy-start | bytes 6148
  139.5 2.4 %collective-permute-start.29 = (f32[4,128]{1,0:T(4,128)S(1)}, f32[4,128]{1,0:T(4,128)S(1)}, u32[]{:S(2)}, u32[]{:S(2)}) collective-permute-start(f32[4,128]{1,0:T(4,128)S(1)} %log_add_fusion.refs_18_), channel_id=1, source_target_pairs={{0,1},{1,0},{2,3},{3,2},{4,5},{5,4},{6,7},{7,6},{8,9},{9,8},{10,11... | collective-permute-start | bytes 6152 | tf_op jit(solution)/shard_map/ppermute | solution.py:42
  141.9 0.5 copy-start.17
  141.9 1.0 copy-start.16

commit v4 on v3

--- a/solution.py
+++ b/solution.py
@@ -14,6 +14,7 @@
 WIDE = 4096
 HALF = 512
 BLOCK = 1024
+DEEP = 2048
 MIB = 1 << 20
 
 
@@ -122,70 +123,71 @@
 
 
 def put_slots(table, first, tmp, total):
-    for slot in range(tmp.shape[0] // 128):
+    for slot in range(4):
         put_rows(table, first + 16 * slot, tmp[128 * slot : 128 * slot + 128, :], total)
 
 
-def early_kernel(table, *refs):
-    pieces, (head, head_2, mine, other, xbuf, tmp, sems) = refs[:6], refs[6:]
-    places = [pl.ds(128 * k, 128) for k in range(3)]
-    arrive = [
-        copies_of(pieces[part::2], [xbuf.at[part, place, :] for place in places], sems.at[part])
-        for part in (0, 1)
-    ]
-    start(arrive[0])
-    start(arrive[1])
-    wait(arrive[0])
-    for side, columns in enumerate((head, head_2)):
-        tmp[side] = jnp.dot(xbuf[0], columns[0:WIDE, :], preferred_element_type=jnp.float32)
-    wait(arrive[1])
-    for side, (columns, total) in enumerate(((head, mine), (head_2, other))):
-        tmp[side] += jnp.dot(
-            xbuf[1], columns[WIDE : 2 * WIDE, :], preferred_element_type=jnp.float32
-        )
+def add_product(tmp, step, rows, columns):
+    product = jnp.dot(rows, columns, preferred_element_type=jnp.float32)
+    tmp[...] = tmp[...] + product if step else product
+
+
+class Stages:
+    def __init__(self, stages, sems):
+        self.copies = []
+        for number, (sources, targets) in enumerate(stages):
+            self.copies.append(copies_of(sources, targets, sems.at[number]))
+        for number in range(3):
+            self.start(number)
+
+    def start(self, number):
+        if number < len(self.copies):
+            start(self.copies[number])
+
+    def wait(self, number):
+        wait(self.copies[number])
+        self.start(number + 3)
+
+
+def own_kernel(table, *refs):
+    pieces, (head, head_2, info, mine, other, stats, xbuf, hbuf, tmp, sems) = refs[:8], refs[8:]
+    stages = []
+    for step in range(2 * WIDE // DEEP):
+        cut = pl.ds(DEEP * step, DEEP)
+        part, within = DEEP * step // WIDE, pl.ds(DEEP * step % WIDE, DEEP)
+        sources = [piece.at[:, within] for piece in pieces[part::2]]
+        targets = [xbuf.at[pl.ds(128 * k, 128), cut] for k in range(4)]
+        stages.append((sources + [head.at[cut, :]], targets + [hbuf.at[0, cut, :]]))
+        stages.append(([head_2.at[cut, :]], [hbuf.at[1, cut, :]]))
+    stages = Stages(stages, sems)
+    for step in range(2 * WIDE // DEEP):
+        cut = slice(DEEP * step, DEEP * step + DEEP)
+        for side in (0, 1):
+            stages.wait(2 * step + side)
+            add_product(tmp.at[side], step, xbuf[:, cut], hbuf[side, cut, :])
+    for side, total in enumerate((mine, other)):
         put_slots(table, 0, tmp.at[side], total)
+    write_stats((mine, other), info, stats)
 
 
 def ref_kernel(table, *refs):
-    pieces, (head, head_2, mine, other, xbuf, hbuf, tmp, sems) = refs[:3], refs[3:]
-    targets = [xbuf.at[pl.ds(128 * k, 128), :] for k in range(3)]
-    arrive = copies_of((*pieces, head, head_2), (*targets, hbuf.at[0], hbuf.at[1]), sems)
-    start(arrive)
-    wait(arrive[:4])
-    for side, total in enumerate((mine, other)):
-        if side:
-            wait(arrive[4:])
-        tmp[...] = jnp.dot(xbuf[...], hbuf[side], preferred_element_type=jnp.float32)
-        put_slots(table, 128, tmp, total)
-
-
-def ref_late_kernel(table, *refs):
-    far, head, head_2, mine, other, info, stats, xbuf, hbuf, totals, tmp, sems = refs
-    sources = (far, head, mine, other, head_2)
-    arrive = copies_of(sources, (xbuf, hbuf.at[0], totals.at[0], totals.at[1], hbuf.at[1]), sems)
-    start(arrive)
-    wait(arrive[:4])
+    pieces, (head, head_2, info, stats, xbuf, hbuf, tmp, total, sems) = refs[:4], refs[4:]
+    stages = []
+    for step in range(WIDE // DEEP):
+        cut = pl.ds(DEEP * step, DEEP)
+        sources = [piece.at[:, cut] for piece in pieces]
+        targets = [xbuf.at[pl.ds(128 * k, 128), cut] for k in range(4)]
+        stages.append((sources + [head.at[cut, :]], targets + [hbuf.at[0, cut, :]]))
+        stages.append(([head_2.at[cut, :]], [hbuf.at[1, cut, :]]))
+    stages = Stages(stages, sems)
+    for step in range(WIDE // DEEP):
+        cut = slice(DEEP * step, DEEP * step + DEEP)
+        for side in (0, 1):
+            stages.wait(2 * step + side)
+            add_product(tmp.at[side], step, xbuf[:, cut], hbuf[side, cut, :])
     for side in (0, 1):
-        if side:
-            wait(arrive[4:])
-        tmp[...] = jnp.dot(xbuf[...], hbuf[side], preferred_element_type=jnp.float32)
-        put_slots(table, 176, tmp, totals.at[side])
-    write_stats((totals.at[0], totals.at[1]), info, stats)
-
-
-def late_kernel(table, *refs):
-    low, top, head, head_2, mine_0, other_0, info, mine, other, stats, xbuf, tmp, sems = refs
-    arrive = copies_of((low, top), (xbuf.at[0], xbuf.at[1]), sems)
-    start(arrive)
-    mine[...], other[...] = mine_0[...], other_0[...]
-    wait(arrive)
-    for columns, total in ((head, mine), (head_2, other)):
-        tmp[...] = jnp.dot(xbuf[0], columns[0:WIDE, :], preferred_element_type=jnp.float32)
-        tmp[...] += jnp.dot(
-            xbuf[1], columns[WIDE : 2 * WIDE, :], preferred_element_type=jnp.float32
-        )
-        put_slots(table, 48, tmp, total)
-    write_stats((mine, other), info, stats)
+        put_slots(table, 128, tmp.at[side], total.at[side])
+    write_stats((total.at[0], total.at[1]), info, stats)
 
 
 def grad_kernel(table, *refs):
@@ -258,14 +260,14 @@
     return jax.ShapeDtypeStruct(shape, jnp.float32)
 
 
-def call(kernel, operands, out_shape, out_specs, scratch, rows, specs, limit=40):
+def call(kernel, operands, out_shape, out_specs, scratch, rows, specs):
     return pl.pallas_call(
         kernel,
         out_shape=out_shape,
         in_specs=[TABLE, *specs],
         out_specs=out_specs,
         scratch_shapes=scratch,
-        compiler_params=pltpu.CompilerParams(vmem_limit_bytes=limit * MIB),
+        compiler_params=pltpu.CompilerParams(vmem_limit_bytes=60 * MIB),
         cost_estimate=pl.CostEstimate(
             flops=4 * rows * HALF * WIDE, bytes_accessed=12 * MIB, transcendentals=0
         ),
@@ -273,50 +275,32 @@
 
 
 TOTALS = (floats(HALF, HALF), floats(HALF, HALF))
-PRODUCT = pltpu.VMEM((128, HALF), jnp.float32)
-
-
-def early_call(table, pieces, heads):
-    operands = (table, *pieces, *heads)
-    specs = [ANY] * 6 + [INSIDE] * 2
+
+
+def own_call(table, pieces, heads, info):
+    operands = (table, *pieces, *heads, info)
+    shapes = (*TOTALS, floats(8, HALF))
     scratch = [
-        pltpu.VMEM((2, 384, WIDE), jnp.bfloat16),
-        pltpu.VMEM((2, 384, HALF), jnp.float32),
-        DMA((2, 3)),
+        pltpu.VMEM((HALF, 2 * WIDE), jnp.bfloat16),
+        pltpu.VMEM((2, 2 * WIDE, HALF), jnp.bfloat16),
+        pltpu.VMEM((2, HALF, HALF), jnp.float32),
+        DMA((4 * WIDE // DEEP, 5)),
     ]
-    return call(early_kernel, operands, TOTALS, (INSIDE,) * 2, scratch, 768, specs)
-
-
-def ref_call(table, pieces, heads):
-    operands = (table, *pieces, *heads)
+    specs = [ANY] * 10 + [INSIDE]
+    return call(own_kernel, operands, shapes, (INSIDE,) * 3, scratch, 1024, specs)
+
+
+def ref_call(table, pieces, heads, info):
+    operands = (table, *pieces, *heads, info)
     scratch = [
-        pltpu.VMEM((384, WIDE), jnp.bfloat16),
-        pltpu.VMEM((2, WIDE, HALF), jnp.bfloat16),
-        pltpu.VMEM((384, HALF), jnp.float32),
-        DMA((5,)),
-    ]
-    return call(ref_kernel, operands, TOTALS, (INSIDE,) * 2, scratch, 384, [ANY] * 5)
-
-
-def ref_late_call(table, far, heads, totals, info):
-    operands = (table, far, *heads, *totals, info)
-    scratch = [
-        pltpu.VMEM((128, WIDE), jnp.bfloat16),
+        pltpu.VMEM((HALF, WIDE), jnp.bfloat16),
         pltpu.VMEM((2, WIDE, HALF), jnp.bfloat16),
         pltpu.VMEM((2, HALF, HALF), jnp.float32),
-        PRODUCT,
-        DMA((5,)),
+        pltpu.VMEM((2, HALF, HALF), jnp.float32),
+        DMA((2 * WIDE // DEEP, 5)),
     ]
-    specs = [ANY] * 5 + [INSIDE]
-    return call(ref_late_kernel, operands, floats(8, HALF), INSIDE, scratch, 128, specs)
-
-
-def late_call(table, fars, heads, totals, info):
-    operands = (table, *fars, *heads, *totals, info)
-    shapes = (*TOTALS, floats(8, HALF))
-    scratch = [pltpu.VMEM((2, 128, WIDE), jnp.bfloat16), PRODUCT, DMA((2,))]
-    specs = [ANY] * 2 + [INSIDE] * 5
-    return call(late_kernel, operands, shapes, (INSIDE,) * 3, scratch, 256, specs)
+    specs = [ANY] * 6 + [INSIDE]
+    return call(ref_kernel, operands, floats(8, HALF), INSIDE, scratch, 512, specs)
 
 
 def grad_call(table, pieces, logits, lses, info):
@@ -332,7 +316,7 @@
     operands = (table, *pieces, *logits, *lses, info)
     specs = [ANY] * 18 + [INSIDE] * 3
     shape = jax.ShapeDtypeStruct((2 * WIDE, HALF), jnp.bfloat16)
-    return call(grad_kernel, operands, shape, ANY, scratch, 1024, specs, 60)
+    return call(grad_kernel, operands, shape, ANY, scratch, 1024, specs)
 
 
 def log_sum(terms, axis):
@@ -379,27 +363,20 @@
     own = ring(own, "xy")
     low, top = fence(stack(own, slice(0, WIDE)), stack(own, slice(WIDE, None)))
 
-    low_near, low_back = send(low, "yx", (1, 1)), send(low, "yx", (-1, -1))
-    top_near, top_back = send(top, "yx", (1, 1)), send(top, "yx", (-1, -1))
-    ref_near, ref_back = fence(ref_near, ref_back)
+    low_near, top_back = send(low, "yx", (1, 1)), send(top, "yx", (-1, -1))
+    low, top, low_near, top_back, ref_near, ref_back = fence(
+        low, top, low_near, top_back, ref_near, ref_back
+    )
+
+    low_far, top_far = send(low_near, "yx", (1, 1)), send(top_back, "yx", (-1, -1))
+    top_near, low_back = send(top, "yx", (1, 1)), send(low, "yx", (-1, -1))
     ref_far = send(ref_near, "zz", (1, -1))
-    ref_totals = ref_call(table, (ref, ref_near, ref_back), ref_heads)
-    low, top, low_near, top_near, low_back, top_back, ref_far, *ref_totals = fence(
-        low, top, low_near, top_near, low_back, top_back, ref_far, *ref_totals
-    )
-
-    low_far, top_far = send(low_near, "yx", (1, 1)), send(top_back, "yx", (-1, -1))
-    pieces = (low, top, low_near, top_near, low_back, top_back)
-    totals = early_call(table, pieces, heads)
-    ref_stats = ref_late_call(table, ref_far, ref_heads, ref_totals, info)
-    near_2 = swap(low_near), swap(top_near)
-    low_back_2 = swap(low_back)
-    low_far, top_far, low_back_2, ref_stats, top_back, low, top, *rest = fence(
-        low_far, top_far, low_back_2, ref_stats, top_back, low, top, *totals, *near_2
-    )
-    totals, near_2 = rest[:2], rest[2:]
-    swapped = [swap(piece) for piece in (low, top, top_back, low_far, top_far)]
-    mine, other, stats = late_call(table, (low_far, top_far), heads, totals, info)
+    ref_stats = ref_call(table, (ref, ref_near, ref_back, ref_far), ref_heads, info)
+    pieces = (low, top, low_near, top_near, low_back, top_back, low_far, top_far)
+    *pieces, ref_stats = fence(*pieces, ref_stats)
+
+    swapped = [swap(piece) for piece in pieces[:5]]
+    mine, other, stats = own_call(table, pieces, heads, info)
 
     rest = jnp.concatenate(
         [ref_stats[0].reshape(64, 8), (stats[1] - ref_stats[1]).reshape(64, 8)], axis=1
@@ -409,7 +386,7 @@
         [jnp.broadcast_to(stats[0].reshape(1, 4, 128), (64, 4, 128)), rest[:, None]], axis=1
     )
     message, other, *swapped = fence(message, other, *swapped)
-    low_2, top_2, top_back_2, low_far_2, top_far_2 = swapped
+    swapped += [swap(piece) for piece in pieces[5:]]
     arrived = lax.all_to_all(message, CHIPS, 0, 0, tiled=True)
     other_2 = swap(other)
     lse = log_sum(arrived[:, :4], 0)
@@ -418,10 +395,8 @@
     hits = jnp.sum(arrived[:, 4, 8:16], axis=0)
     excess = lax.dynamic_slice_in_dim(lse.reshape(HALF), 8 * chip, 8) - found - hits
 
-    pieces = (low, top, low_near, top_near, low_back, top_back, low_far, top_far)
-    pieces += (low_2, top_2, *near_2, low_back_2, top_back_2, low_far_2, top_far_2)
     both = jnp.concatenate([info, info_2], axis=1)
-    head_grad = grad_call(table, pieces, (mine, other_2), (lse, lse_2), both)
+    head_grad = grad_call(table, (*pieces, *swapped), (mine, other_2), (lse, lse_2), both)
     return excess, head_grad
 
 

time: 160 us -> 153 us (0.956)
  waiting for transfers between devices: 35.9 us -> 49.2 us
  Pallas kernels: 49.9 us -> 39.5 us
  local copies, waits for them, and re-layouts: 17.4 us -> 7.75 us
    ppermute x18, waiting for transfers between devices: 25.5 us -> 39.5 us  [send(): return lax.ppermute(values, ALL, pairs)]
    pallas_call x5 -> x3, Pallas kernels: 49.9 us -> 39.5 us  [call(): pl.pallas_call(kernel, out_shape=out_shape, in_specs=[TABLE, *specs], out...]
    unnamed x43 -> x39, local copies, waits for them, and re-layouts: 13.7 us -> 4 us
  transfers between devices with their start and end apart: 32 -> 32, of which waited for: 10 -> 12; matrix products, arithmetic and copies ran while one was open for 7% -> 8% of each run, Pallas kernels for 21% -> 15%
where the time goes in v4:
time: 153 us; the launch traced here: 152 us
  waiting for transfers between devices  49.2 us (32%)
  starting transfers between devices  46.6 us (30%)
  Pallas kernels  39.5 us (26%)
  other arithmetic  7.84 us (5%)
  local copies, waits for them, and re-layouts  7.75 us (5%)
    pallas_call x3, Pallas kernels, call(): pl.pallas_call(kernel, out_shape=out_shape, in_specs=[TABLE, *specs], out...  39.5 us
    ppermute x18, waiting for transfers between devices, send(): return lax.ppermute(values, ALL, pairs)  39.5 us
    ppermute x18, starting transfers between devices, send(): return lax.ppermute(values, ALL, pairs)  23.5 us
    ppermute x12, starting transfers between devices, swap(): lax.ppermute(values, ALL, [(index, index ^ 1) for index in range(128)])  11.1 us
    all_to_all x1, waiting for transfers between devices, shards(): arrived = lax.all_to_all(message, CHIPS, 0, 0, tiled=True)  8.19 us
    all_to_all x1, starting transfers between devices, shards(): lax.all_to_all(raw, ('zl', 'zh', 'c'), 0, 0, tiled=True)  7.32 us
    all_to_all x1, starting transfers between devices, shards(): arrived = lax.all_to_all(message, CHIPS, 0, 0, tiled=True)  4.75 us
    unnamed x39, local copies, waits for them, and re-layouts  4 us
  transfers between devices with their start and end apart: 32, of which 12 were waited for; matrix products, arithmetic and copies ran while one was open for 8% of the time, Pallas kernels for 15%

profile of v4, /device:TPU:1, one launch (start us, length us, event | category | flops | bytes accessed | tf_op | source)
XLA Modules:
  0.0 152.2 jit_solution(16463088202400247700)
XLA Ops:
  0.6 1.5 collective-permute-start.6
  2.1 0.9 copy.59
  3.0 1.0 fusion
  4.0 0.9 fusion.2
  5.0 0.9 broadcast_in_dim.87
  5.9 3.0 %collective-permute-start.2 = (bf16[8,4096]{1,0:T(8,128)(2,1)S(1)}, bf16[8,4096]{1,0:T(8,128)(2,1)S(1)}, u32[]{:S(2)}, u32[]{:S(2)}) collective-permute-start(bf16[8,4096]{1,0:T(8,128)(2,1)S(1)} %fusion.2), channel_id=1, source_target_pairs={{0,8},{1,65},{2,10},{3,67},{4,12},{5,69},{6,14},{7,71},{8,0},{9,73... | collective-permute-start | bytes 196616 | tf_op jit(solution)/shard_map/ppermute | solution.py:39
  8.9 0.8 collective-permute-start.1
  9.6 0.7 collective-permute-start
  10.3 0.7 collective-permute-start.7
  11.0 2.9 %collective-permute-done = bf16[8,4096]{1,0:T(8,128)(2,1)S(1)} collective-permute-done((bf16[8,4096]{1,0:T(8,128)(2,1)S(1)}, bf16[8,4096]{1,0:T(8,128)(2,1)S(1)}, u32[]{:S(2)}, u32[]{:S(2)}) %collective-permute-start) | collective-permute-done | bytes 65568 | tf_op jit(solution)/shard_map/ppermute | solution.py:39
  14.0 1.3 collective-permute-start.3
  15.3 7.3 %all-to-all-start = ((bf16[8,16,2048]{2,1,0:T(8,128)(2,1)}), bf16[8,16,2048]{2,1,0:T(8,128)(2,1)S(1)}, u32[]{:S(2)}, u32[]{:S(2)}) async-start(bf16[8,16,2048]{2,1,0:T(8,128)(2,1)} %bitcast.3), calls=%async_computation | async-start | bytes 1048576 | tf_op jit(solution)/shard_map/all_to_all | solution.py:355
  22.6 0.6 collective-permute-start.5
  23.2 1.2 collective-permute-start.4
  24.5 5.3 %collective-permute-done.4 = bf16[32,4096]{1,0:T(8,128)(2,1)S(1)} collective-permute-done((bf16[32,4096]{1,0:T(8,128)(2,1)S(1)}, bf16[32,4096]{1,0:T(8,128)(2,1)S(1)}, u32[]{:S(2)}, u32[]{:S(2)}) %collective-permute-start.4) | collective-permute-done | bytes 262176 | tf_op jit(solution)/shard_map/ppermute | solution.py:39
  29.8 1.5 %all-to-all-done = bf16[8,16,2048]{2,1,0:T(8,128)(2,1)S(1)} async-done(((bf16[8,16,2048]{2,1,0:T(8,128)(2,1)}), bf16[8,16,2048]{2,1,0:T(8,128)(2,1)S(1)}, u32[]{:S(2)}, u32[]{:S(2)}) %all-to-all-start) | async-done | bytes 524320 | tf_op jit(solution)/shard_map/all_to_all | solution.py:355
  31.4 0.2 multiply_reduce_fusion
  31.8 0.7 copy.46
  32.5 0.6 copy.57
  33.1 0.2 multiply_convert_fusion
  33.3 2.7 %collective-permute-start.10 = (bf16[32,8192]{1,0:T(8,128)(2,1)S(1)}, bf16[32,8192]{1,0:T(8,128)(2,1)S(1)}, u32[]{:S(2)}, u32[]{:S(2)}) collective-permute-start(bf16[32,8192]{1,0:T(8,128)(2,1)S(1)} %multiply_convert_fusion), channel_id=1, source_target_pairs={{0,8},{1,65},{2,10},{3,67},{4,12},{5,69},{6,14},{7,71},{8,0},{9,73... | collective-permute-start | bytes 1572872 | tf_op jit(solution)/shard_map/ppermute | solution.py:39
  36.0 1.1 collective-permute-start.9
  37.1 0.4 collective-permute-start.8
  37.5 2.7 %collective-permute-start.13 = (bf16[128,4096]{1,0:T(8,128)(2,1)S(1)}, bf16[128,4096]{1,0:T(8,128)(2,1)}, u32[]{:S(2)}, u32[]{:S(2)}) collective-permute-start(bf16[128,4096]{1,0:T(8,128)(2,1)S(1)} %constant_dynamic-update-slice_fusion.4.refs_0_), channel_id=1, source_target_pairs={{0,16},{1,19},{2,18},{3,17},{4,20},{5,23},{6,22},{7,21},{8,24},{9,... | collective-permute-start | bytes 3145736 | tf_op jit(solution)/shard_map/ppermute | solution.py:39
  40.2 3.1 %collective-permute-done.10 = bf16[32,8192]{1,0:T(8,128)(2,1)S(1)} collective-permute-done((bf16[32,8192]{1,0:T(8,128)(2,1)S(1)}, bf16[32,8192]{1,0:T(8,128)(2,1)S(1)}, u32[]{:S(2)}, u32[]{:S(2)}) %collective-permute-start.10) | collective-permute-done | bytes 524320 | tf_op jit(solution)/shard_map/ppermute | solution.py:39
  43.3 4.7 %collective-permute-done.9 = bf16[32,8192]{1,0:T(8,128)(2,1)S(1)} collective-permute-done((bf16[32,8192]{1,0:T(8,128)(2,1)S(1)}, bf16[32,8192]{1,0:T(8,128)(2,1)S(1)}, u32[]{:S(2)}, u32[]{:S(2)}) %collective-permute-start.9) | collective-permute-done | bytes 524320 | tf_op jit(solution)/shard_map/ppermute | solution.py:39
  48.0 0.9 collective-permute-done.8
  49.2 0.5 collective-permute-start.11
  49.7 2.3 %collective-permute-start.12 = (bf16[128,4096]{1,0:T(8,128)(2,1)S(1)}, bf16[128,4096]{1,0:T(8,128)(2,1)S(1)}, u32[]{:S(2)}, u32[]{:S(2)}) collective-permute-start(bf16[128,4096]{1,0:T(8,128)(2,1)S(1)} %get-tuple-element.49.refs_1_), channel_id=1, source_target_pairs={{0,96},{1,13},{2,98},{3,15},{4,100},{5,1},{6,102},{7,3},{8,104},{9... | collective-permute-start | bytes 3145736 | tf_op jit(solution)/shard_map/ppermute | solution.py:39
  51.9 9.0 %collective-permute-done.14.refs_2_ = bf16[128,4096]{1,0:T(8,128)(2,1)S(1)} collective-permute-done((bf16[128,4096]{1,0:T(8,128)(2,1)S(1)}, bf16[128,4096]{1,0:T(8,128)(2,1)S(1)}, u32[]{:S(2)}, u32[]{:S(2)}) %collective-permute-start.14) | collective-permute-done | bytes 1048608 | tf_op jit(solution)/shard_map/ppermute | solution.py:39
  60.9 2.2 %collective-permute-done.13.refs_1_ = bf16[128,4096]{1,0:T(8,128)(2,1)} collective-permute-done((bf16[128,4096]{1,0:T(8,128)(2,1)S(1)}, bf16[128,4096]{1,0:T(8,128)(2,1)}, u32[]{:S(2)}, u32[]{:S(2)}) %collective-permute-start.13) | collective-permute-done | bytes 1048608 | tf_op jit(solution)/shard_map/ppermute | solution.py:39
  63.1 1.3 collective-permute-done.11.refs_2_
  64.4 1.0 copy-done.8
  65.4 2.1 %collective-permute-start.19 = (bf16[128,4096]{1,0:T(8,128)(2,1)}, bf16[128,4096]{1,0:T(8,128)(2,1)S(1)}, u32[]{:S(2)}, u32[]{:S(2)}) collective-permute-start(bf16[128,4096]{1,0:T(8,128)(2,1)} %collective-permute-done.13.refs_1_), channel_id=1, source_target_pairs={{0,16},{1,19},{2,18},{3,17},{4,20},{5,23},{6,22},{7,21},{8,24},{9,... | collective-permute-start | bytes 3145736 | tf_op jit(solution)/shard_map/ppermute | solution.py:39
  67.9 0.6 collective-permute-start.16
  68.5 0.9 collective-permute-start.15
  69.4 0.2 collective-permute-start.17
  69.7 2.5 %collective-permute-start.18 = (bf16[128,4096]{1,0:T(8,128)(2,1)}, bf16[128,4096]{1,0:T(8,128)(2,1)}, u32[]{:S(2)}, u32[]{:S(2)}) collective-permute-start(bf16[128,4096]{1,0:T(8,128)(2,1)} %copy-done.10), channel_id=1, source_target_pairs={{0,96},{1,13},{2,98},{3,15},{4,100},{5,1},{6,102},{7,3},{8,104},{9... | collective-permute-start | bytes 3145736 | tf_op jit(solution)/shard_map/ppermute | solution.py:39
  72.1 0.4 fusion.4
  72.9 0.2 convert_reduce_fusion.3
  73.3 0.6 add_multiply_fusion.table
  73.9 0.7 select_select_fusion
  74.6 5.1 %collective-permute-done.19.refs_3_ = bf16[128,4096]{1,0:T(8,128)(2,1)S(1)} collective-permute-done((bf16[128,4096]{1,0:T(8,128)(2,1)}, bf16[128,4096]{1,0:T(8,128)(2,1)S(1)}, u32[]{:S(2)}, u32[]{:S(2)}) %collective-permute-start.19) | collective-permute-done | bytes 1048608 | tf_op jit(solution)/shard_map/ppermute | solution.py:39
  79.6 1.0 copy-done.12
  80.6 9.4 %shard_map.95 = f32[8,512]{1,0:T(8,128)} custom-call(s32[256]{0:T(256)} %add_multiply_fusion.table, bf16[128,4096]{1,0:T(8,128)(2,1)} %copy-done.4, bf16[128,4096]{1,0:T(8,128)(2,1)} %collective-permute-done.13.refs_1_, bf16[128,4096]{1,0:T(8,128)(2,1)} %copy-done.11, bf16[128,4096]{1,0:T(8,128)(2,1)} %copy-done.12, bf16[4096,512]{1,0:T(8,128)(2,1)} %refs_4_.1, ...), custom_call_target="tpu_custom_call" | custom-call | flops 4294967296 | bytes 12582912 | tf_op jit(solution)/shard_map/pallas_call | solution.py:264
  90.0 5.0 %collective-permute-done.17.refs_6_ = bf16[128,4096]{1,0:T(8,128)(2,1)} collective-permute-done((bf16[128,4096]{1,0:T(8,128)(2,1)}, bf16[128,4096]{1,0:T(8,128)(2,1)}, u32[]{:S(2)}, u32[]{:S(2)}) %collective-permute-start.17) | collective-permute-done | bytes 1048608 | tf_op jit(solution)/shard_map/ppermute | solution.py:39
  95.0 5.1 %collective-permute-start.20 = (bf16[128,4096]{1,0:T(8,128)(2,1)S(1)}, bf16[128,4096]{1,0:T(8,128)(2,1)}, u32[]{:S(2)}, u32[]{:S(2)}) collective-permute-start(bf16[128,4096]{1,0:T(8,128)(2,1)S(1)} %get-tuple-element.48.refs_0_), channel_id=1, source_target_pairs={{0,1},{1,0},{2,3},{3,2},{4,5},{5,4},{6,7},{7,6},{8,9},{9,8},{10,11... | collective-permute-start | bytes 3145736 | tf_op jit(solution)/shard_map/ppermute | solution.py:43
  100.2 0.4 collective-permute-start.22
  100.7 0.4 collective-permute-start.24
  101.1 14.0 %shard_map.96 = (f32[512,512]{1,0:T(8,128)}, f32[512,512]{1,0:T(8,128)}, f32[8,512]{1,0:T(8,128)}) custom-call(s32[256]{0:T(256)} %add_multiply_fusion.table, bf16[128,4096]{1,0:T(8,128)(2,1)} %copy-done, bf16[128,4096]{1,0:T(8,128)(2,1)} %copy-done.1, bf16[128,4096]{1,0:T(8,128)(2,1)} %copy-done.8, bf16[128,4096]{1,0:T(8,128)(2,1)} %collective-permute-done.15.refs_3_, ...), custom_call_target="tpu_custom_call" | custom-call | flops 8589934592 | bytes 12582912 | tf_op jit(solution)/shard_map/pallas_call | solution.py:264
  115.1 0.8 slice_reduce_fusion.2
  116.2 0.8 pad_maximum_fusion.2
  117.0 4.7 %all-to-all-start.1 = ((f32[64,5,128]{2,1,0:T(8,128)}), f32[64,5,128]{2,1,0:T(8,128)S(1)}, u32[]{:S(2)}, u32[]{:S(2)}) async-start(f32[64,5,128]{2,1,0:T(8,128)} %pad_maximum_fusion.2), calls=%async_computation.1 | async-start | bytes 524288 | tf_op jit(solution)/shard_map/all_to_all | solution.py:390
  121.8 0.7 collective-permute-start.25
  122.6 0.4 collective-permute-start.27
  123.1 0.6 pad_maximum_fusion.3.refs_20_
  123.7 8.2 %all-to-all-done.1 = f32[64,5,128]{2,1,0:T(8,128)S(1)} async-done(((f32[64,5,128]{2,1,0:T(8,128)}), f32[64,5,128]{2,1,0:T(8,128)S(1)}, u32[]{:S(2)}, u32[]{:S(2)}) %all-to-all-start.1) | async-done | bytes 163872 | tf_op jit(solution)/shard_map/all_to_all | solution.py:390
  131.9 0.2 slice_reduce_fusion.3
  132.3 1.4 collective-permute-start.29
  133.7 0.2 fusion.6
  133.9 0.6 subtract_subtract_fusion
  134.6 0.9 copy-done.13
  135.5 0.3 copy-done.14
  135.8 16.1 %shard_map.97 = bf16[8192,512]{1,0:T(8,128)(2,1)} custom-call(s32[256]{0:T(256)} %add_multiply_fusion.table, bf16[128,4096]{1,0:T(8,128)(2,1)} %copy-done, bf16[128,4096]{1,0:T(8,128)(2,1)} %copy-done.1, bf16[128,4096]{1,0:T(8,128)(2,1)} %copy-done.8, bf16[128,4096]{1,0:T(8,128)(2,1)} %collective-permute-done.15.refs_3_, ...), custom_call_target="tpu_custom_call" | custom-call | flops 8589934592 | bytes 12582912 | tf_op jit(solution)/shard_map/pallas_call | solution.py:264
  (89 shorter events, 2.6 us)
Async XLA Ops:
  0.6 32.7 %collective-permute-start.6 = (bf16[8192,512]{1,0:T(8,128)(2,1)}, bf16[8192,512]{1,0:T(8,128)(2,1)}, u32[]{:S(2)}, u32[]{:S(2)}) collective-permute-start(bf16[8192,512]{1,0:T(8,128)(2,1)} %refs_8_.1), channel_id=1, source_target_pairs={{0,1},{1,0},{2,3},{3,2},{4,5},{5,4},{6,7},{7,6},{8,9},{9,8},{10,11... | collective-permute-start | bytes 25165832 | tf_op jit(solution)/shard_map/ppermute | solution.py:43
  5.9 8.1 %collective-permute-start.2 = (bf16[8,4096]{1,0:T(8,128)(2,1)S(1)}, bf16[8,4096]{1,0:T(8,128)(2,1)S(1)}, u32[]{:S(2)}, u32[]{:S(2)}) collective-permute-start(bf16[8,4096]{1,0:T(8,128)(2,1)S(1)} %fusion.2), channel_id=1, source_target_pairs={{0,8},{1,65},{2,10},{3,67},{4,12},{5,69},{6,14},{7,71},{8,0},{9,73... | collective-permute-start | bytes 196616 | tf_op jit(solution)/shard_map/ppermute | solution.py:39
  8.9 5.1 %collective-permute-start.1 = (bf16[8,4096]{1,0:T(8,128)(2,1)S(1)}, bf16[8,4096]{1,0:T(8,128)(2,1)S(1)}, u32[]{:S(2)}, u32[]{:S(2)}) collective-permute-start(bf16[8,4096]{1,0:T(8,128)(2,1)S(1)} %fusion.2), channel_id=1, source_target_pairs={{0,12},{1,97},{2,14},{3,99},{4,0},{5,101},{6,2},{7,103},{8,4},{9,1... | collective-permute-start | bytes 196616 | tf_op jit(solution)/shard_map/ppermute | solution.py:39
  9.6 4.3 %collective-permute-start = (bf16[8,4096]{1,0:T(8,128)(2,1)S(1)}, bf16[8,4096]{1,0:T(8,128)(2,1)S(1)}, u32[]{:S(2)}, u32[]{:S(2)}) collective-permute-start(bf16[8,4096]{1,0:T(8,128)(2,1)S(1)} %fusion.2), channel_id=1, source_target_pairs={{0,4},{1,33},{2,6},{3,35},{4,8},{5,37},{6,10},{7,39},{8,12},{9,41}... | collective-permute-start | bytes 196616 | tf_op jit(solution)/shard_map/ppermute | solution.py:39
  10.3 22.9 %collective-permute-start.7 = (bf16[4096,512]{1,0:T(8,128)(2,1)}, bf16[4096,512]{1,0:T(8,128)(2,1)}, u32[]{:S(2)}, u32[]{:S(2)}) collective-permute-start(bf16[4096,512]{1,0:T(8,128)(2,1)} %refs_4_.1), channel_id=1, source_target_pairs={{0,1},{1,0},{2,3},{3,2},{4,5},{5,4},{6,7},{7,6},{8,9},{9,8},{10,11... | collective-permute-start | bytes 12582920 | tf_op jit(solution)/shard_map/ppermute | solution.py:43
  14.0 10.4 %collective-permute-start.3 = (bf16[32,4096]{1,0:T(8,128)(2,1)S(1)}, bf16[32,4096]{1,0:T(8,128)(2,1)S(1)}, u32[]{:S(2)}, u32[]{:S(2)}) collective-permute-start(bf16[32,4096]{1,0:T(8,128)(2,1)S(1)} %get-tuple-element.89), channel_id=1, source_target_pairs={{0,32},{1,5},{2,34},{3,7},{4,36},{5,9},{6,38},{7,11},{8,40},{9,13}... | collective-permute-start | bytes 786440 | tf_op jit(solution)/shard_map/ppermute | solution.py:39
  15.3 16.1 %all-to-all-start = ((bf16[8,16,2048]{2,1,0:T(8,128)(2,1)}), bf16[8,16,2048]{2,1,0:T(8,128)(2,1)S(1)}, u32[]{:S(2)}, u32[]{:S(2)}) async-start(bf16[8,16,2048]{2,1,0:T(8,128)(2,1)} %bitcast.3), calls=%async_computation | async-start | bytes 1048576 | tf_op jit(solution)/shard_map/all_to_all | solution.py:355
  22.6 7.2 %collective-permute-start.5 = (bf16[32,4096]{1,0:T(8,128)(2,1)S(1)}, bf16[32,4096]{1,0:T(8,128)(2,1)S(1)}, u32[]{:S(2)}, u32[]{:S(2)}) collective-permute-start(bf16[32,4096]{1,0:T(8,128)(2,1)S(1)} %get-tuple-element.89), channel_id=1, source_target_pairs={{0,64},{1,9},{2,66},{3,11},{4,68},{5,13},{6,70},{7,15},{8,72},{9,1... | collective-permute-start | bytes 786440 | tf_op jit(solution)/shard_map/ppermute | solution.py:39
  23.2 6.6 %collective-permute-start.4 = (bf16[32,4096]{1,0:T(8,128)(2,1)S(1)}, bf16[32,4096]{1,0:T(8,128)(2,1)S(1)}, u32[]{:S(2)}, u32[]{:S(2)}) collective-permute-start(bf16[32,4096]{1,0:T(8,128)(2,1)S(1)} %get-tuple-element.89), channel_id=1, source_target_pairs={{0,96},{1,13},{2,98},{3,15},{4,100},{5,1},{6,102},{7,3},{8,104},{9... | collective-permute-start | bytes 786440 | tf_op jit(solution)/shard_map/ppermute | solution.py:39
  29.8 7.6 %copy-start.4 = (bf16[128,4096]{1,0:T(8,128)(2,1)}, bf16[128,4096]{1,0:T(8,128)(2,1)S(1)}, u32[]{:S(2)}) copy-start(bf16[128,4096]{1,0:T(8,128)(2,1)S(1)} %constant_dynamic-update-slice_fusion.4.refs_0_) | copy-start | bytes 3145732
  31.8 1.3 copy-start.3
  33.3 10.0 %collective-permute-start.10 = (bf16[32,8192]{1,0:T(8,128)(2,1)S(1)}, bf16[32,8192]{1,0:T(8,128)(2,1)S(1)}, u32[]{:S(2)}, u32[]{:S(2)}) collective-permute-start(bf16[32,8192]{1,0:T(8,128)(2,1)S(1)} %multiply_convert_fusion), channel_id=1, source_target_pairs={{0,8},{1,65},{2,10},{3,67},{4,12},{5,69},{6,14},{7,71},{8,0},{9,73... | collective-permute-start | bytes 1572872 | tf_op jit(solution)/shard_map/ppermute | solution.py:39
  36.0 12.0 %collective-permute-start.9 = (bf16[32,8192]{1,0:T(8,128)(2,1)S(1)}, bf16[32,8192]{1,0:T(8,128)(2,1)S(1)}, u32[]{:S(2)}, u32[]{:S(2)}) collective-permute-start(bf16[32,8192]{1,0:T(8,128)(2,1)S(1)} %multiply_convert_fusion), channel_id=1, source_target_pairs={{0,12},{1,97},{2,14},{3,99},{4,0},{5,101},{6,2},{7,103},{8,4},{9,1... | collective-permute-start | bytes 1572872 | tf_op jit(solution)/shard_map/ppermute | solution.py:39
  37.1 11.9 %collective-permute-start.8 = (bf16[32,8192]{1,0:T(8,128)(2,1)S(1)}, bf16[32,8192]{1,0:T(8,128)(2,1)S(1)}, u32[]{:S(2)}, u32[]{:S(2)}) collective-permute-start(bf16[32,8192]{1,0:T(8,128)(2,1)S(1)} %multiply_convert_fusion), channel_id=1, source_target_pairs={{0,4},{1,33},{2,6},{3,35},{4,8},{5,37},{6,10},{7,39},{8,12},{9,41}... | collective-permute-start | bytes 1572872 | tf_op jit(solution)/shard_map/ppermute | solution.py:39
  37.5 23.4 %collective-permute-start.14 = (bf16[128,4096]{1,0:T(8,128)(2,1)S(1)}, bf16[128,4096]{1,0:T(8,128)(2,1)S(1)}, u32[]{:S(2)}, u32[]{:S(2)}) collective-permute-start(bf16[128,4096]{1,0:T(8,128)(2,1)S(1)} %constant_dynamic-update-slice_fusion.4.refs_0_), channel_id=1, source_target_pairs={{0,18},{1,17},{2,16},{3,19},{4,22},{5,21},{6,20},{7,23},{8,26},{9,... | collective-permute-start | bytes 3145736 | tf_op jit(solution)/shard_map/ppermute | solution.py:39
  37.5 25.6 %collective-permute-start.13 = (bf16[128,4096]{1,0:T(8,128)(2,1)S(1)}, bf16[128,4096]{1,0:T(8,128)(2,1)}, u32[]{:S(2)}, u32[]{:S(2)}) collective-permute-start(bf16[128,4096]{1,0:T(8,128)(2,1)S(1)} %constant_dynamic-update-slice_fusion.4.refs_0_), channel_id=1, source_target_pairs={{0,16},{1,19},{2,18},{3,17},{4,20},{5,23},{6,22},{7,21},{8,24},{9,... | collective-permute-start | bytes 3145736 | tf_op jit(solution)/shard_map/ppermute | solution.py:39
  49.0 18.5 %copy-start.6 = (s32[1024]{0:T(1024)S(1)}, s32[1024]{0:T(1024)}, u32[]{:S(2)}) copy-start(s32[1024]{0:T(1024)} %param.15) | copy-start | bytes 12292
  49.0 18.7 %copy-start.5 = (s32[1024]{0:T(1024)S(1)}, s32[1024]{0:T(1024)}, u32[]{:S(2)}) copy-start(s32[1024]{0:T(1024)} %param.14) | copy-start | bytes 12292
  49.1 45.9 %copy-start = (bf16[128,4096]{1,0:T(8,128)(2,1)}, bf16[128,4096]{1,0:T(8,128)(2,1)S(1)}, u32[]{:S(2)}) copy-start(bf16[128,4096]{1,0:T(8,128)(2,1)S(1)} %get-tuple-element.48.refs_0_) | copy-start | bytes 3145732
  49.2 50.9 %copy-start.1 = (bf16[128,4096]{1,0:T(8,128)(2,1)}, bf16[128,4096]{1,0:T(8,128)(2,1)S(1)}, u32[]{:S(2)}) copy-start(bf16[128,4096]{1,0:T(8,128)(2,1)S(1)} %get-tuple-element.49.refs_1_) | copy-start | bytes 3145732
  49.2 15.2 %collective-permute-start.11 = (bf16[128,4096]{1,0:T(8,128)(2,1)S(1)}, bf16[128,4096]{1,0:T(8,128)(2,1)S(1)}, u32[]{:S(2)}, u32[]{:S(2)}) collective-permute-start(bf16[128,4096]{1,0:T(8,128)(2,1)S(1)} %get-tuple-element.48.refs_0_), channel_id=1, source_target_pairs={{0,32},{1,5},{2,34},{3,7},{4,36},{5,9},{6,38},{7,11},{8,40},{9,13}... | collective-permute-start | bytes 3145736 | tf_op jit(solution)/shard_map/ppermute | solution.py:39
  49.7 14.7 %collective-permute-start.12 = (bf16[128,4096]{1,0:T(8,128)(2,1)S(1)}, bf16[128,4096]{1,0:T(8,128)(2,1)S(1)}, u32[]{:S(2)}, u32[]{:S(2)}) collective-permute-start(bf16[128,4096]{1,0:T(8,128)(2,1)S(1)} %get-tuple-element.49.refs_1_), channel_id=1, source_target_pairs={{0,96},{1,13},{2,98},{3,15},{4,100},{5,1},{6,102},{7,3},{8,104},{9... | collective-permute-start | bytes 3145736 | tf_op jit(solution)/shard_map/ppermute | solution.py:39
  60.9 6.6 %copy-start.11 = (bf16[128,4096]{1,0:T(8,128)(2,1)}, bf16[128,4096]{1,0:T(8,128)(2,1)S(1)}, u32[]{:S(2)}) copy-start(bf16[128,4096]{1,0:T(8,128)(2,1)S(1)} %collective-permute-done.14.refs_2_) | copy-start | bytes 3145732
  64.4 1.0 copy-start.8
  65.4 2.1 %copy-start.10 = (bf16[128,4096]{1,0:T(8,128)(2,1)}, bf16[128,4096]{1,0:T(8,128)(2,1)S(1)}, u32[]{:S(2)}) copy-start(bf16[128,4096]{1,0:T(8,128)(2,1)S(1)} %collective-permute-done.12.refs_5_) | copy-start | bytes 3145732
  65.4 14.3 %collective-permute-start.19 = (bf16[128,4096]{1,0:T(8,128)(2,1)}, bf16[128,4096]{1,0:T(8,128)(2,1)S(1)}, u32[]{:S(2)}, u32[]{:S(2)}) collective-permute-start(bf16[128,4096]{1,0:T(8,128)(2,1)} %collective-permute-done.13.refs_1_), channel_id=1, source_target_pairs={{0,16},{1,19},{2,18},{3,17},{4,20},{5,23},{6,22},{7,21},{8,24},{9,... | collective-permute-start | bytes 3145736 | tf_op jit(solution)/shard_map/ppermute | solution.py:39
  67.9 22.1 %collective-permute-start.16 = (bf16[128,4096]{1,0:T(8,128)(2,1)S(1)}, bf16[128,4096]{1,0:T(8,128)(2,1)}, u32[]{:S(2)}, u32[]{:S(2)}) collective-permute-start(bf16[128,4096]{1,0:T(8,128)(2,1)S(1)} %get-tuple-element.48.refs_0_), channel_id=1, source_target_pairs={{0,96},{1,13},{2,98},{3,15},{4,100},{5,1},{6,102},{7,3},{8,104},{9... | collective-permute-start | bytes 3145736 | tf_op jit(solution)/shard_map/ppermute | solution.py:39
  68.5 21.5 %collective-permute-start.15 = (bf16[128,4096]{1,0:T(8,128)(2,1)S(1)}, bf16[128,4096]{1,0:T(8,128)(2,1)}, u32[]{:S(2)}, u32[]{:S(2)}) collective-permute-start(bf16[128,4096]{1,0:T(8,128)(2,1)S(1)} %get-tuple-element.49.refs_1_), channel_id=1, source_target_pairs={{0,32},{1,5},{2,34},{3,7},{4,36},{5,9},{6,38},{7,11},{8,40},{9,13}... | collective-permute-start | bytes 3145736 | tf_op jit(solution)/shard_map/ppermute | solution.py:39
  69.4 25.6 %collective-permute-start.17 = (bf16[128,4096]{1,0:T(8,128)(2,1)}, bf16[128,4096]{1,0:T(8,128)(2,1)}, u32[]{:S(2)}, u32[]{:S(2)}) collective-permute-start(bf16[128,4096]{1,0:T(8,128)(2,1)} %copy-done.8), channel_id=1, source_target_pairs={{0,32},{1,5},{2,34},{3,7},{4,36},{5,9},{6,38},{7,11},{8,40},{9,13}... | collective-permute-start | bytes 3145736 | tf_op jit(solution)/shard_map/ppermute | solution.py:39
  69.7 25.3 %collective-permute-start.18 = (bf16[128,4096]{1,0:T(8,128)(2,1)}, bf16[128,4096]{1,0:T(8,128)(2,1)}, u32[]{:S(2)}, u32[]{:S(2)}) collective-permute-start(bf16[128,4096]{1,0:T(8,128)(2,1)} %copy-done.10), channel_id=1, source_target_pairs={{0,96},{1,13},{2,98},{3,15},{4,100},{5,1},{6,102},{7,3},{8,104},{9... | collective-permute-start | bytes 3145736 | tf_op jit(solution)/shard_map/ppermute | solution.py:39
  79.6 1.0 copy-start.12
  80.6 19.6 %copy-start.9 = (bf16[128,4096]{1,0:T(8,128)(2,1)S(1)}, bf16[128,4096]{1,0:T(8,128)(2,1)}, u32[]{:S(2)}) copy-start(bf16[128,4096]{1,0:T(8,128)(2,1)} %copy-done.8) | copy-start | bytes 3145732
  90.0 33.1 %copy-start.2 = (f32[8,512]{1,0:T(8,128)S(1)}, f32[8,512]{1,0:T(8,128)}, u32[]{:S(2)}) copy-start(f32[8,512]{1,0:T(8,128)} %get-tuple-element.99.refs_6_.refs_10_) | copy-start | bytes 49156
  95.0 22.0 %collective-permute-start.20 = (bf16[128,4096]{1,0:T(8,128)(2,1)S(1)}, bf16[128,4096]{1,0:T(8,128)(2,1)}, u32[]{:S(2)}, u32[]{:S(2)}) collective-permute-start(bf16[128,4096]{1,0:T(8,128)(2,1)S(1)} %get-tuple-element.48.refs_0_), channel_id=1, source_target_pairs={{0,1},{1,0},{2,3},{3,2},{4,5},{5,4},{6,7},{7,6},{8,9},{9,8},{10,11... | collective-permute-start | bytes 3145736 | tf_op jit(solution)/shard_map/ppermute | solution.py:43
  100.1 16.9 %collective-permute-start.21 = (bf16[128,4096]{1,0:T(8,128)(2,1)S(1)}, bf16[128,4096]{1,0:T(8,128)(2,1)}, u32[]{:S(2)}, u32[]{:S(2)}) collective-permute-start(bf16[128,4096]{1,0:T(8,128)(2,1)S(1)} %get-tuple-element.49.refs_1_), channel_id=1, source_target_pairs={{0,1},{1,0},{2,3},{3,2},{4,5},{5,4},{6,7},{7,6},{8,9},{9,8},{10,11... | collective-permute-start | bytes 3145736 | tf_op jit(solution)/shard_map/ppermute | solution.py:43
  100.2 16.8 %collective-permute-start.22 = (bf16[128,4096]{1,0:T(8,128)(2,1)S(1)}, bf16[128,4096]{1,0:T(8,128)(2,1)}, u32[]{:S(2)}, u32[]{:S(2)}) collective-permute-start(bf16[128,4096]{1,0:T(8,128)(2,1)S(1)} %copy-done.9), channel_id=1, source_target_pairs={{0,1},{1,0},{2,3},{3,2},{4,5},{5,4},{6,7},{7,6},{8,9},{9,8},{10,11... | collective-permute-start | bytes 3145736 | tf_op jit(solution)/shard_map/ppermute | solution.py:43
  100.6 16.4 %collective-permute-start.23 = (bf16[128,4096]{1,0:T(8,128)(2,1)}, bf16[128,4096]{1,0:T(8,128)(2,1)}, u32[]{:S(2)}, u32[]{:S(2)}) collective-permute-start(bf16[128,4096]{1,0:T(8,128)(2,1)} %collective-permute-done.15.refs_3_), channel_id=1, source_target_pairs={{0,1},{1,0},{2,3},{3,2},{4,5},{5,4},{6,7},{7,6},{8,9},{9,8},{10,11... | collective-permute-start | bytes 3145736 | tf_op jit(solution)/shard_map/ppermute | solution.py:43
  100.7 16.3 %collective-permute-start.24 = (bf16[128,4096]{1,0:T(8,128)(2,1)}, bf16[128,4096]{1,0:T(8,128)(2,1)}, u32[]{:S(2)}, u32[]{:S(2)}) collective-permute-start(bf16[128,4096]{1,0:T(8,128)(2,1)} %collective-permute-done.16.refs_4_), channel_id=1, source_target_pairs={{0,1},{1,0},{2,3},{3,2},{4,5},{5,4},{6,7},{7,6},{8,9},{9,8},{10,11... | collective-permute-start | bytes 3145736 | tf_op jit(solution)/shard_map/ppermute | solution.py:43
  117.0 14.9 %all-to-all-start.1 = ((f32[64,5,128]{2,1,0:T(8,128)}), f32[64,5,128]{2,1,0:T(8,128)S(1)}, u32[]{:S(2)}, u32[]{:S(2)}) async-start(f32[64,5,128]{2,1,0:T(8,128)} %pad_maximum_fusion.2), calls=%async_computation.1 | async-start | bytes 524288 | tf_op jit(solution)/shard_map/all_to_all | solution.py:390
  121.8 12.7 %collective-permute-start.25 = (bf16[128,4096]{1,0:T(8,128)(2,1)}, bf16[128,4096]{1,0:T(8,128)(2,1)S(1)}, u32[]{:S(2)}, u32[]{:S(2)}) collective-permute-start(bf16[128,4096]{1,0:T(8,128)(2,1)} %copy-done.10), channel_id=1, source_target_pairs={{0,1},{1,0},{2,3},{3,2},{4,5},{5,4},{6,7},{7,6},{8,9},{9,8},{10,11... | collective-permute-start | bytes 3145736 | tf_op jit(solution)/shard_map/ppermute | solution.py:43
  122.4 12.1 %collective-permute-start.26 = (bf16[128,4096]{1,0:T(8,128)(2,1)}, bf16[128,4096]{1,0:T(8,128)(2,1)S(1)}, u32[]{:S(2)}, u32[]{:S(2)}) collective-permute-start(bf16[128,4096]{1,0:T(8,128)(2,1)} %collective-permute-done.17.refs_6_), channel_id=1, source_target_pairs={{0,1},{1,0},{2,3},{3,2},{4,5},{5,4},{6,7},{7,6},{8,9},{9,8},{10,11... | collective-permute-start | bytes 3145736 | tf_op jit(solution)/shard_map/ppermute | solution.py:43
  122.6 11.9 %collective-permute-start.27 = (bf16[128,4096]{1,0:T(8,128)(2,1)}, bf16[128,4096]{1,0:T(8,128)(2,1)}, u32[]{:S(2)}, u32[]{:S(2)}) collective-permute-start(bf16[128,4096]{1,0:T(8,128)(2,1)} %collective-permute-done.18.refs_7_), channel_id=1, source_target_pairs={{0,1},{1,0},{2,3},{3,2},{4,5},{5,4},{6,7},{7,6},{8,9},{9,8},{10,11... | collective-permute-start | bytes 3145736 | tf_op jit(solution)/shard_map/ppermute | solution.py:43
  123.0 11.6 %collective-permute-start.28 = (f32[512,512]{1,0:T(8,128)}, f32[512,512]{1,0:T(8,128)}, u32[]{:S(2)}, u32[]{:S(2)}) collective-permute-start(f32[512,512]{1,0:T(8,128)} %get-tuple-element.67), channel_id=1, source_target_pairs={{0,1},{1,0},{2,3},{3,2},{4,5},{5,4},{6,7},{7,6},{8,9},{9,8},{10,11... | collective-permute-start | bytes 3145736 | tf_op jit(solution)/shard_map/ppermute | solution.py:43
  132.3 2.3 %copy-start.7 = (f32[4,128]{1,0:T(4,128)}, f32[4,128]{1,0:T(4,128)S(1)}, u32[]{:S(2)}) copy-start(f32[4,128]{1,0:T(4,128)S(1)} %log_add_fusion.refs_18_) | copy-start | bytes 6148
  132.3 2.2 %collective-permute-start.29 = (f32[4,128]{1,0:T(4,128)S(1)}, f32[4,128]{1,0:T(4,128)S(1)}, u32[]{:S(2)}, u32[]{:S(2)}) collective-permute-start(f32[4,128]{1,0:T(4,128)S(1)} %log_add_fusion.refs_18_), channel_id=1, source_target_pairs={{0,1},{1,0},{2,3},{3,2},{4,5},{5,4},{6,7},{7,6},{8,9},{9,8},{10,11... | collective-permute-start | bytes 6152 | tf_op jit(solution)/shard_map/ppermute | solution.py:43
  134.5 1.0 copy-start.13
  134.5 1.3 copy-start.14
  134.6 1.3 copy-start.15

commit v5 on v4

--- a/solution.py
+++ b/solution.py
@@ -15,6 +15,8 @@
 HALF = 512
 BLOCK = 1024
 DEEP = 2048
+FIRST = 448
+OWN_STEPS = ((0, 1024), (1024, 3072), (4096, 4096))
 MIB = 1 << 20
 
 
@@ -152,16 +154,15 @@
 def own_kernel(table, *refs):
     pieces, (head, head_2, info, mine, other, stats, xbuf, hbuf, tmp, sems) = refs[:8], refs[8:]
     stages = []
-    for step in range(2 * WIDE // DEEP):
-        cut = pl.ds(DEEP * step, DEEP)
-        part, within = DEEP * step // WIDE, pl.ds(DEEP * step % WIDE, DEEP)
+    for first, depth in OWN_STEPS:
+        cut, part, within = pl.ds(first, depth), first // WIDE, pl.ds(first % WIDE, depth)
         sources = [piece.at[:, within] for piece in pieces[part::2]]
         targets = [xbuf.at[pl.ds(128 * k, 128), cut] for k in range(4)]
         stages.append((sources + [head.at[cut, :]], targets + [hbuf.at[0, cut, :]]))
         stages.append(([head_2.at[cut, :]], [hbuf.at[1, cut, :]]))
     stages = Stages(stages, sems)
-    for step in range(2 * WIDE // DEEP):
-        cut = slice(DEEP * step, DEEP * step + DEEP)
+    for step, (first, depth) in enumerate(OWN_STEPS):
+        cut = slice(first, first + depth)
         for side in (0, 1):
             stages.wait(2 * step + side)
             add_product(tmp.at[side], step, xbuf[:, cut], hbuf[side, cut, :])
@@ -171,14 +172,19 @@
 
 
 def ref_kernel(table, *refs):
-    pieces, (head, head_2, info, stats, xbuf, hbuf, tmp, total, sems) = refs[:4], refs[4:]
+    pieces, (head, first_2, head_2, info, stats, xbuf, hbuf, tmp, total, sems) = refs[:4], refs[4:]
     stages = []
     for step in range(WIDE // DEEP):
         cut = pl.ds(DEEP * step, DEEP)
         sources = [piece.at[:, cut] for piece in pieces]
         targets = [xbuf.at[pl.ds(128 * k, 128), cut] for k in range(4)]
         stages.append((sources + [head.at[cut, :]], targets + [hbuf.at[0, cut, :]]))
-        stages.append(([head_2.at[cut, :]], [hbuf.at[1, cut, :]]))
+        sources, targets = [head_2.at[cut, :]], [hbuf.at[1, cut, :]]
+        if step == 0:
+            rest = pl.ds(FIRST, DEEP - FIRST)
+            sources = [first_2, head_2.at[rest, :]]
+            targets = [hbuf.at[1, pl.ds(0, FIRST), :], hbuf.at[1, rest, :]]
+        stages.append((sources, targets))
     stages = Stages(stages, sems)
     for step in range(WIDE // DEEP):
         cut = slice(DEEP * step, DEEP * step + DEEP)
@@ -260,14 +266,14 @@
     return jax.ShapeDtypeStruct(shape, jnp.float32)
 
 
-def call(kernel, operands, out_shape, out_specs, scratch, rows, specs):
+def call(kernel, operands, out_shape, out_specs, scratch, rows, specs, limit=60):
     return pl.pallas_call(
         kernel,
         out_shape=out_shape,
         in_specs=[TABLE, *specs],
         out_specs=out_specs,
         scratch_shapes=scratch,
-        compiler_params=pltpu.CompilerParams(vmem_limit_bytes=60 * MIB),
+        compiler_params=pltpu.CompilerParams(vmem_limit_bytes=limit * MIB),
         cost_estimate=pl.CostEstimate(
             flops=4 * rows * HALF * WIDE, bytes_accessed=12 * MIB, transcendentals=0
         ),
@@ -284,7 +290,7 @@
         pltpu.VMEM((HALF, 2 * WIDE), jnp.bfloat16),
         pltpu.VMEM((2, 2 * WIDE, HALF), jnp.bfloat16),
         pltpu.VMEM((2, HALF, HALF), jnp.float32),
-        DMA((4 * WIDE // DEEP, 5)),
+        DMA((2 * len(OWN_STEPS), 5)),
     ]
     specs = [ANY] * 10 + [INSIDE]
     return call(own_kernel, operands, shapes, (INSIDE,) * 3, scratch, 1024, specs)
@@ -299,7 +305,7 @@
         pltpu.VMEM((2, HALF, HALF), jnp.float32),
         DMA((2 * WIDE // DEEP, 5)),
     ]
-    specs = [ANY] * 6 + [INSIDE]
+    specs = [ANY] * 7 + [INSIDE]
     return call(ref_kernel, operands, floats(8, HALF), INSIDE, scratch, 512, specs)
 
 
@@ -316,7 +322,7 @@
     operands = (table, *pieces, *logits, *lses, info)
     specs = [ANY] * 18 + [INSIDE] * 3
     shape = jax.ShapeDtypeStruct((2 * WIDE, HALF), jnp.bfloat16)
-    return call(grad_kernel, operands, shape, ANY, scratch, 1024, specs)
+    return call(grad_kernel, operands, shape, ANY, scratch, 1024, specs, 58)
 
 
 def log_sum(terms, axis):
@@ -354,10 +360,11 @@
     raw, ref = fence(raw, normalize(ref_rows, ref_gain))
     raw = lax.all_to_all(raw, ("zl", "zh", "c"), 0, 0, tiled=True).reshape(2, 4, 16, 2048)
     own = normalize(raw.transpose(0, 2, 1, 3).reshape(32, 2 * WIDE), trainee_gain)
-    ref = stack(ring(stack(ring(ref, "xy")), "yx"))
+    ref, first_2 = fence(stack(ring(ref, "xy")), swap(ref_head[:FIRST]))
+    ref = stack(ring(ref, "yx"))
     head_2, ref_head_2 = swap(trainee_head), swap(ref_head)
     own, ref, head_2, ref_head_2 = fence(own, ref, head_2, ref_head_2)
-    heads, ref_heads = (trainee_head, head_2), (ref_head, ref_head_2)
+    heads, ref_heads = (trainee_head, head_2), (ref_head, first_2, ref_head_2)
 
     ref_near, ref_back = send(ref, "zz", (1, -1)), send(ref, "zz", (-1, 1))
     own = ring(own, "xy")
@@ -378,22 +385,19 @@
     swapped = [swap(piece) for piece in pieces[:5]]
     mine, other, stats = own_call(table, pieces, heads, info)
 
-    rest = jnp.concatenate(
-        [ref_stats[0].reshape(64, 8), (stats[1] - ref_stats[1]).reshape(64, 8)], axis=1
-    )
-    rest = jnp.pad(rest, ((0, 0), (0, 112)))
-    message = jnp.concatenate(
-        [jnp.broadcast_to(stats[0].reshape(1, 4, 128), (64, 4, 128)), rest[:, None]], axis=1
-    )
+    rest = jnp.stack([ref_stats[0], stats[1] - ref_stats[1]]).reshape(2, 4, 1, 128)
+    rest = jnp.broadcast_to(rest, (2, 4, 16, 128)).reshape(2, 64, 1, 128)
+    whole = jnp.broadcast_to(stats[0].reshape(1, 4, 128), (64, 4, 128))
+    message = jnp.concatenate([whole, rest[0], rest[1]], axis=1)
     message, other, *swapped = fence(message, other, *swapped)
     swapped += [swap(piece) for piece in pieces[5:]]
     arrived = lax.all_to_all(message, CHIPS, 0, 0, tiled=True)
     other_2 = swap(other)
     lse = log_sum(arrived[:, :4], 0)
     lse_2 = swap(lse)
-    found = log_sum(arrived[:, 4, :8], 0)
-    hits = jnp.sum(arrived[:, 4, 8:16], axis=0)
-    excess = lax.dynamic_slice_in_dim(lse.reshape(HALF), 8 * chip, 8) - found - hits
+    rest = log_sum(arrived[:, 4], 0) + jnp.sum(arrived[:, 5], axis=0)
+    rest = lax.dynamic_slice_in_dim(rest, 8 * (chip % 16), 8)
+    excess = lax.dynamic_slice_in_dim(lse.reshape(HALF), 8 * chip, 8) - rest
 
     both = jnp.concatenate([info, info_2], axis=1)
     head_grad = grad_call(table, (*pieces, *swapped), (mine, other_2), (lse, lse_2), both)

time: 153 us -> 151 us (0.987)
  waiting for transfers between devices: 49.2 us -> 46.7 us
    ppermute x18, waiting for transfers between devices: 39.5 us -> 33.3 us  [send(): return lax.ppermute(values, ALL, pairs)]
    all_to_all x1, waiting for transfers between devices: 1.53 us -> 4.81 us  [shards(): lax.all_to_all(raw, ('zl', 'zh', 'c'), 0, 0, tiled=True)]
    ppermute x18, starting transfers between devices: 23.5 us -> 25.6 us  [send(): return lax.ppermute(values, ALL, pairs)]
    all_to_all x1, starting transfers between devices: 4.75 us -> 6.75 us  [shards(): arrived = lax.all_to_all(message, CHIPS, 0, 0, tiled=True)]
    all_to_all x1, starting transfers between devices: 7.32 us -> 5.42 us  [shards(): lax.all_to_all(raw, ('zl', 'zh', 'c'), 0, 0, tiled=True)]
    unnamed x39 -> x31, local copies, waits for them, and re-layouts: 4 us -> 2.83 us
    ppermute x12 -> x13, starting transfers between devices: 11.1 us -> 10.2 us  [swap(): lax.ppermute(values, ALL, [(index, index ^ 1) for index in range(128)])]
  transfers between devices with their start and end apart: 32 -> 33, of which waited for: 12 -> 10; matrix products, arithmetic and copies ran while one was open for 8% -> 9% of each run, Pallas kernels for 15% -> 16%
where the time goes in v5:
time: 151 us
  starting transfers between devices  47.9 us (32%)
  waiting for transfers between devices  46.7 us (31%)
  Pallas kernels  39.7 us (26%)
  other arithmetic  7.63 us (5%)
  local copies, waits for them, and re-layouts  7.44 us (5%)
    pallas_call x3, Pallas kernels, call(): pl.pallas_call(kernel, out_shape=out_shape, in_specs=[TABLE, *specs], out...  39.7 us
    ppermute x18, waiting for transfers between devices, send(): return lax.ppermute(values, ALL, pairs)  33.3 us
    ppermute x18, starting transfers between devices, send(): return lax.ppermute(values, ALL, pairs)  25.6 us
    ppermute x13, starting transfers between devices, swap(): lax.ppermute(values, ALL, [(index, index ^ 1) for index in range(128)])  10.2 us
    all_to_all x1, waiting for transfers between devices, shards(): arrived = lax.all_to_all(message, CHIPS, 0, 0, tiled=True)  8.44 us
    all_to_all x1, starting transfers between devices, shards(): arrived = lax.all_to_all(message, CHIPS, 0, 0, tiled=True)  6.75 us
    all_to_all x1, starting transfers between devices, shards(): lax.all_to_all(raw, ('zl', 'zh', 'c'), 0, 0, tiled=True)  5.42 us
    all_to_all x1, waiting for transfers between devices, shards(): lax.all_to_all(raw, ('zl', 'zh', 'c'), 0, 0, tiled=True)  4.81 us
  transfers between devices with their start and end apart: 33, of which 10 were waited for; matrix products, arithmetic and copies ran while one was open for 9% of the time, Pallas kernels for 16%

profile of v5, /device:TPU:1, one launch (start us, length us, event | category | flops | bytes accessed | tf_op | source)
XLA Modules:
  0.0 150.7 jit_solution(1967520495770407548)
XLA Ops:
  0.6 1.5 collective-permute-start.7
  2.2 1.0 fusion
  3.2 0.9 copy.25
  4.1 0.9 fusion.2
  5.1 0.8 broadcast_in_dim.95
  5.9 3.0 %collective-permute-start.2 = (bf16[8,4096]{1,0:T(8,128)(2,1)S(1)}, bf16[8,4096]{1,0:T(8,128)(2,1)S(1)}, u32[]{:S(2)}, u32[]{:S(2)}) collective-permute-start(bf16[8,4096]{1,0:T(8,128)(2,1)S(1)} %fusion.2), channel_id=1, source_target_pairs={{0,8},{1,65},{2,10},{3,67},{4,12},{5,69},{6,14},{7,71},{8,0},{9,73... | collective-permute-start | bytes 196616 | tf_op jit(solution)/shard_map/ppermute | solution.py:41
  8.9 0.8 collective-permute-start.1
  9.7 0.7 collective-permute-start
  10.4 1.0 slice.76
  11.4 1.2 collective-permute-start.3
  12.6 5.4 %all-to-all-start = ((bf16[8,16,2048]{2,1,0:T(8,128)(2,1)}), bf16[8,16,2048]{2,1,0:T(8,128)(2,1)S(1)}, u32[]{:S(2)}, u32[]{:S(2)}) async-start(bf16[8,16,2048]{2,1,0:T(8,128)(2,1)} %bitcast.3), calls=%async_computation | async-start | bytes 1048576 | tf_op jit(solution)/shard_map/all_to_all | solution.py:361
  18.1 2.4 %collective-permute-start.6 = (bf16[32,4096]{1,0:T(8,128)(2,1)S(1)}, bf16[32,4096]{1,0:T(8,128)(2,1)S(1)}, u32[]{:S(2)}, u32[]{:S(2)}) collective-permute-start(bf16[32,4096]{1,0:T(8,128)(2,1)S(1)} %pad_maximum_fusion.3), channel_id=1, source_target_pairs={{0,64},{1,9},{2,66},{3,11},{4,68},{5,13},{6,70},{7,15},{8,72},{9,1... | collective-permute-start | bytes 786440 | tf_op jit(solution)/shard_map/ppermute | solution.py:41
  20.5 0.9 collective-permute-start.5
  21.4 0.6 collective-permute-start.4
  22.0 4.8 %all-to-all-done = bf16[8,16,2048]{2,1,0:T(8,128)(2,1)S(1)} async-done(((bf16[8,16,2048]{2,1,0:T(8,128)(2,1)}), bf16[8,16,2048]{2,1,0:T(8,128)(2,1)S(1)}, u32[]{:S(2)}, u32[]{:S(2)}) %all-to-all-start) | async-done | bytes 524320 | tf_op jit(solution)/shard_map/all_to_all | solution.py:361
  26.8 0.2 multiply_reduce_fusion
  27.2 0.7 copy.16
  27.9 0.6 copy.23
  28.5 0.2 multiply_convert_fusion
  28.8 3.0 %collective-permute-start.11 = (bf16[32,8192]{1,0:T(8,128)(2,1)S(1)}, bf16[32,8192]{1,0:T(8,128)(2,1)S(1)}, u32[]{:S(2)}, u32[]{:S(2)}) collective-permute-start(bf16[32,8192]{1,0:T(8,128)(2,1)S(1)} %multiply_convert_fusion), channel_id=1, source_target_pairs={{0,8},{1,65},{2,10},{3,67},{4,12},{5,69},{6,14},{7,71},{8,0},{9,73... | collective-permute-start | bytes 1572872 | tf_op jit(solution)/shard_map/ppermute | solution.py:41
  31.8 0.8 collective-permute-start.10
  32.6 0.7 collective-permute-start.9
  33.3 0.5 collective-permute-start.15
  33.7 2.2 %collective-permute-start.14 = (bf16[128,4096]{1,0:T(8,128)(2,1)S(1)}, bf16[128,4096]{1,0:T(8,128)(2,1)}, u32[]{:S(2)}, u32[]{:S(2)}) collective-permute-start(bf16[128,4096]{1,0:T(8,128)(2,1)S(1)} %pad_maximum_fusion.refs_0_), channel_id=1, source_target_pairs={{0,16},{1,19},{2,18},{3,17},{4,20},{5,23},{6,22},{7,21},{8,24},{9,... | collective-permute-start | bytes 3145736 | tf_op jit(solution)/shard_map/ppermute | solution.py:41
  36.0 2.8 %collective-permute-done.11 = bf16[32,8192]{1,0:T(8,128)(2,1)S(1)} collective-permute-done((bf16[32,8192]{1,0:T(8,128)(2,1)S(1)}, bf16[32,8192]{1,0:T(8,128)(2,1)S(1)}, u32[]{:S(2)}, u32[]{:S(2)}) %collective-permute-start.11) | collective-permute-done | bytes 524320 | tf_op jit(solution)/shard_map/ppermute | solution.py:41
  38.8 6.0 %collective-permute-done.10 = bf16[32,8192]{1,0:T(8,128)(2,1)S(1)} collective-permute-done((bf16[32,8192]{1,0:T(8,128)(2,1)S(1)}, bf16[32,8192]{1,0:T(8,128)(2,1)S(1)}, u32[]{:S(2)}, u32[]{:S(2)}) %collective-permute-start.10) | collective-permute-done | bytes 524320 | tf_op jit(solution)/shard_map/ppermute | solution.py:41
  45.0 0.2 pad_maximum_fusion.1
  45.1 0.9 collective-permute-start.12
  46.0 1.9 %collective-permute-start.13 = (bf16[128,4096]{1,0:T(8,128)(2,1)S(1)}, bf16[128,4096]{1,0:T(8,128)(2,1)S(1)}, u32[]{:S(2)}, u32[]{:S(2)}) collective-permute-start(bf16[128,4096]{1,0:T(8,128)(2,1)S(1)} %get-tuple-element.53.refs_1_), channel_id=1, source_target_pairs={{0,96},{1,13},{2,98},{3,15},{4,100},{5,1},{6,102},{7,3},{8,104},{9... | collective-permute-start | bytes 3145736 | tf_op jit(solution)/shard_map/ppermute | solution.py:41
  47.9 6.6 %collective-permute-done.15.refs_2_ = bf16[128,4096]{1,0:T(8,128)(2,1)S(1)} collective-permute-done((bf16[128,4096]{1,0:T(8,128)(2,1)S(1)}, bf16[128,4096]{1,0:T(8,128)(2,1)S(1)}, u32[]{:S(2)}, u32[]{:S(2)}) %collective-permute-start.15) | collective-permute-done | bytes 1048608 | tf_op jit(solution)/shard_map/ppermute | solution.py:41
  54.5 2.9 %collective-permute-done.14.refs_1_ = bf16[128,4096]{1,0:T(8,128)(2,1)} collective-permute-done((bf16[128,4096]{1,0:T(8,128)(2,1)S(1)}, bf16[128,4096]{1,0:T(8,128)(2,1)}, u32[]{:S(2)}, u32[]{:S(2)}) %collective-permute-start.14) | collective-permute-done | bytes 1048608 | tf_op jit(solution)/shard_map/ppermute | solution.py:41
  57.4 3.0 %collective-permute-done.12.refs_2_ = bf16[128,4096]{1,0:T(8,128)(2,1)S(1)} collective-permute-done((bf16[128,4096]{1,0:T(8,128)(2,1)S(1)}, bf16[128,4096]{1,0:T(8,128)(2,1)S(1)}, u32[]{:S(2)}, u32[]{:S(2)}) %collective-permute-start.12) | collective-permute-done | bytes 1048608 | tf_op jit(solution)/shard_map/ppermute | solution.py:41
  60.4 1.0 copy-done.9
  61.4 2.0 %collective-permute-start.20 = (bf16[128,4096]{1,0:T(8,128)(2,1)}, bf16[128,4096]{1,0:T(8,128)(2,1)}, u32[]{:S(2)}, u32[]{:S(2)}) collective-permute-start(bf16[128,4096]{1,0:T(8,128)(2,1)} %collective-permute-done.14.refs_1_), channel_id=1, source_target_pairs={{0,16},{1,19},{2,18},{3,17},{4,20},{5,23},{6,22},{7,21},{8,24},{9,... | collective-permute-start | bytes 3145736 | tf_op jit(solution)/shard_map/ppermute | solution.py:41
  63.4 0.1 reshape.171
  63.5 0.1 reshape.170
  63.7 2.7 %collective-permute-start.17 = (bf16[128,4096]{1,0:T(8,128)(2,1)S(1)}, bf16[128,4096]{1,0:T(8,128)(2,1)}, u32[]{:S(2)}, u32[]{:S(2)}) collective-permute-start(bf16[128,4096]{1,0:T(8,128)(2,1)S(1)} %get-tuple-element.52.refs_0_), channel_id=1, source_target_pairs={{0,96},{1,13},{2,98},{3,15},{4,100},{5,1},{6,102},{7,3},{8,104},{9... | collective-permute-start | bytes 3145736 | tf_op jit(solution)/shard_map/ppermute | solution.py:41
  66.4 2.7 %collective-permute-start.19 = (bf16[128,4096]{1,0:T(8,128)(2,1)}, bf16[128,4096]{1,0:T(8,128)(2,1)}, u32[]{:S(2)}, u32[]{:S(2)}) collective-permute-start(bf16[128,4096]{1,0:T(8,128)(2,1)} %copy-done.9), channel_id=1, source_target_pairs={{0,96},{1,13},{2,98},{3,15},{4,100},{5,1},{6,102},{7,3},{8,104},{9... | collective-permute-start | bytes 3145736 | tf_op jit(solution)/shard_map/ppermute | solution.py:41
  69.2 0.4 fusion.4
  69.9 0.2 convert_reduce_fusion.3
  70.3 0.6 add_multiply_fusion.table
  70.9 0.7 select_select_fusion
  71.6 4.0 %collective-permute-done.20.refs_3_ = bf16[128,4096]{1,0:T(8,128)(2,1)} collective-permute-done((bf16[128,4096]{1,0:T(8,128)(2,1)}, bf16[128,4096]{1,0:T(8,128)(2,1)}, u32[]{:S(2)}, u32[]{:S(2)}) %collective-permute-start.20) | collective-permute-done | bytes 1048608 | tf_op jit(solution)/shard_map/ppermute | solution.py:41
  75.6 9.3 %shard_map.95 = f32[8,512]{1,0:T(8,128)} custom-call(s32[256]{0:T(256)} %add_multiply_fusion.table, bf16[128,4096]{1,0:T(8,128)(2,1)} %copy-done, bf16[128,4096]{1,0:T(8,128)(2,1)} %collective-permute-done.14.refs_1_, bf16[128,4096]{1,0:T(8,128)(2,1)} %copy-done.10, bf16[128,4096]{1,0:T(8,128)(2,1)} %collective-permute-done.20.refs_3_, ...), custom_call_target="tpu_custom_call" | custom-call | flops 4294967296 | bytes 12582912 | tf_op jit(solution)/shard_map/pallas_call | solution.py:270
  84.9 8.0 %collective-permute-done.18.refs_6_ = bf16[128,4096]{1,0:T(8,128)(2,1)} collective-permute-done((bf16[128,4096]{1,0:T(8,128)(2,1)S(1)}, bf16[128,4096]{1,0:T(8,128)(2,1)}, u32[]{:S(2)}, u32[]{:S(2)}) %collective-permute-start.18) | collective-permute-done | bytes 1048608 | tf_op jit(solution)/shard_map/ppermute | solution.py:41
  92.9 3.9 %collective-permute-start.21 = (bf16[128,4096]{1,0:T(8,128)(2,1)S(1)}, bf16[128,4096]{1,0:T(8,128)(2,1)}, u32[]{:S(2)}, u32[]{:S(2)}) collective-permute-start(bf16[128,4096]{1,0:T(8,128)(2,1)S(1)} %get-tuple-element.52.refs_0_), channel_id=1, source_target_pairs={{0,1},{1,0},{2,3},{3,2},{4,5},{5,4},{6,7},{7,6},{8,9},{9,8},{10,11... | collective-permute-start | bytes 3145736 | tf_op jit(solution)/shard_map/ppermute | solution.py:45
  97.0 0.4 collective-permute-start.23
  97.5 0.4 collective-permute-start.25
  97.9 14.3 %shard_map.96 = (f32[512,512]{1,0:T(8,128)}, f32[512,512]{1,0:T(8,128)}, f32[8,512]{1,0:T(8,128)}) custom-call(s32[256]{0:T(256)} %add_multiply_fusion.table, bf16[128,4096]{1,0:T(8,128)(2,1)} %copy-done.1, bf16[128,4096]{1,0:T(8,128)(2,1)} %copy-done.2, bf16[128,4096]{1,0:T(8,128)(2,1)} %copy-done.8, bf16[128,4096]{1,0:T(8,128)(2,1)} %collective-permute-done.16.refs_3_, ...), custom_call_target="tpu_custom_call" | custom-call | flops 8589934592 | bytes 12582912 | tf_op jit(solution)/shard_map/pallas_call | solution.py:270
  112.2 0.8 fusion.30
  113.0 0.8 pad_maximum_fusion.4
  113.9 6.7 %all-to-all-start.1 = ((f32[64,6,128]{2,1,0:T(8,128)}), f32[64,6,128]{2,1,0:T(8,128)S(1)}, u32[]{:S(2)}, u32[]{:S(2)}) async-start(f32[64,6,128]{2,1,0:T(8,128)} %pad_maximum_fusion.4), calls=%async_computation.1 | async-start | bytes 524288 | tf_op jit(solution)/shard_map/all_to_all | solution.py:394
  120.7 0.6 pad_maximum_fusion.5.refs_20_
  121.3 0.4 collective-permute-start.26
  121.6 0.1 collective-permute-start.27
  121.8 0.4 collective-permute-start.28
  122.1 0.1 collective-permute-start.29
  122.3 8.4 %all-to-all-done.1 = f32[64,6,128]{2,1,0:T(8,128)S(1)} async-done(((f32[64,6,128]{2,1,0:T(8,128)}), f32[64,6,128]{2,1,0:T(8,128)S(1)}, u32[]{:S(2)}, u32[]{:S(2)}) %all-to-all-start.1) | async-done | bytes 196640 | tf_op jit(solution)/shard_map/all_to_all | solution.py:394
  131.0 1.4 collective-permute-start.30
  132.5 0.6 dynamic-slice_subtract_fusion
  133.1 0.1 collective-permute-done.30.refs_19_
  133.3 0.8 copy-done.11
  134.1 0.3 copy-done.12
  134.4 16.1 %shard_map.97 = bf16[8192,512]{1,0:T(8,128)(2,1)} custom-call(s32[256]{0:T(256)} %add_multiply_fusion.table, bf16[128,4096]{1,0:T(8,128)(2,1)} %copy-done.1, bf16[128,4096]{1,0:T(8,128)(2,1)} %copy-done.2, bf16[128,4096]{1,0:T(8,128)(2,1)} %copy-done.8, bf16[128,4096]{1,0:T(8,128)(2,1)} %collective-permute-done.16.refs_3_, ...), custom_call_target="tpu_custom_call" | custom-call | flops 8589934592 | bytes 12582912 | tf_op jit(solution)/shard_map/pallas_call | solution.py:270
  (86 shorter events, 1.8 us)
Async XLA Ops:
  0.6 28.2 %collective-permute-start.7 = (bf16[8192,512]{1,0:T(8,128)(2,1)}, bf16[8192,512]{1,0:T(8,128)(2,1)}, u32[]{:S(2)}, u32[]{:S(2)}) collective-permute-start(bf16[8192,512]{1,0:T(8,128)(2,1)} %refs_8_.1), channel_id=1, source_target_pairs={{0,1},{1,0},{2,3},{3,2},{4,5},{5,4},{6,7},{7,6},{8,9},{9,8},{10,11... | collective-permute-start | bytes 25165832 | tf_op jit(solution)/shard_map/ppermute | solution.py:45
  2.1 26.7 %collective-permute-start.8 = (bf16[4096,512]{1,0:T(8,128)(2,1)}, bf16[4096,512]{1,0:T(8,128)(2,1)}, u32[]{:S(2)}, u32[]{:S(2)}) collective-permute-start(bf16[4096,512]{1,0:T(8,128)(2,1)} %refs_4_.1), channel_id=1, source_target_pairs={{0,1},{1,0},{2,3},{3,2},{4,5},{5,4},{6,7},{7,6},{8,9},{9,8},{10,11... | collective-permute-start | bytes 12582920 | tf_op jit(solution)/shard_map/ppermute | solution.py:45
  5.9 5.5 %collective-permute-start.2 = (bf16[8,4096]{1,0:T(8,128)(2,1)S(1)}, bf16[8,4096]{1,0:T(8,128)(2,1)S(1)}, u32[]{:S(2)}, u32[]{:S(2)}) collective-permute-start(bf16[8,4096]{1,0:T(8,128)(2,1)S(1)} %fusion.2), channel_id=1, source_target_pairs={{0,8},{1,65},{2,10},{3,67},{4,12},{5,69},{6,14},{7,71},{8,0},{9,73... | collective-permute-start | bytes 196616 | tf_op jit(solution)/shard_map/ppermute | solution.py:41
  8.9 9.1 %collective-permute-start.1 = (bf16[8,4096]{1,0:T(8,128)(2,1)S(1)}, bf16[8,4096]{1,0:T(8,128)(2,1)S(1)}, u32[]{:S(2)}, u32[]{:S(2)}) collective-permute-start(bf16[8,4096]{1,0:T(8,128)(2,1)S(1)} %fusion.2), channel_id=1, source_target_pairs={{0,12},{1,97},{2,14},{3,99},{4,0},{5,101},{6,2},{7,103},{8,4},{9,1... | collective-permute-start | bytes 196616 | tf_op jit(solution)/shard_map/ppermute | solution.py:41
  9.7 8.3 %collective-permute-start = (bf16[8,4096]{1,0:T(8,128)(2,1)S(1)}, bf16[8,4096]{1,0:T(8,128)(2,1)S(1)}, u32[]{:S(2)}, u32[]{:S(2)}) collective-permute-start(bf16[8,4096]{1,0:T(8,128)(2,1)S(1)} %fusion.2), channel_id=1, source_target_pairs={{0,4},{1,33},{2,6},{3,35},{4,8},{5,37},{6,10},{7,39},{8,12},{9,41}... | collective-permute-start | bytes 196616 | tf_op jit(solution)/shard_map/ppermute | solution.py:41
  11.4 6.6 %collective-permute-start.3 = (bf16[448,512]{1,0:T(8,128)(2,1)S(1)}, bf16[448,512]{1,0:T(8,128)(2,1)S(1)}, u32[]{:S(2)}, u32[]{:S(2)}) collective-permute-start(bf16[448,512]{1,0:T(8,128)(2,1)S(1)} %slice.76), channel_id=1, source_target_pairs={{0,1},{1,0},{2,3},{3,2},{4,5},{5,4},{6,7},{7,6},{8,9},{9,8},{10,11... | collective-permute-start | bytes 1376264 | tf_op jit(solution)/shard_map/ppermute | solution.py:45
  12.6 14.2 %all-to-all-start = ((bf16[8,16,2048]{2,1,0:T(8,128)(2,1)}), bf16[8,16,2048]{2,1,0:T(8,128)(2,1)S(1)}, u32[]{:S(2)}, u32[]{:S(2)}) async-start(bf16[8,16,2048]{2,1,0:T(8,128)(2,1)} %bitcast.3), calls=%async_computation | async-start | bytes 1048576 | tf_op jit(solution)/shard_map/all_to_all | solution.py:361
  18.1 8.9 %copy-start.13 = (bf16[448,512]{1,0:T(8,128)(2,1)}, bf16[448,512]{1,0:T(8,128)(2,1)S(1)}, u32[]{:S(2)}) copy-start(bf16[448,512]{1,0:T(8,128)(2,1)S(1)} %collective-permute-done.3.refs_5_) | copy-start | bytes 1376260
  18.1 10.6 %collective-permute-start.6 = (bf16[32,4096]{1,0:T(8,128)(2,1)S(1)}, bf16[32,4096]{1,0:T(8,128)(2,1)S(1)}, u32[]{:S(2)}, u32[]{:S(2)}) collective-permute-start(bf16[32,4096]{1,0:T(8,128)(2,1)S(1)} %pad_maximum_fusion.3), channel_id=1, source_target_pairs={{0,64},{1,9},{2,66},{3,11},{4,68},{5,13},{6,70},{7,15},{8,72},{9,1... | collective-permute-start | bytes 786440 | tf_op jit(solution)/shard_map/ppermute | solution.py:41
  20.5 8.2 %collective-permute-start.5 = (bf16[32,4096]{1,0:T(8,128)(2,1)S(1)}, bf16[32,4096]{1,0:T(8,128)(2,1)S(1)}, u32[]{:S(2)}, u32[]{:S(2)}) collective-permute-start(bf16[32,4096]{1,0:T(8,128)(2,1)S(1)} %pad_maximum_fusion.3), channel_id=1, source_target_pairs={{0,96},{1,13},{2,98},{3,15},{4,100},{5,1},{6,102},{7,3},{8,104},{9... | collective-permute-start | bytes 786440 | tf_op jit(solution)/shard_map/ppermute | solution.py:41
  21.4 7.3 %collective-permute-start.4 = (bf16[32,4096]{1,0:T(8,128)(2,1)S(1)}, bf16[32,4096]{1,0:T(8,128)(2,1)S(1)}, u32[]{:S(2)}, u32[]{:S(2)}) collective-permute-start(bf16[32,4096]{1,0:T(8,128)(2,1)S(1)} %pad_maximum_fusion.3), channel_id=1, source_target_pairs={{0,32},{1,5},{2,34},{3,7},{4,36},{5,9},{6,38},{7,11},{8,40},{9,13}... | collective-permute-start | bytes 786440 | tf_op jit(solution)/shard_map/ppermute | solution.py:41
  27.2 1.3 copy-start.4
  28.8 16.1 %copy-start = (bf16[128,4096]{1,0:T(8,128)(2,1)}, bf16[128,4096]{1,0:T(8,128)(2,1)S(1)}, u32[]{:S(2)}) copy-start(bf16[128,4096]{1,0:T(8,128)(2,1)S(1)} %pad_maximum_fusion.refs_0_) | copy-start | bytes 3145732
  28.8 10.0 %collective-permute-start.11 = (bf16[32,8192]{1,0:T(8,128)(2,1)S(1)}, bf16[32,8192]{1,0:T(8,128)(2,1)S(1)}, u32[]{:S(2)}, u32[]{:S(2)}) collective-permute-start(bf16[32,8192]{1,0:T(8,128)(2,1)S(1)} %multiply_convert_fusion), channel_id=1, source_target_pairs={{0,8},{1,65},{2,10},{3,67},{4,12},{5,69},{6,14},{7,71},{8,0},{9,73... | collective-permute-start | bytes 1572872 | tf_op jit(solution)/shard_map/ppermute | solution.py:41
  31.8 13.0 %collective-permute-start.10 = (bf16[32,8192]{1,0:T(8,128)(2,1)S(1)}, bf16[32,8192]{1,0:T(8,128)(2,1)S(1)}, u32[]{:S(2)}, u32[]{:S(2)}) collective-permute-start(bf16[32,8192]{1,0:T(8,128)(2,1)S(1)} %multiply_convert_fusion), channel_id=1, source_target_pairs={{0,12},{1,97},{2,14},{3,99},{4,0},{5,101},{6,2},{7,103},{8,4},{9,1... | collective-permute-start | bytes 1572872 | tf_op jit(solution)/shard_map/ppermute | solution.py:41
  32.6 12.3 %collective-permute-start.9 = (bf16[32,8192]{1,0:T(8,128)(2,1)S(1)}, bf16[32,8192]{1,0:T(8,128)(2,1)S(1)}, u32[]{:S(2)}, u32[]{:S(2)}) collective-permute-start(bf16[32,8192]{1,0:T(8,128)(2,1)S(1)} %multiply_convert_fusion), channel_id=1, source_target_pairs={{0,4},{1,33},{2,6},{3,35},{4,8},{5,37},{6,10},{7,39},{8,12},{9,41}... | collective-permute-start | bytes 1572872 | tf_op jit(solution)/shard_map/ppermute | solution.py:41
  33.3 21.2 %collective-permute-start.15 = (bf16[128,4096]{1,0:T(8,128)(2,1)S(1)}, bf16[128,4096]{1,0:T(8,128)(2,1)S(1)}, u32[]{:S(2)}, u32[]{:S(2)}) collective-permute-start(bf16[128,4096]{1,0:T(8,128)(2,1)S(1)} %pad_maximum_fusion.refs_0_), channel_id=1, source_target_pairs={{0,18},{1,17},{2,16},{3,19},{4,22},{5,21},{6,20},{7,23},{8,26},{9,... | collective-permute-start | bytes 3145736 | tf_op jit(solution)/shard_map/ppermute | solution.py:41
  33.7 23.7 %collective-permute-start.14 = (bf16[128,4096]{1,0:T(8,128)(2,1)S(1)}, bf16[128,4096]{1,0:T(8,128)(2,1)}, u32[]{:S(2)}, u32[]{:S(2)}) collective-permute-start(bf16[128,4096]{1,0:T(8,128)(2,1)S(1)} %pad_maximum_fusion.refs_0_), channel_id=1, source_target_pairs={{0,16},{1,19},{2,18},{3,17},{4,20},{5,23},{6,22},{7,21},{8,24},{9,... | collective-permute-start | bytes 3145736 | tf_op jit(solution)/shard_map/ppermute | solution.py:41
  44.9 18.4 %copy-start.6 = (s32[1024]{0:T(1024)S(1)}, s32[1024]{0:T(1024)}, u32[]{:S(2)}) copy-start(s32[1024]{0:T(1024)} %param.15) | copy-start | bytes 12292
  44.9 18.6 %copy-start.5 = (s32[1024]{0:T(1024)S(1)}, s32[1024]{0:T(1024)}, u32[]{:S(2)}) copy-start(s32[1024]{0:T(1024)} %param.14) | copy-start | bytes 12292
  45.1 47.8 %copy-start.1 = (bf16[128,4096]{1,0:T(8,128)(2,1)}, bf16[128,4096]{1,0:T(8,128)(2,1)S(1)}, u32[]{:S(2)}) copy-start(bf16[128,4096]{1,0:T(8,128)(2,1)S(1)} %get-tuple-element.52.refs_0_) | copy-start | bytes 3145732
  45.1 51.7 %copy-start.2 = (bf16[128,4096]{1,0:T(8,128)(2,1)}, bf16[128,4096]{1,0:T(8,128)(2,1)S(1)}, u32[]{:S(2)}) copy-start(bf16[128,4096]{1,0:T(8,128)(2,1)S(1)} %get-tuple-element.53.refs_1_) | copy-start | bytes 3145732
  45.1 15.2 %collective-permute-start.12 = (bf16[128,4096]{1,0:T(8,128)(2,1)S(1)}, bf16[128,4096]{1,0:T(8,128)(2,1)S(1)}, u32[]{:S(2)}, u32[]{:S(2)}) collective-permute-start(bf16[128,4096]{1,0:T(8,128)(2,1)S(1)} %get-tuple-element.52.refs_0_), channel_id=1, source_target_pairs={{0,32},{1,5},{2,34},{3,7},{4,36},{5,9},{6,38},{7,11},{8,40},{9,13}... | collective-permute-start | bytes 3145736 | tf_op jit(solution)/shard_map/ppermute | solution.py:41
  46.0 14.4 %collective-permute-start.13 = (bf16[128,4096]{1,0:T(8,128)(2,1)S(1)}, bf16[128,4096]{1,0:T(8,128)(2,1)S(1)}, u32[]{:S(2)}, u32[]{:S(2)}) collective-permute-start(bf16[128,4096]{1,0:T(8,128)(2,1)S(1)} %get-tuple-element.53.refs_1_), channel_id=1, source_target_pairs={{0,96},{1,13},{2,98},{3,15},{4,100},{5,1},{6,102},{7,3},{8,104},{9... | collective-permute-start | bytes 3145736 | tf_op jit(solution)/shard_map/ppermute | solution.py:41
  54.5 8.9 %copy-start.10 = (bf16[128,4096]{1,0:T(8,128)(2,1)}, bf16[128,4096]{1,0:T(8,128)(2,1)S(1)}, u32[]{:S(2)}) copy-start(bf16[128,4096]{1,0:T(8,128)(2,1)S(1)} %collective-permute-done.15.refs_2_) | copy-start | bytes 3145732
  60.4 36.6 %copy-start.8 = (bf16[128,4096]{1,0:T(8,128)(2,1)}, bf16[128,4096]{1,0:T(8,128)(2,1)S(1)}, u32[]{:S(2)}) copy-start(bf16[128,4096]{1,0:T(8,128)(2,1)S(1)} %collective-permute-done.12.refs_2_) | copy-start | bytes 3145732
  60.4 1.0 copy-start.9
  61.4 14.3 %collective-permute-start.20 = (bf16[128,4096]{1,0:T(8,128)(2,1)}, bf16[128,4096]{1,0:T(8,128)(2,1)}, u32[]{:S(2)}, u32[]{:S(2)}) collective-permute-start(bf16[128,4096]{1,0:T(8,128)(2,1)} %collective-permute-done.14.refs_1_), channel_id=1, source_target_pairs={{0,16},{1,19},{2,18},{3,17},{4,20},{5,23},{6,22},{7,21},{8,24},{9,... | collective-permute-start | bytes 3145736 | tf_op jit(solution)/shard_map/ppermute | solution.py:41
  63.7 21.2 %collective-permute-start.17 = (bf16[128,4096]{1,0:T(8,128)(2,1)S(1)}, bf16[128,4096]{1,0:T(8,128)(2,1)}, u32[]{:S(2)}, u32[]{:S(2)}) collective-permute-start(bf16[128,4096]{1,0:T(8,128)(2,1)S(1)} %get-tuple-element.52.refs_0_), channel_id=1, source_target_pairs={{0,96},{1,13},{2,98},{3,15},{4,100},{5,1},{6,102},{7,3},{8,104},{9... | collective-permute-start | bytes 3145736 | tf_op jit(solution)/shard_map/ppermute | solution.py:41
  66.4 18.5 %collective-permute-start.16 = (bf16[128,4096]{1,0:T(8,128)(2,1)S(1)}, bf16[128,4096]{1,0:T(8,128)(2,1)}, u32[]{:S(2)}, u32[]{:S(2)}) collective-permute-start(bf16[128,4096]{1,0:T(8,128)(2,1)S(1)} %get-tuple-element.53.refs_1_), channel_id=1, source_target_pairs={{0,32},{1,5},{2,34},{3,7},{4,36},{5,9},{6,38},{7,11},{8,40},{9,13}... | collective-permute-start | bytes 3145736 | tf_op jit(solution)/shard_map/ppermute | solution.py:41
  66.4 26.5 %collective-permute-start.18 = (bf16[128,4096]{1,0:T(8,128)(2,1)S(1)}, bf16[128,4096]{1,0:T(8,128)(2,1)}, u32[]{:S(2)}, u32[]{:S(2)}) collective-permute-start(bf16[128,4096]{1,0:T(8,128)(2,1)S(1)} %collective-permute-done.12.refs_2_), channel_id=1, source_target_pairs={{0,32},{1,5},{2,34},{3,7},{4,36},{5,9},{6,38},{7,11},{8,40},{9,13}... | collective-permute-start | bytes 3145736 | tf_op jit(solution)/shard_map/ppermute | solution.py:41
  66.4 26.5 %collective-permute-start.19 = (bf16[128,4096]{1,0:T(8,128)(2,1)}, bf16[128,4096]{1,0:T(8,128)(2,1)}, u32[]{:S(2)}, u32[]{:S(2)}) collective-permute-start(bf16[128,4096]{1,0:T(8,128)(2,1)} %copy-done.9), channel_id=1, source_target_pairs={{0,96},{1,13},{2,98},{3,15},{4,100},{5,1},{6,102},{7,3},{8,104},{9... | collective-permute-start | bytes 3145736 | tf_op jit(solution)/shard_map/ppermute | solution.py:41
  84.9 35.7 %copy-start.3 = (f32[8,512]{1,0:T(8,128)S(1)}, f32[8,512]{1,0:T(8,128)}, u32[]{:S(2)}) copy-start(f32[8,512]{1,0:T(8,128)} %get-tuple-element.94.refs_7_.refs_10_) | copy-start | bytes 49156
  92.9 20.9 %collective-permute-start.21 = (bf16[128,4096]{1,0:T(8,128)(2,1)S(1)}, bf16[128,4096]{1,0:T(8,128)(2,1)}, u32[]{:S(2)}, u32[]{:S(2)}) collective-permute-start(bf16[128,4096]{1,0:T(8,128)(2,1)S(1)} %get-tuple-element.52.refs_0_), channel_id=1, source_target_pairs={{0,1},{1,0},{2,3},{3,2},{4,5},{5,4},{6,7},{7,6},{8,9},{9,8},{10,11... | collective-permute-start | bytes 3145736 | tf_op jit(solution)/shard_map/ppermute | solution.py:45
  96.9 17.0 %collective-permute-start.22 = (bf16[128,4096]{1,0:T(8,128)(2,1)S(1)}, bf16[128,4096]{1,0:T(8,128)(2,1)}, u32[]{:S(2)}, u32[]{:S(2)}) collective-permute-start(bf16[128,4096]{1,0:T(8,128)(2,1)S(1)} %get-tuple-element.53.refs_1_), channel_id=1, source_target_pairs={{0,1},{1,0},{2,3},{3,2},{4,5},{5,4},{6,7},{7,6},{8,9},{9,8},{10,11... | collective-permute-start | bytes 3145736 | tf_op jit(solution)/shard_map/ppermute | solution.py:45
  97.0 16.9 %collective-permute-start.23 = (bf16[128,4096]{1,0:T(8,128)(2,1)S(1)}, bf16[128,4096]{1,0:T(8,128)(2,1)}, u32[]{:S(2)}, u32[]{:S(2)}) collective-permute-start(bf16[128,4096]{1,0:T(8,128)(2,1)S(1)} %collective-permute-done.12.refs_2_), channel_id=1, source_target_pairs={{0,1},{1,0},{2,3},{3,2},{4,5},{5,4},{6,7},{7,6},{8,9},{9,8},{10,11... | collective-permute-start | bytes 3145736 | tf_op jit(solution)/shard_map/ppermute | solution.py:45
  97.4 16.5 %collective-permute-start.24 = (bf16[128,4096]{1,0:T(8,128)(2,1)}, bf16[128,4096]{1,0:T(8,128)(2,1)}, u32[]{:S(2)}, u32[]{:S(2)}) collective-permute-start(bf16[128,4096]{1,0:T(8,128)(2,1)} %collective-permute-done.16.refs_3_), channel_id=1, source_target_pairs={{0,1},{1,0},{2,3},{3,2},{4,5},{5,4},{6,7},{7,6},{8,9},{9,8},{10,11... | collective-permute-start | bytes 3145736 | tf_op jit(solution)/shard_map/ppermute | solution.py:45
  97.5 16.4 %collective-permute-start.25 = (bf16[128,4096]{1,0:T(8,128)(2,1)}, bf16[128,4096]{1,0:T(8,128)(2,1)}, u32[]{:S(2)}, u32[]{:S(2)}) collective-permute-start(bf16[128,4096]{1,0:T(8,128)(2,1)} %collective-permute-done.17.refs_4_), channel_id=1, source_target_pairs={{0,1},{1,0},{2,3},{3,2},{4,5},{5,4},{6,7},{7,6},{8,9},{9,8},{10,11... | collective-permute-start | bytes 3145736 | tf_op jit(solution)/shard_map/ppermute | solution.py:45
  113.9 16.9 %all-to-all-start.1 = ((f32[64,6,128]{2,1,0:T(8,128)}), f32[64,6,128]{2,1,0:T(8,128)S(1)}, u32[]{:S(2)}, u32[]{:S(2)}) async-start(f32[64,6,128]{2,1,0:T(8,128)} %pad_maximum_fusion.4), calls=%async_computation.1 | async-start | bytes 524288 | tf_op jit(solution)/shard_map/all_to_all | solution.py:394
  121.3 11.8 %collective-permute-start.26 = (bf16[128,4096]{1,0:T(8,128)(2,1)}, bf16[128,4096]{1,0:T(8,128)(2,1)S(1)}, u32[]{:S(2)}, u32[]{:S(2)}) collective-permute-start(bf16[128,4096]{1,0:T(8,128)(2,1)} %copy-done.9), channel_id=1, source_target_pairs={{0,1},{1,0},{2,3},{3,2},{4,5},{5,4},{6,7},{7,6},{8,9},{9,8},{10,11... | collective-permute-start | bytes 3145736 | tf_op jit(solution)/shard_map/ppermute | solution.py:45
  121.6 11.5 %collective-permute-start.27 = (bf16[128,4096]{1,0:T(8,128)(2,1)}, bf16[128,4096]{1,0:T(8,128)(2,1)S(1)}, u32[]{:S(2)}, u32[]{:S(2)}) collective-permute-start(bf16[128,4096]{1,0:T(8,128)(2,1)} %collective-permute-done.18.refs_6_), channel_id=1, source_target_pairs={{0,1},{1,0},{2,3},{3,2},{4,5},{5,4},{6,7},{7,6},{8,9},{9,8},{10,11... | collective-permute-start | bytes 3145736 | tf_op jit(solution)/shard_map/ppermute | solution.py:45
  121.8 11.3 %collective-permute-start.28 = (bf16[128,4096]{1,0:T(8,128)(2,1)}, bf16[128,4096]{1,0:T(8,128)(2,1)}, u32[]{:S(2)}, u32[]{:S(2)}) collective-permute-start(bf16[128,4096]{1,0:T(8,128)(2,1)} %collective-permute-done.19.refs_7_), channel_id=1, source_target_pairs={{0,1},{1,0},{2,3},{3,2},{4,5},{5,4},{6,7},{7,6},{8,9},{9,8},{10,11... | collective-permute-start | bytes 3145736 | tf_op jit(solution)/shard_map/ppermute | solution.py:45
  122.1 11.1 %collective-permute-start.29 = (f32[512,512]{1,0:T(8,128)}, f32[512,512]{1,0:T(8,128)}, u32[]{:S(2)}, u32[]{:S(2)}) collective-permute-start(f32[512,512]{1,0:T(8,128)} %get-tuple-element.71), channel_id=1, source_target_pairs={{0,1},{1,0},{2,3},{3,2},{4,5},{5,4},{6,7},{7,6},{8,9},{9,8},{10,11... | collective-permute-start | bytes 3145736 | tf_op jit(solution)/shard_map/ppermute | solution.py:45
  131.0 2.3 %copy-start.7 = (f32[4,128]{1,0:T(4,128)}, f32[4,128]{1,0:T(4,128)S(1)}, u32[]{:S(2)}) copy-start(f32[4,128]{1,0:T(4,128)S(1)} %log_add_fusion.refs_18_) | copy-start | bytes 6148
  131.0 2.2 %collective-permute-start.30 = (f32[4,128]{1,0:T(4,128)S(1)}, f32[4,128]{1,0:T(4,128)S(1)}, u32[]{:S(2)}, u32[]{:S(2)}) collective-permute-start(f32[4,128]{1,0:T(4,128)S(1)} %log_add_fusion.refs_18_), channel_id=1, source_target_pairs={{0,1},{1,0},{2,3},{3,2},{4,5},{5,4},{6,7},{7,6},{8,9},{9,8},{10,11... | collective-permute-start | bytes 6152 | tf_op jit(solution)/shard_map/ppermute | solution.py:45
  133.1 1.0 copy-start.11
  133.1 1.3 copy-start.12
  133.3 1.2 copy-start.14

commit v6 on v5

--- a/solution.py
+++ b/solution.py
@@ -16,7 +16,6 @@
 BLOCK = 1024
 DEEP = 2048
 FIRST = 448
-OWN_STEPS = ((0, 1024), (1024, 3072), (4096, 4096))
 MIB = 1 << 20
 
 
@@ -151,23 +150,47 @@
         self.start(number + 3)
 
 
-def own_kernel(table, *refs):
-    pieces, (head, head_2, info, mine, other, stats, xbuf, hbuf, tmp, sems) = refs[:8], refs[8:]
+def half_products(low, top, heads, xbuf, hbuf, tmp, sems):
     stages = []
-    for first, depth in OWN_STEPS:
-        cut, part, within = pl.ds(first, depth), first // WIDE, pl.ds(first % WIDE, depth)
-        sources = [piece.at[:, within] for piece in pieces[part::2]]
-        targets = [xbuf.at[pl.ds(128 * k, 128), cut] for k in range(4)]
-        stages.append((sources + [head.at[cut, :]], targets + [hbuf.at[0, cut, :]]))
-        stages.append(([head_2.at[cut, :]], [hbuf.at[1, cut, :]]))
+    for step in range(2 * WIDE // DEEP):
+        cut = pl.ds(DEEP * step, DEEP)
+        part, within = DEEP * step // WIDE, pl.ds(DEEP * step % WIDE, DEEP)
+        sources = [piece.at[:, within] for piece in (low, top)[part]]
+        targets = [xbuf.at[pl.ds(128 * k, 128), cut] for k in (0, 1)]
+        stages.append((sources + [heads[0].at[cut, :]], targets + [hbuf.at[0, cut, :]]))
+        stages.append(([heads[1].at[cut, :]], [hbuf.at[1, cut, :]]))
     stages = Stages(stages, sems)
-    for step, (first, depth) in enumerate(OWN_STEPS):
-        cut = slice(first, first + depth)
+    for step in range(2 * WIDE // DEEP):
+        cut, part = slice(DEEP * step, DEEP * step + DEEP), DEEP * step // WIDE
         for side in (0, 1):
             stages.wait(2 * step + side)
-            add_product(tmp.at[side], step, xbuf[:, cut], hbuf[side, cut, :])
+            add_product(
+                tmp.at[side, part], DEEP * step % WIDE, xbuf[:, cut], hbuf[side, cut, :]
+            )
+
+
+def early_kernel(low, low_near, top, top_back, head, head_2, out, xbuf, hbuf, sems):
+    half_products((low, low_near), (top, top_back), (head, head_2), xbuf, hbuf, out, sems)
+
+
+def late_kernel(table, *refs):
+    low_back, low_far, top_near, top_far, head, head_2, before, info = refs[:8]
+    mine, other, stats, xbuf, hbuf, tmp, first, sems, before_sem = refs[8:]
+    copy = pltpu.make_async_copy(before, first, before_sem)
+    copy.start()
+    low, top = (low_back, low_far), (top_near, top_far)
+    half_products(low, top, (head, head_2), xbuf, hbuf, tmp, sems)
+    copy.wait()
     for side, total in enumerate((mine, other)):
-        put_slots(table, 0, tmp.at[side], total)
+        a, b = slice(0, 128), slice(128, 256)
+        slots = (
+            first[side, 0, a, :] + first[side, 1, a, :],
+            first[side, 0, b, :] + tmp[side, 1, a, :],
+            first[side, 1, b, :] + tmp[side, 0, a, :],
+            tmp[side, 0, b, :] + tmp[side, 1, b, :],
+        )
+        for number, values in enumerate(slots):
+            put_rows(table, 16 * number, values, total)
     write_stats((mine, other), info, stats)
 
 
@@ -266,14 +289,14 @@
     return jax.ShapeDtypeStruct(shape, jnp.float32)
 
 
-def call(kernel, operands, out_shape, out_specs, scratch, rows, specs, limit=60):
+def call(kernel, operands, out_shape, out_specs, scratch, rows, specs):
     return pl.pallas_call(
         kernel,
         out_shape=out_shape,
-        in_specs=[TABLE, *specs],
+        in_specs=specs,
         out_specs=out_specs,
         scratch_shapes=scratch,
-        compiler_params=pltpu.CompilerParams(vmem_limit_bytes=limit * MIB),
+        compiler_params=pltpu.CompilerParams(vmem_limit_bytes=60 * MIB),
         cost_estimate=pl.CostEstimate(
             flops=4 * rows * HALF * WIDE, bytes_accessed=12 * MIB, transcendentals=0
         ),
@@ -283,17 +306,33 @@
 TOTALS = (floats(HALF, HALF), floats(HALF, HALF))
 
 
-def own_call(table, pieces, heads, info):
-    operands = (table, *pieces, *heads, info)
+PARTIAL = (2, 2, 256, HALF)
+
+
+def half_scratch():
+    return [
+        pltpu.VMEM((256, 2 * WIDE), jnp.bfloat16),
+        pltpu.VMEM((2, 2 * WIDE, HALF), jnp.bfloat16),
+    ]
+
+
+def early_call(pieces, heads):
+    scratch = [*half_scratch(), DMA((4 * WIDE // DEEP, 3))]
+    return call(early_kernel, (*pieces, *heads), floats(*PARTIAL), INSIDE, scratch, 512, [ANY] * 6)
+
+
+def late_call(table, pieces, heads, before, info):
+    operands = (table, *pieces, *heads, before, info)
     shapes = (*TOTALS, floats(8, HALF))
     scratch = [
-        pltpu.VMEM((HALF, 2 * WIDE), jnp.bfloat16),
-        pltpu.VMEM((2, 2 * WIDE, HALF), jnp.bfloat16),
-        pltpu.VMEM((2, HALF, HALF), jnp.float32),
-        DMA((2 * len(OWN_STEPS), 5)),
-    ]
-    specs = [ANY] * 10 + [INSIDE]
-    return call(own_kernel, operands, shapes, (INSIDE,) * 3, scratch, 1024, specs)
+        *half_scratch(),
+        pltpu.VMEM(PARTIAL, jnp.float32),
+        pltpu.VMEM(PARTIAL, jnp.float32),
+        DMA((4 * WIDE // DEEP, 3)),
+        DMA,
+    ]
+    specs = [TABLE] + [ANY] * 7 + [INSIDE]
+    return call(late_kernel, operands, shapes, (INSIDE,) * 3, scratch, 512, specs)
 
 
 def ref_call(table, pieces, heads, info):
@@ -305,7 +344,7 @@
         pltpu.VMEM((2, HALF, HALF), jnp.float32),
         DMA((2 * WIDE // DEEP, 5)),
     ]
-    specs = [ANY] * 7 + [INSIDE]
+    specs = [TABLE] + [ANY] * 7 + [INSIDE]
     return call(ref_kernel, operands, floats(8, HALF), INSIDE, scratch, 512, specs)
 
 
@@ -320,9 +359,9 @@
         DMA((2,)),
     ]
     operands = (table, *pieces, *logits, *lses, info)
-    specs = [ANY] * 18 + [INSIDE] * 3
+    specs = [TABLE] + [ANY] * 18 + [INSIDE] * 3
     shape = jax.ShapeDtypeStruct((2 * WIDE, HALF), jnp.bfloat16)
-    return call(grad_kernel, operands, shape, ANY, scratch, 1024, specs, 58)
+    return call(grad_kernel, operands, shape, ANY, scratch, 1024, specs)
 
 
 def log_sum(terms, axis):
@@ -379,16 +418,20 @@
     top_near, low_back = send(top, "yx", (1, 1)), send(low, "yx", (-1, -1))
     ref_far = send(ref_near, "zz", (1, -1))
     ref_stats = ref_call(table, (ref, ref_near, ref_back, ref_far), ref_heads, info)
+    before = early_call((low, low_near, top, top_back), heads)
     pieces = (low, top, low_near, top_near, low_back, top_back, low_far, top_far)
-    *pieces, ref_stats = fence(*pieces, ref_stats)
+    *pieces, ref_stats, before = fence(*pieces, ref_stats, before)
 
     swapped = [swap(piece) for piece in pieces[:5]]
-    mine, other, stats = own_call(table, pieces, heads, info)
+    late = (pieces[4], pieces[6], pieces[3], pieces[7])
+    mine, other, stats = late_call(table, late, heads, before, info)
 
     rest = jnp.stack([ref_stats[0], stats[1] - ref_stats[1]]).reshape(2, 4, 1, 128)
-    rest = jnp.broadcast_to(rest, (2, 4, 16, 128)).reshape(2, 64, 1, 128)
-    whole = jnp.broadcast_to(stats[0].reshape(1, 4, 128), (64, 4, 128))
-    message = jnp.concatenate([whole, rest[0], rest[1]], axis=1)
+    rest = jnp.broadcast_to(rest, (2, 4, 16, 128)).reshape(2, 64, 128)
+    message = jnp.concatenate(
+        [jnp.broadcast_to(stats[0].reshape(1, 4, 128), (64, 4, 128)), rest[0][:, None], rest[1][:, None]],
+        axis=1,
+    )
     message, other, *swapped = fence(message, other, *swapped)
     swapped += [swap(piece) for piece in pieces[5:]]
     arrived = lax.all_to_all(message, CHIPS, 0, 0, tiled=True)

time: 151 us -> 151 us (level)
  waiting for transfers between devices: 46.7 us -> 37.9 us
  Pallas kernels: 39.7 us -> 46.8 us
    ppermute x18, waiting for transfers between devices: 33.3 us -> 24.5 us  [send(): return lax.ppermute(values, ALL, pairs)]
    pallas_call x3 -> x4, Pallas kernels: 39.7 us -> 46.8 us  [call(): pl.pallas_call(kernel, out_shape=out_shape, in_specs=specs, out_specs=out...]
  transfers between devices with their start and end apart: 33 -> 33, of which waited for: 10 -> 9; matrix products, arithmetic and copies ran while one was open for 9% -> 9% of each run, Pallas kernels for 16% -> 20%
where the time goes in v6:
time: 151 us; the launch traced here: 150 us
  starting transfers between devices  48.1 us (32%)
  Pallas kernels  46.8 us (31%)
  waiting for transfers between devices  37.9 us (25%)
  other arithmetic  8.98 us (6%)
  local copies, waits for them, and re-layouts  6.78 us (4%)
    pallas_call x4, Pallas kernels, call(): pl.pallas_call(kernel, out_shape=out_shape, in_specs=specs, out_specs=out...  46.8 us
    ppermute x18, starting transfers between devices, send(): return lax.ppermute(values, ALL, pairs)  25.6 us
    ppermute x18, waiting for transfers between devices, send(): return lax.ppermute(values, ALL, pairs)  24.5 us
    ppermute x13, starting transfers between devices, swap(): lax.ppermute(values, ALL, [(index, index ^ 1) for index in range(128)])  10.2 us
    all_to_all x1, waiting for transfers between devices, shards(): arrived = lax.all_to_all(message, CHIPS, 0, 0, tiled=True)  8.42 us
    all_to_all x1, starting transfers between devices, shards(): arrived = lax.all_to_all(message, CHIPS, 0, 0, tiled=True)  6.97 us
    all_to_all x1, starting transfers between devices, shards(): lax.all_to_all(raw, ('zl', 'zh', 'c'), 0, 0, tiled=True)  5.42 us
    all_to_all x1, waiting for transfers between devices, shards(): lax.all_to_all(raw, ('zl', 'zh', 'c'), 0, 0, tiled=True)  4.82 us
  transfers between devices with their start and end apart: 33, of which 9 were waited for; matrix products, arithmetic and copies ran while one was open for 9% of the time, Pallas kernels for 20%

profile of v6, /device:TPU:1, one launch (start us, length us, event | category | flops | bytes accessed | tf_op | source)
XLA Modules:
  0.0 150.0 jit_solution(7478413036024971517)
XLA Ops:
  0.6 1.5 %collective-permute-start.7 = (bf16[8192,512]{1,0:T(8,128)(2,1)}, bf16[8192,512]{1,0:T(8,128)(2,1)}, u32[]{:S(2)}, u32[]{:S(2)}) collective-permute-start(bf16[8192,512]{1,0:T(8,128)(2,1)} %refs_4_.3), channel_id=1, source_target_pairs={{0,1},{1,0},{2,3},{3,2},{4,5},{5,4},{6,7},{7,6},{8,9},{9,8},{10,11... | collective-permute-start | bytes 25165832 | tf_op jit(solution)/shard_map/ppermute | solution.py:44
  2.2 1.0 fusion
  3.2 0.9 copy.25
  4.1 0.9 fusion.2
  5.1 0.8 broadcast_in_dim.95
  5.9 3.0 %collective-permute-start.2 = (bf16[8,4096]{1,0:T(8,128)(2,1)S(1)}, bf16[8,4096]{1,0:T(8,128)(2,1)S(1)}, u32[]{:S(2)}, u32[]{:S(2)}) collective-permute-start(bf16[8,4096]{1,0:T(8,128)(2,1)S(1)} %fusion.2), channel_id=1, source_target_pairs={{0,8},{1,65},{2,10},{3,67},{4,12},{5,69},{6,14},{7,71},{8,0},{9,73... | collective-permute-start | bytes 196616 | tf_op jit(solution)/shard_map/ppermute | solution.py:40
  8.9 0.8 collective-permute-start.1
  9.7 0.7 collective-permute-start
  10.4 1.0 slice.76
  11.4 1.2 collective-permute-start.3
  12.6 5.4 %all-to-all-start = ((bf16[8,16,2048]{2,1,0:T(8,128)(2,1)}), bf16[8,16,2048]{2,1,0:T(8,128)(2,1)S(1)}, u32[]{:S(2)}, u32[]{:S(2)}) async-start(bf16[8,16,2048]{2,1,0:T(8,128)(2,1)} %bitcast.3), calls=%async_computation | async-start | bytes 1048576 | tf_op jit(solution)/shard_map/all_to_all | solution.py:400
  18.1 2.4 %collective-permute-start.6 = (bf16[32,4096]{1,0:T(8,128)(2,1)S(1)}, bf16[32,4096]{1,0:T(8,128)(2,1)S(1)}, u32[]{:S(2)}, u32[]{:S(2)}) collective-permute-start(bf16[32,4096]{1,0:T(8,128)(2,1)S(1)} %pad_maximum_fusion.3), channel_id=1, source_target_pairs={{0,64},{1,9},{2,66},{3,11},{4,68},{5,13},{6,70},{7,15},{8,72},{9,1... | collective-permute-start | bytes 786440 | tf_op jit(solution)/shard_map/ppermute | solution.py:40
  20.5 0.9 collective-permute-start.5
  21.3 0.6 collective-permute-start.4
  22.0 4.8 %all-to-all-done = bf16[8,16,2048]{2,1,0:T(8,128)(2,1)S(1)} async-done(((bf16[8,16,2048]{2,1,0:T(8,128)(2,1)}), bf16[8,16,2048]{2,1,0:T(8,128)(2,1)S(1)}, u32[]{:S(2)}, u32[]{:S(2)}) %all-to-all-start) | async-done | bytes 524320 | tf_op jit(solution)/shard_map/all_to_all | solution.py:400
  26.8 0.2 multiply_reduce_fusion
  27.1 0.1 convert_element_type.88
  27.2 0.7 copy.16
  27.9 0.6 copy.23
  28.5 0.2 multiply_convert_fusion
  28.8 3.0 %collective-permute-start.11 = (bf16[32,8192]{1,0:T(8,128)(2,1)S(1)}, bf16[32,8192]{1,0:T(8,128)(2,1)S(1)}, u32[]{:S(2)}, u32[]{:S(2)}) collective-permute-start(bf16[32,8192]{1,0:T(8,128)(2,1)S(1)} %multiply_convert_fusion), channel_id=1, source_target_pairs={{0,8},{1,65},{2,10},{3,67},{4,12},{5,69},{6,14},{7,71},{8,0},{9,73... | collective-permute-start | bytes 1572872 | tf_op jit(solution)/shard_map/ppermute | solution.py:40
  31.8 0.8 collective-permute-start.10
  32.6 0.7 collective-permute-start.9
  33.3 0.5 collective-permute-start.15
  33.8 2.2 %collective-permute-start.14 = (bf16[128,4096]{1,0:T(8,128)(2,1)S(1)}, bf16[128,4096]{1,0:T(8,128)(2,1)}, u32[]{:S(2)}, u32[]{:S(2)}) collective-permute-start(bf16[128,4096]{1,0:T(8,128)(2,1)S(1)} %pad_maximum_fusion.refs_0_), channel_id=1, source_target_pairs={{0,16},{1,19},{2,18},{3,17},{4,20},{5,23},{6,22},{7,21},{8,24},{9,... | collective-permute-start | bytes 3145736 | tf_op jit(solution)/shard_map/ppermute | solution.py:40
  36.0 2.8 %collective-permute-done.11 = bf16[32,8192]{1,0:T(8,128)(2,1)S(1)} collective-permute-done((bf16[32,8192]{1,0:T(8,128)(2,1)S(1)}, bf16[32,8192]{1,0:T(8,128)(2,1)S(1)}, u32[]{:S(2)}, u32[]{:S(2)}) %collective-permute-start.11) | collective-permute-done | bytes 524320 | tf_op jit(solution)/shard_map/ppermute | solution.py:40
  38.8 6.0 %collective-permute-done.10 = bf16[32,8192]{1,0:T(8,128)(2,1)S(1)} collective-permute-done((bf16[32,8192]{1,0:T(8,128)(2,1)S(1)}, bf16[32,8192]{1,0:T(8,128)(2,1)S(1)}, u32[]{:S(2)}, u32[]{:S(2)}) %collective-permute-start.10) | collective-permute-done | bytes 524320 | tf_op jit(solution)/shard_map/ppermute | solution.py:40
  45.0 1.5 pad_maximum_fusion.1
  46.5 0.8 collective-permute-start.12
  47.3 1.9 %collective-permute-start.13 = (bf16[128,4096]{1,0:T(8,128)(2,1)}, bf16[128,4096]{1,0:T(8,128)(2,1)}, u32[]{:S(2)}, u32[]{:S(2)}) collective-permute-start(bf16[128,4096]{1,0:T(8,128)(2,1)} %get-tuple-element.63.top.refs_1_), channel_id=1, source_target_pairs={{0,96},{1,13},{2,98},{3,15},{4,100},{5,1},{6,102},{7,3},{8,104},{9... | collective-permute-start | bytes 3145736 | tf_op jit(solution)/shard_map/ppermute | solution.py:40
  49.2 0.1 reshape.170
  49.4 5.1 %collective-permute-done.15.refs_2_ = bf16[128,4096]{1,0:T(8,128)(2,1)S(1)} collective-permute-done((bf16[128,4096]{1,0:T(8,128)(2,1)S(1)}, bf16[128,4096]{1,0:T(8,128)(2,1)S(1)}, u32[]{:S(2)}, u32[]{:S(2)}) %collective-permute-start.15) | collective-permute-done | bytes 1048608 | tf_op jit(solution)/shard_map/ppermute | solution.py:40
  54.5 2.9 %collective-permute-done.14.refs_1_ = bf16[128,4096]{1,0:T(8,128)(2,1)} collective-permute-done((bf16[128,4096]{1,0:T(8,128)(2,1)S(1)}, bf16[128,4096]{1,0:T(8,128)(2,1)}, u32[]{:S(2)}, u32[]{:S(2)}) %collective-permute-start.14) | collective-permute-done | bytes 1048608 | tf_op jit(solution)/shard_map/ppermute | solution.py:40
  57.4 4.5 %collective-permute-done.12.low_near.refs_2_ = bf16[128,4096]{1,0:T(8,128)(2,1)} collective-permute-done((bf16[128,4096]{1,0:T(8,128)(2,1)}, bf16[128,4096]{1,0:T(8,128)(2,1)}, u32[]{:S(2)}, u32[]{:S(2)}) %collective-permute-start.12) | collective-permute-done | bytes 1048608 | tf_op jit(solution)/shard_map/ppermute | solution.py:40
  61.9 2.0 %collective-permute-start.20 = (bf16[128,4096]{1,0:T(8,128)(2,1)}, bf16[128,4096]{1,0:T(8,128)(2,1)}, u32[]{:S(2)}, u32[]{:S(2)}) collective-permute-start(bf16[128,4096]{1,0:T(8,128)(2,1)} %collective-permute-done.14.refs_1_), channel_id=1, source_target_pairs={{0,16},{1,19},{2,18},{3,17},{4,20},{5,23},{6,22},{7,21},{8,24},{9,... | collective-permute-start | bytes 3145736 | tf_op jit(solution)/shard_map/ppermute | solution.py:40
  63.9 0.1 reshape.171
  64.1 0.2 convert_reduce_fusion.3
  64.3 0.4 fusion.4
  64.7 2.7 %collective-permute-start.17 = (bf16[128,4096]{1,0:T(8,128)(2,1)}, bf16[128,4096]{1,0:T(8,128)(2,1)S(1)}, u32[]{:S(2)}, u32[]{:S(2)}) collective-permute-start(bf16[128,4096]{1,0:T(8,128)(2,1)} %get-tuple-element.62.low.refs_0_), channel_id=1, source_target_pairs={{0,96},{1,13},{2,98},{3,15},{4,100},{5,1},{6,102},{7,3},{8,104},{9... | collective-permute-start | bytes 3145736 | tf_op jit(solution)/shard_map/ppermute | solution.py:40
  67.5 2.7 %collective-permute-start.19 = (bf16[128,4096]{1,0:T(8,128)(2,1)}, bf16[128,4096]{1,0:T(8,128)(2,1)}, u32[]{:S(2)}, u32[]{:S(2)}) collective-permute-start(bf16[128,4096]{1,0:T(8,128)(2,1)} %collective-permute-done.13.top_back.refs_5_), channel_id=1, source_target_pairs={{0,96},{1,13},{2,98},{3,15},{4,100},{5,1},{6,102},{7,3},{8,104},{9... | collective-permute-start | bytes 3145736 | tf_op jit(solution)/shard_map/ppermute | solution.py:40
  70.2 0.6 add_multiply_fusion.table
  71.3 0.7 select_select_fusion
  72.0 9.6 %shard_map.96.refs_6_ = f32[2,2,256,512]{3,2,1,0:T(8,128)} custom-call(bf16[128,4096]{1,0:T(8,128)(2,1)} %get-tuple-element.62.low.refs_0_, bf16[128,4096]{1,0:T(8,128)(2,1)} %collective-permute-done.12.low_near.refs_2_, bf16[128,4096]{1,0:T(8,128)(2,1)} %get-tuple-element.63.top.refs_1_, bf16[128,4096]{1,0:T(8,128)(2,1)} %collective-permute-done.13.top_back.refs_5_, ...), custom_call_target="tpu_custom_call" | custom-call | flops 4294967296 | bytes 12582912 | tf_op jit(solution)/shard_map/pallas_call | solution.py:293
  81.6 9.3 %shard_map.95 = f32[8,512]{1,0:T(8,128)} custom-call(s32[256]{0:T(256)} %add_multiply_fusion.table, bf16[128,4096]{1,0:T(8,128)(2,1)} %copy-done.3, bf16[128,4096]{1,0:T(8,128)(2,1)} %collective-permute-done.14.refs_1_, bf16[128,4096]{1,0:T(8,128)(2,1)} %copy-done.9, bf16[128,4096]{1,0:T(8,128)(2,1)} %collective-permute-done.20.refs_3_, ...), custom_call_target="tpu_custom_call" | custom-call | flops 4294967296 | bytes 12582912 | tf_op jit(solution)/shard_map/pallas_call | solution.py:293
  90.9 3.1 %collective-permute-done.18.refs_1_.refs_6_ = bf16[128,4096]{1,0:T(8,128)(2,1)S(1)} collective-permute-done((bf16[128,4096]{1,0:T(8,128)(2,1)}, bf16[128,4096]{1,0:T(8,128)(2,1)S(1)}, u32[]{:S(2)}, u32[]{:S(2)}) %collective-permute-start.18) | collective-permute-done | bytes 1048608 | tf_op jit(solution)/shard_map/ppermute | solution.py:40
  94.1 3.9 %collective-permute-start.21 = (bf16[128,4096]{1,0:T(8,128)(2,1)}, bf16[128,4096]{1,0:T(8,128)(2,1)}, u32[]{:S(2)}, u32[]{:S(2)}) collective-permute-start(bf16[128,4096]{1,0:T(8,128)(2,1)} %get-tuple-element.62.low.refs_0_), channel_id=1, source_target_pairs={{0,1},{1,0},{2,3},{3,2},{4,5},{5,4},{6,7},{7,6},{8,9},{9,8},{10,11... | collective-permute-start | bytes 3145736 | tf_op jit(solution)/shard_map/ppermute | solution.py:44
  98.1 0.4 collective-permute-start.23
  98.6 0.4 collective-permute-start.24
  99.0 11.8 %shard_map.97 = (f32[512,512]{1,0:T(8,128)}, f32[512,512]{1,0:T(8,128)}, f32[8,512]{1,0:T(8,128)}) custom-call(s32[256]{0:T(256)} %add_multiply_fusion.table, bf16[128,4096]{1,0:T(8,128)(2,1)} %copy-done, bf16[128,4096]{1,0:T(8,128)(2,1)} %copy-done.2, bf16[128,4096]{1,0:T(8,128)(2,1)} %copy-done.1, ...), custom_call_target="tpu_custom_call" | custom-call | flops 4294967296 | bytes 12582912 | tf_op jit(solution)/shard_map/pallas_call | solution.py:293
  110.9 0.8 fusion.30
  111.7 0.8 pad_maximum_fusion.4
  112.5 7.0 %all-to-all-start.1 = ((f32[64,6,128]{2,1,0:T(8,128)}), f32[64,6,128]{2,1,0:T(8,128)S(1)}, u32[]{:S(2)}, u32[]{:S(2)}) async-start(f32[64,6,128]{2,1,0:T(8,128)} %pad_maximum_fusion.4), calls=%async_computation.1 | async-start | bytes 524288 | tf_op jit(solution)/shard_map/all_to_all | solution.py:437
  119.6 0.6 pad_maximum_fusion.5.refs_20_
  120.2 0.3 collective-permute-start.27
  120.5 0.2 collective-permute-start.28
  120.7 0.3 collective-permute-start.26
  121.0 0.2 collective-permute-start.29
  121.2 8.4 %all-to-all-done.1 = f32[64,6,128]{2,1,0:T(8,128)S(1)} async-done(((f32[64,6,128]{2,1,0:T(8,128)}), f32[64,6,128]{2,1,0:T(8,128)S(1)}, u32[]{:S(2)}, u32[]{:S(2)}) %all-to-all-start.1) | async-done | bytes 196640 | tf_op jit(solution)/shard_map/all_to_all | solution.py:437
  129.9 1.4 collective-permute-start.30
  131.4 0.6 dynamic-slice_subtract_fusion
  132.2 0.8 copy-done.12
  133.0 0.3 copy-done.10
  133.3 0.3 copy-done.11
  133.7 16.1 %shard_map.98 = bf16[8192,512]{1,0:T(8,128)(2,1)} custom-call(s32[256]{0:T(256)} %add_multiply_fusion.table, bf16[128,4096]{1,0:T(8,128)(2,1)} %get-tuple-element.62.low.refs_0_, bf16[128,4096]{1,0:T(8,128)(2,1)} %get-tuple-element.63.top.refs_1_, bf16[128,4096]{1,0:T(8,128)(2,1)} %collective-permute-done.12.low_near.refs_2_, bf16[128,4096]{1,0:T(8,128)(2,1)} %copy-done.1, ...), custom_call_target="tpu_custom_call" | custom-call | flops 8589934592 | bytes 12582912 | tf_op jit(solution)/shard_map/pallas_call | solution.py:293
  (85 shorter events, 1.8 us)
Async XLA Ops:
  0.6 28.2 %collective-permute-start.7 = (bf16[8192,512]{1,0:T(8,128)(2,1)}, bf16[8192,512]{1,0:T(8,128)(2,1)}, u32[]{:S(2)}, u32[]{:S(2)}) collective-permute-start(bf16[8192,512]{1,0:T(8,128)(2,1)} %refs_4_.3), channel_id=1, source_target_pairs={{0,1},{1,0},{2,3},{3,2},{4,5},{5,4},{6,7},{7,6},{8,9},{9,8},{10,11... | collective-permute-start | bytes 25165832 | tf_op jit(solution)/shard_map/ppermute | solution.py:44
  2.1 26.7 %collective-permute-start.8 = (bf16[4096,512]{1,0:T(8,128)(2,1)}, bf16[4096,512]{1,0:T(8,128)(2,1)}, u32[]{:S(2)}, u32[]{:S(2)}) collective-permute-start(bf16[4096,512]{1,0:T(8,128)(2,1)} %refs_4_.2), channel_id=1, source_target_pairs={{0,1},{1,0},{2,3},{3,2},{4,5},{5,4},{6,7},{7,6},{8,9},{9,8},{10,11... | collective-permute-start | bytes 12582920 | tf_op jit(solution)/shard_map/ppermute | solution.py:44
  5.9 5.5 %collective-permute-start.2 = (bf16[8,4096]{1,0:T(8,128)(2,1)S(1)}, bf16[8,4096]{1,0:T(8,128)(2,1)S(1)}, u32[]{:S(2)}, u32[]{:S(2)}) collective-permute-start(bf16[8,4096]{1,0:T(8,128)(2,1)S(1)} %fusion.2), channel_id=1, source_target_pairs={{0,8},{1,65},{2,10},{3,67},{4,12},{5,69},{6,14},{7,71},{8,0},{9,73... | collective-permute-start | bytes 196616 | tf_op jit(solution)/shard_map/ppermute | solution.py:40
  8.9 9.1 %collective-permute-start.1 = (bf16[8,4096]{1,0:T(8,128)(2,1)S(1)}, bf16[8,4096]{1,0:T(8,128)(2,1)S(1)}, u32[]{:S(2)}, u32[]{:S(2)}) collective-permute-start(bf16[8,4096]{1,0:T(8,128)(2,1)S(1)} %fusion.2), channel_id=1, source_target_pairs={{0,12},{1,97},{2,14},{3,99},{4,0},{5,101},{6,2},{7,103},{8,4},{9,1... | collective-permute-start | bytes 196616 | tf_op jit(solution)/shard_map/ppermute | solution.py:40
  9.7 8.3 %collective-permute-start = (bf16[8,4096]{1,0:T(8,128)(2,1)S(1)}, bf16[8,4096]{1,0:T(8,128)(2,1)S(1)}, u32[]{:S(2)}, u32[]{:S(2)}) collective-permute-start(bf16[8,4096]{1,0:T(8,128)(2,1)S(1)} %fusion.2), channel_id=1, source_target_pairs={{0,4},{1,33},{2,6},{3,35},{4,8},{5,37},{6,10},{7,39},{8,12},{9,41}... | collective-permute-start | bytes 196616 | tf_op jit(solution)/shard_map/ppermute | solution.py:40
  11.4 6.6 %collective-permute-start.3 = (bf16[448,512]{1,0:T(8,128)(2,1)S(1)}, bf16[448,512]{1,0:T(8,128)(2,1)}, u32[]{:S(2)}, u32[]{:S(2)}) collective-permute-start(bf16[448,512]{1,0:T(8,128)(2,1)S(1)} %slice.76), channel_id=1, source_target_pairs={{0,1},{1,0},{2,3},{3,2},{4,5},{5,4},{6,7},{7,6},{8,9},{9,8},{10,11... | collective-permute-start | bytes 1376264 | tf_op jit(solution)/shard_map/ppermute | solution.py:44
  12.6 14.2 %all-to-all-start = ((bf16[8,16,2048]{2,1,0:T(8,128)(2,1)}), bf16[8,16,2048]{2,1,0:T(8,128)(2,1)S(1)}, u32[]{:S(2)}, u32[]{:S(2)}) async-start(bf16[8,16,2048]{2,1,0:T(8,128)(2,1)} %bitcast.3), calls=%async_computation | async-start | bytes 1048576 | tf_op jit(solution)/shard_map/all_to_all | solution.py:400
  18.1 10.6 %collective-permute-start.6 = (bf16[32,4096]{1,0:T(8,128)(2,1)S(1)}, bf16[32,4096]{1,0:T(8,128)(2,1)S(1)}, u32[]{:S(2)}, u32[]{:S(2)}) collective-permute-start(bf16[32,4096]{1,0:T(8,128)(2,1)S(1)} %pad_maximum_fusion.3), channel_id=1, source_target_pairs={{0,64},{1,9},{2,66},{3,11},{4,68},{5,13},{6,70},{7,15},{8,72},{9,1... | collective-permute-start | bytes 786440 | tf_op jit(solution)/shard_map/ppermute | solution.py:40
  20.5 8.2 %collective-permute-start.5 = (bf16[32,4096]{1,0:T(8,128)(2,1)S(1)}, bf16[32,4096]{1,0:T(8,128)(2,1)S(1)}, u32[]{:S(2)}, u32[]{:S(2)}) collective-permute-start(bf16[32,4096]{1,0:T(8,128)(2,1)S(1)} %pad_maximum_fusion.3), channel_id=1, source_target_pairs={{0,96},{1,13},{2,98},{3,15},{4,100},{5,1},{6,102},{7,3},{8,104},{9... | collective-permute-start | bytes 786440 | tf_op jit(solution)/shard_map/ppermute | solution.py:40
  21.3 7.4 %collective-permute-start.4 = (bf16[32,4096]{1,0:T(8,128)(2,1)S(1)}, bf16[32,4096]{1,0:T(8,128)(2,1)S(1)}, u32[]{:S(2)}, u32[]{:S(2)}) collective-permute-start(bf16[32,4096]{1,0:T(8,128)(2,1)S(1)} %pad_maximum_fusion.3), channel_id=1, source_target_pairs={{0,32},{1,5},{2,34},{3,7},{4,36},{5,9},{6,38},{7,11},{8,40},{9,13}... | collective-permute-start | bytes 786440 | tf_op jit(solution)/shard_map/ppermute | solution.py:40
  27.2 1.3 copy-start.5
  28.8 16.1 %copy-start.3 = (bf16[128,4096]{1,0:T(8,128)(2,1)}, bf16[128,4096]{1,0:T(8,128)(2,1)S(1)}, u32[]{:S(2)}) copy-start(bf16[128,4096]{1,0:T(8,128)(2,1)S(1)} %pad_maximum_fusion.refs_0_) | copy-start | bytes 3145732
  28.8 10.0 %collective-permute-start.11 = (bf16[32,8192]{1,0:T(8,128)(2,1)S(1)}, bf16[32,8192]{1,0:T(8,128)(2,1)S(1)}, u32[]{:S(2)}, u32[]{:S(2)}) collective-permute-start(bf16[32,8192]{1,0:T(8,128)(2,1)S(1)} %multiply_convert_fusion), channel_id=1, source_target_pairs={{0,8},{1,65},{2,10},{3,67},{4,12},{5,69},{6,14},{7,71},{8,0},{9,73... | collective-permute-start | bytes 1572872 | tf_op jit(solution)/shard_map/ppermute | solution.py:40
  31.8 13.0 %collective-permute-start.10 = (bf16[32,8192]{1,0:T(8,128)(2,1)S(1)}, bf16[32,8192]{1,0:T(8,128)(2,1)S(1)}, u32[]{:S(2)}, u32[]{:S(2)}) collective-permute-start(bf16[32,8192]{1,0:T(8,128)(2,1)S(1)} %multiply_convert_fusion), channel_id=1, source_target_pairs={{0,12},{1,97},{2,14},{3,99},{4,0},{5,101},{6,2},{7,103},{8,4},{9,1... | collective-permute-start | bytes 1572872 | tf_op jit(solution)/shard_map/ppermute | solution.py:40
  32.6 12.3 %collective-permute-start.9 = (bf16[32,8192]{1,0:T(8,128)(2,1)S(1)}, bf16[32,8192]{1,0:T(8,128)(2,1)S(1)}, u32[]{:S(2)}, u32[]{:S(2)}) collective-permute-start(bf16[32,8192]{1,0:T(8,128)(2,1)S(1)} %multiply_convert_fusion), channel_id=1, source_target_pairs={{0,4},{1,33},{2,6},{3,35},{4,8},{5,37},{6,10},{7,39},{8,12},{9,41}... | collective-permute-start | bytes 1572872 | tf_op jit(solution)/shard_map/ppermute | solution.py:40
  33.3 21.2 %collective-permute-start.15 = (bf16[128,4096]{1,0:T(8,128)(2,1)S(1)}, bf16[128,4096]{1,0:T(8,128)(2,1)S(1)}, u32[]{:S(2)}, u32[]{:S(2)}) collective-permute-start(bf16[128,4096]{1,0:T(8,128)(2,1)S(1)} %pad_maximum_fusion.refs_0_), channel_id=1, source_target_pairs={{0,18},{1,17},{2,16},{3,19},{4,22},{5,21},{6,20},{7,23},{8,26},{9,... | collective-permute-start | bytes 3145736 | tf_op jit(solution)/shard_map/ppermute | solution.py:40
  33.8 23.6 %collective-permute-start.14 = (bf16[128,4096]{1,0:T(8,128)(2,1)S(1)}, bf16[128,4096]{1,0:T(8,128)(2,1)}, u32[]{:S(2)}, u32[]{:S(2)}) collective-permute-start(bf16[128,4096]{1,0:T(8,128)(2,1)S(1)} %pad_maximum_fusion.refs_0_), channel_id=1, source_target_pairs={{0,16},{1,19},{2,18},{3,17},{4,20},{5,23},{6,22},{7,21},{8,24},{9,... | collective-permute-start | bytes 3145736 | tf_op jit(solution)/shard_map/ppermute | solution.py:40
  45.0 4.2 %copy-start.6 = (s32[1024]{0:T(1024)S(1)}, s32[1024]{0:T(1024)}, u32[]{:S(2)}) copy-start(s32[1024]{0:T(1024)} %param.14) | copy-start | bytes 12292
  45.0 18.9 %copy-start.7 = (s32[1024]{0:T(1024)S(1)}, s32[1024]{0:T(1024)}, u32[]{:S(2)}) copy-start(s32[1024]{0:T(1024)} %param.15) | copy-start | bytes 12292
  46.5 15.5 %collective-permute-start.12 = (bf16[128,4096]{1,0:T(8,128)(2,1)}, bf16[128,4096]{1,0:T(8,128)(2,1)}, u32[]{:S(2)}, u32[]{:S(2)}) collective-permute-start(bf16[128,4096]{1,0:T(8,128)(2,1)} %get-tuple-element.62.low.refs_0_), channel_id=1, source_target_pairs={{0,32},{1,5},{2,34},{3,7},{4,36},{5,9},{6,38},{7,11},{8,40},{9,13}... | collective-permute-start | bytes 3145736 | tf_op jit(solution)/shard_map/ppermute | solution.py:40
  47.3 14.7 %collective-permute-start.13 = (bf16[128,4096]{1,0:T(8,128)(2,1)}, bf16[128,4096]{1,0:T(8,128)(2,1)}, u32[]{:S(2)}, u32[]{:S(2)}) collective-permute-start(bf16[128,4096]{1,0:T(8,128)(2,1)} %get-tuple-element.63.top.refs_1_), channel_id=1, source_target_pairs={{0,96},{1,13},{2,98},{3,15},{4,100},{5,1},{6,102},{7,3},{8,104},{9... | collective-permute-start | bytes 3145736 | tf_op jit(solution)/shard_map/ppermute | solution.py:40
  54.5 10.2 %copy-start.9 = (bf16[128,4096]{1,0:T(8,128)(2,1)}, bf16[128,4096]{1,0:T(8,128)(2,1)S(1)}, u32[]{:S(2)}) copy-start(bf16[128,4096]{1,0:T(8,128)(2,1)S(1)} %collective-permute-done.15.refs_2_) | copy-start | bytes 3145732
  61.9 19.7 %collective-permute-start.20 = (bf16[128,4096]{1,0:T(8,128)(2,1)}, bf16[128,4096]{1,0:T(8,128)(2,1)}, u32[]{:S(2)}, u32[]{:S(2)}) collective-permute-start(bf16[128,4096]{1,0:T(8,128)(2,1)} %collective-permute-done.14.refs_1_), channel_id=1, source_target_pairs={{0,16},{1,19},{2,18},{3,17},{4,20},{5,23},{6,22},{7,21},{8,24},{9,... | collective-permute-start | bytes 3145736 | tf_op jit(solution)/shard_map/ppermute | solution.py:40
  64.7 26.2 %collective-permute-start.17 = (bf16[128,4096]{1,0:T(8,128)(2,1)}, bf16[128,4096]{1,0:T(8,128)(2,1)S(1)}, u32[]{:S(2)}, u32[]{:S(2)}) collective-permute-start(bf16[128,4096]{1,0:T(8,128)(2,1)} %get-tuple-element.62.low.refs_0_), channel_id=1, source_target_pairs={{0,96},{1,13},{2,98},{3,15},{4,100},{5,1},{6,102},{7,3},{8,104},{9... | collective-permute-start | bytes 3145736 | tf_op jit(solution)/shard_map/ppermute | solution.py:40
  67.5 23.5 %collective-permute-start.16 = (bf16[128,4096]{1,0:T(8,128)(2,1)}, bf16[128,4096]{1,0:T(8,128)(2,1)S(1)}, u32[]{:S(2)}, u32[]{:S(2)}) collective-permute-start(bf16[128,4096]{1,0:T(8,128)(2,1)} %get-tuple-element.63.top.refs_1_), channel_id=1, source_target_pairs={{0,32},{1,5},{2,34},{3,7},{4,36},{5,9},{6,38},{7,11},{8,40},{9,13}... | collective-permute-start | bytes 3145736 | tf_op jit(solution)/shard_map/ppermute | solution.py:40
  67.5 26.6 %collective-permute-start.18 = (bf16[128,4096]{1,0:T(8,128)(2,1)}, bf16[128,4096]{1,0:T(8,128)(2,1)S(1)}, u32[]{:S(2)}, u32[]{:S(2)}) collective-permute-start(bf16[128,4096]{1,0:T(8,128)(2,1)} %collective-permute-done.12.low_near.refs_2_), channel_id=1, source_target_pairs={{0,32},{1,5},{2,34},{3,7},{4,36},{5,9},{6,38},{7,11},{8,40},{9,13}... | collective-permute-start | bytes 3145736 | tf_op jit(solution)/shard_map/ppermute | solution.py:40
  67.5 26.6 %collective-permute-start.19 = (bf16[128,4096]{1,0:T(8,128)(2,1)}, bf16[128,4096]{1,0:T(8,128)(2,1)}, u32[]{:S(2)}, u32[]{:S(2)}) collective-permute-start(bf16[128,4096]{1,0:T(8,128)(2,1)} %collective-permute-done.13.top_back.refs_5_), channel_id=1, source_target_pairs={{0,96},{1,13},{2,98},{3,15},{4,100},{5,1},{6,102},{7,3},{8,104},{9... | collective-permute-start | bytes 3145736 | tf_op jit(solution)/shard_map/ppermute | solution.py:40
  90.9 28.7 %copy-start.4 = (f32[8,512]{1,0:T(8,128)S(1)}, f32[8,512]{1,0:T(8,128)}, u32[]{:S(2)}) copy-start(f32[8,512]{1,0:T(8,128)} %get-tuple-element.96.refs_7_) | copy-start | bytes 49156
  90.9 8.1 %copy-start = (bf16[128,4096]{1,0:T(8,128)(2,1)}, bf16[128,4096]{1,0:T(8,128)(2,1)S(1)}, u32[]{:S(2)}) copy-start(bf16[128,4096]{1,0:T(8,128)(2,1)S(1)} %collective-permute-done.17.refs_0_.refs_4_) | copy-start | bytes 3145732
  90.9 8.1 %copy-start.1 = (bf16[128,4096]{1,0:T(8,128)(2,1)}, bf16[128,4096]{1,0:T(8,128)(2,1)S(1)}, u32[]{:S(2)}) copy-start(bf16[128,4096]{1,0:T(8,128)(2,1)S(1)} %collective-permute-done.16.refs_2_.refs_3_) | copy-start | bytes 3145732
  94.1 5.0 %copy-start.2 = (bf16[128,4096]{1,0:T(8,128)(2,1)}, bf16[128,4096]{1,0:T(8,128)(2,1)S(1)}, u32[]{:S(2)}) copy-start(bf16[128,4096]{1,0:T(8,128)(2,1)S(1)} %collective-permute-done.18.refs_1_.refs_6_) | copy-start | bytes 3145732
  94.1 18.5 %collective-permute-start.21 = (bf16[128,4096]{1,0:T(8,128)(2,1)}, bf16[128,4096]{1,0:T(8,128)(2,1)}, u32[]{:S(2)}, u32[]{:S(2)}) collective-permute-start(bf16[128,4096]{1,0:T(8,128)(2,1)} %get-tuple-element.62.low.refs_0_), channel_id=1, source_target_pairs={{0,1},{1,0},{2,3},{3,2},{4,5},{5,4},{6,7},{7,6},{8,9},{9,8},{10,11... | collective-permute-start | bytes 3145736 | tf_op jit(solution)/shard_map/ppermute | solution.py:44
  98.0 14.5 %collective-permute-start.22 = (bf16[128,4096]{1,0:T(8,128)(2,1)}, bf16[128,4096]{1,0:T(8,128)(2,1)}, u32[]{:S(2)}, u32[]{:S(2)}) collective-permute-start(bf16[128,4096]{1,0:T(8,128)(2,1)} %get-tuple-element.63.top.refs_1_), channel_id=1, source_target_pairs={{0,1},{1,0},{2,3},{3,2},{4,5},{5,4},{6,7},{7,6},{8,9},{9,8},{10,11... | collective-permute-start | bytes 3145736 | tf_op jit(solution)/shard_map/ppermute | solution.py:44
  98.1 14.5 %collective-permute-start.23 = (bf16[128,4096]{1,0:T(8,128)(2,1)}, bf16[128,4096]{1,0:T(8,128)(2,1)}, u32[]{:S(2)}, u32[]{:S(2)}) collective-permute-start(bf16[128,4096]{1,0:T(8,128)(2,1)} %collective-permute-done.12.low_near.refs_2_), channel_id=1, source_target_pairs={{0,1},{1,0},{2,3},{3,2},{4,5},{5,4},{6,7},{7,6},{8,9},{9,8},{10,11... | collective-permute-start | bytes 3145736 | tf_op jit(solution)/shard_map/ppermute | solution.py:44
  98.5 14.0 %collective-permute-start.25 = (bf16[128,4096]{1,0:T(8,128)(2,1)S(1)}, bf16[128,4096]{1,0:T(8,128)(2,1)}, u32[]{:S(2)}, u32[]{:S(2)}) collective-permute-start(bf16[128,4096]{1,0:T(8,128)(2,1)S(1)} %collective-permute-done.17.refs_0_.refs_4_), channel_id=1, source_target_pairs={{0,1},{1,0},{2,3},{3,2},{4,5},{5,4},{6,7},{7,6},{8,9},{9,8},{10,11... | collective-permute-start | bytes 3145736 | tf_op jit(solution)/shard_map/ppermute | solution.py:44
  98.6 14.0 %collective-permute-start.24 = (bf16[128,4096]{1,0:T(8,128)(2,1)S(1)}, bf16[128,4096]{1,0:T(8,128)(2,1)}, u32[]{:S(2)}, u32[]{:S(2)}) collective-permute-start(bf16[128,4096]{1,0:T(8,128)(2,1)S(1)} %collective-permute-done.16.refs_2_.refs_3_), channel_id=1, source_target_pairs={{0,1},{1,0},{2,3},{3,2},{4,5},{5,4},{6,7},{7,6},{8,9},{9,8},{10,11... | collective-permute-start | bytes 3145736 | tf_op jit(solution)/shard_map/ppermute | solution.py:44
  112.5 17.1 %all-to-all-start.1 = ((f32[64,6,128]{2,1,0:T(8,128)}), f32[64,6,128]{2,1,0:T(8,128)S(1)}, u32[]{:S(2)}, u32[]{:S(2)}) async-start(f32[64,6,128]{2,1,0:T(8,128)} %pad_maximum_fusion.4), calls=%async_computation.1 | async-start | bytes 524288 | tf_op jit(solution)/shard_map/all_to_all | solution.py:437
  120.2 11.8 %collective-permute-start.27 = (bf16[128,4096]{1,0:T(8,128)(2,1)}, bf16[128,4096]{1,0:T(8,128)(2,1)S(1)}, u32[]{:S(2)}, u32[]{:S(2)}) collective-permute-start(bf16[128,4096]{1,0:T(8,128)(2,1)} %copy-done.2), channel_id=1, source_target_pairs={{0,1},{1,0},{2,3},{3,2},{4,5},{5,4},{6,7},{7,6},{8,9},{9,8},{10,11... | collective-permute-start | bytes 3145736 | tf_op jit(solution)/shard_map/ppermute | solution.py:44
  120.5 11.5 %collective-permute-start.28 = (bf16[128,4096]{1,0:T(8,128)(2,1)}, bf16[128,4096]{1,0:T(8,128)(2,1)S(1)}, u32[]{:S(2)}, u32[]{:S(2)}) collective-permute-start(bf16[128,4096]{1,0:T(8,128)(2,1)} %collective-permute-done.19.refs_3_.refs_7_), channel_id=1, source_target_pairs={{0,1},{1,0},{2,3},{3,2},{4,5},{5,4},{6,7},{7,6},{8,9},{9,8},{10,11... | collective-permute-start | bytes 3145736 | tf_op jit(solution)/shard_map/ppermute | solution.py:44
  120.7 11.3 %collective-permute-start.26 = (bf16[128,4096]{1,0:T(8,128)(2,1)}, bf16[128,4096]{1,0:T(8,128)(2,1)S(1)}, u32[]{:S(2)}, u32[]{:S(2)}) collective-permute-start(bf16[128,4096]{1,0:T(8,128)(2,1)} %collective-permute-done.13.top_back.refs_5_), channel_id=1, source_target_pairs={{0,1},{1,0},{2,3},{3,2},{4,5},{5,4},{6,7},{7,6},{8,9},{9,8},{10,11... | collective-permute-start | bytes 3145736 | tf_op jit(solution)/shard_map/ppermute | solution.py:44
  121.0 11.1 %collective-permute-start.29 = (f32[512,512]{1,0:T(8,128)}, f32[512,512]{1,0:T(8,128)}, u32[]{:S(2)}, u32[]{:S(2)}) collective-permute-start(f32[512,512]{1,0:T(8,128)} %get-tuple-element.73), channel_id=1, source_target_pairs={{0,1},{1,0},{2,3},{3,2},{4,5},{5,4},{6,7},{7,6},{8,9},{9,8},{10,11... | collective-permute-start | bytes 3145736 | tf_op jit(solution)/shard_map/ppermute | solution.py:44
  129.9 2.3 %copy-start.8 = (f32[4,128]{1,0:T(4,128)}, f32[4,128]{1,0:T(4,128)S(1)}, u32[]{:S(2)}) copy-start(f32[4,128]{1,0:T(4,128)S(1)} %log_add_fusion.refs_18_) | copy-start | bytes 6148
  129.9 2.3 %collective-permute-start.30 = (f32[4,128]{1,0:T(4,128)S(1)}, f32[4,128]{1,0:T(4,128)S(1)}, u32[]{:S(2)}, u32[]{:S(2)}) collective-permute-start(f32[4,128]{1,0:T(4,128)S(1)} %log_add_fusion.refs_18_), channel_id=1, source_target_pairs={{0,1},{1,0},{2,3},{3,2},{4,5},{5,4},{6,7},{7,6},{8,9},{9,8},{10,11... | collective-permute-start | bytes 6152 | tf_op jit(solution)/shard_map/ppermute | solution.py:44
  132.0 1.0 copy-start.12
  132.0 1.3 copy-start.10
  132.0 1.6 %copy-start.11 = (bf16[128,4096]{1,0:T(8,128)(2,1)}, bf16[128,4096]{1,0:T(8,128)(2,1)S(1)}, u32[]{:S(2)}) copy-start(bf16[128,4096]{1,0:T(8,128)(2,1)S(1)} %collective-permute-done.28.refs_15_) | copy-start | bytes 3145732
  132.2 1.5 %copy-start.13 = (f32[4,128]{1,0:T(4,128)}, f32[4,128]{1,0:T(4,128)S(1)}, u32[]{:S(2)}) copy-start(f32[4,128]{1,0:T(4,128)S(1)} %collective-permute-done.30.refs_19_) | copy-start | bytes 6148
